TPU v7x, 512 devices: a whole 4x8x8 slice. The times are simulated.
512 devices in a mesh: cache: 64 (over x, z, core), tp: 8 (over y).
Axes of the slice: x: 4, y: 8, z: 8, core: 2. Of those that a mesh axis runs over, the one named last changes fastest.
Arguments:
- query: bfloat16 [64, 256, 8192], P('cache', 'tp')
- qkeys: bfloat16 [64, 256, 1024], P('cache', 'tp')
- qvalues: bfloat16 [64, 256, 1024], P('cache', 'tp'), may hold values from -6 to 6
- cache_keys: bfloat16 [256, 512, 1024], P('cache', None, 'tp'), may hold values from -6 to 6
- cache_values: bfloat16 [256, 512, 1024], P('cache', None, 'tp'), may hold values from -6 to 6
- lists: int32 [64, 8], P('cache'), may hold values from 0 to 255, all different within a row
Outputs:
- attended: bfloat16 [64, 256, 8192], P('cache', 'tp')
Inputs may be any that keep to these rules, and one draw needn't show every extreme that they name: `lists`: each row names 8 different passages; every passage is named by some request.
All inputs are finite; a program needn't handle non-finite values.
Results may differ from a plain program's by a relative error of at most 0.0046.
Values may be sent and summed in bfloat16 or wider, within the bound.
No kernel may reach another device: no remote copies, remote signals or barrier semaphores. Data moves between devices by JAX's collectives and lax.ppermute only.
A program may use at most 64 MiB of HBM per device.

v0:
```python
import jax
import jax.numpy as jnp
from jax import lax
from jax.sharding import PartitionSpec as P

HD = 128


NEG = -1e30


def block_part(queries, keys, values, mask):
    kv_count = queries.shape[0]
    head_dim = queries.shape[3]
    keys_h = keys.reshape(keys.shape[0], kv_count, head_dim).transpose(1, 0, 2)
    values_h = values.reshape(values.shape[0], kv_count, head_dim).transpose(1, 0, 2)
    scale = head_dim ** (-0.5)

    def one_head(items):
        query_h, key_h, value_h = items
        scores = (
            jnp.einsum("gqd,nd->gqn", query_h, key_h, preferred_element_type=jnp.float32) * scale
        )
        if mask is not None:
            scores = jnp.where(mask[None], scores, NEG)
        top = jnp.max(scores, axis=-1)
        weights = jnp.exp(scores - top[..., None])
        totals = jnp.sum(weights, axis=-1)
        rounded = weights.astype(jnp.bfloat16)
        output = jnp.einsum("gqn,nd->gqd", rounded, value_h, preferred_element_type=jnp.float32)
        return (output, top, totals)

    return lax.map(one_head, (queries, keys_h, values_h))


def combine(own, outs_b, maxes, totals):
    own_out, own_max, own_tot = own
    top = jnp.maximum(own_max, jnp.max(maxes, axis=0))
    own_w = jnp.exp(own_max - top)
    block_w = jnp.exp(maxes - top[None])
    numer = own_out * own_w[..., None] + jnp.sum(outs_b * block_w[..., None], axis=0)
    denom = own_tot * own_w + jnp.sum(totals * block_w, axis=0)
    return (numer / denom[..., None]).astype(jnp.bfloat16)


def local(query, qkeys, qvalues, cache_keys, cache_values, lists):
    all_lists = lax.all_gather(lists, "cache", axis=0, tiled=True)
    banded_k, banded_v = (
        lax.all_to_all(cache_keys, "cache", split_axis=1, concat_axis=0, tiled=True),
        lax.all_to_all(cache_values, "cache", split_axis=1, concat_axis=0, tiled=True),
    )
    q_heads, k_heads, v_heads = (
        lax.all_to_all(query, "tp", split_axis=2, concat_axis=1, tiled=True),
        lax.all_to_all(qkeys, "tp", split_axis=2, concat_axis=1, tiled=True),
        lax.all_to_all(qvalues, "tp", split_axis=2, concat_axis=1, tiled=True),
    )
    kv_local = k_heads.shape[2] // HD
    q_local = q_heads.shape[2] // HD
    group = q_local // kv_local
    qlen = q_heads.shape[1]
    queries = q_heads[0].reshape(qlen, kv_local, group, HD).transpose(1, 2, 0, 3)
    causal = jnp.arange(qlen)[:, None] >= jnp.arange(qlen)[None, :]
    own = block_part(queries, k_heads[0], v_heads[0], causal)
    picked_k = jnp.take(banded_k, all_lists, axis=0)
    picked_v = jnp.take(banded_v, all_lists, axis=0)

    def passage_part(pair):
        return block_part(queries, pair[0], pair[1], None)

    keys_all, values_all = (
        lax.all_to_all(picked_k, "cache", split_axis=0, concat_axis=2, tiled=True),
        lax.all_to_all(picked_v, "cache", split_axis=0, concat_axis=2, tiled=True),
    )
    outs_b, maxes, totals = lax.map(passage_part, (keys_all[0], values_all[0]))
    merged = combine(own, outs_b, maxes, totals)
    result = merged.transpose(2, 0, 1, 3).reshape(1, qlen, q_local * HD)
    return lax.all_to_all(result, "tp", split_axis=1, concat_axis=2, tiled=True)


def solution(mesh):
    return jax.shard_map(
        local,
        mesh=mesh,
        in_specs=(
            P("cache", "tp", None),
            P("cache", "tp", None),
            P("cache", "tp", None),
            P("cache", None, "tp"),
            P("cache", None, "tp"),
            P("cache", None),
        ),
        out_specs=P("cache", "tp", None),
        check_vma=False,
    )
```

profile of v0, /device:TPU:1, one launch (start us, length us, event | category | flops | bytes accessed | tf_op | source)
XLA Modules:
  0.0 322.0 jit_solution(9090482906256413749)
XLA Ops:
  4.9 7.7 %all-to-all-start.1 = ((bf16[8,2,2048]{2,1,0:T(2,128)(2,1)}), bf16[8,2,2048]{2,1,0:T(2,128)(2,1)S(1)}, u32[]{:S(2)}, u32[]{:S(2)}) async-start(bf16[8,2,2048]{2,1,0:T(2,128)(2,1)} %reshape.124), calls=%async_computation.1 | async-start | bytes 131072 | tf_op jit(solution)/shard_map/all_to_all | solution.py:54
  16.9 2.9 all-to-all-done.1
  19.8 3.7 %all-to-all-start.2 = ((bf16[8,2,2048]{2,1,0:T(2,128)(2,1)}), bf16[8,2,2048]{2,1,0:T(2,128)(2,1)S(1)}, u32[]{:S(2)}, u32[]{:S(2)}) async-start(bf16[8,2,2048]{2,1,0:T(2,128)(2,1)} %reshape.126), calls=%async_computation.2 | async-start | bytes 131072 | tf_op jit(solution)/shard_map/all_to_all | solution.py:55
  25.8 5.0 %all-to-all-done.2 = bf16[8,2,2048]{2,1,0:T(2,128)(2,1)S(1)} async-done(((bf16[8,2,2048]{2,1,0:T(2,128)(2,1)}), bf16[8,2,2048]{2,1,0:T(2,128)(2,1)S(1)}, u32[]{:S(2)}, u32[]{:S(2)}) %all-to-all-start.2) | async-done | bytes 65568 | tf_op jit(solution)/shard_map/all_to_all | solution.py:55
  30.8 16.1 %all-to-all-start.3 = ((bf16[4,512,128]{2,0,1:T(4,128)(2,1)}), bf16[4,512,128]{2,0,1:T(4,128)(2,1)S(1)}, u32[]{:S(2)}, u32[]{:S(2)}) async-start(bf16[4,512,128]{2,0,1:T(4,128)(2,1)} %copy.69), calls=%async_computation.3 | async-start | bytes 1048576 | tf_op jit(solution)/shard_map/all_to_all | solution.py:49
  48.1 16.1 %all-to-all-done.3 = bf16[4,512,128]{2,0,1:T(4,128)(2,1)S(1)} async-done(((bf16[4,512,128]{2,0,1:T(4,128)(2,1)}), bf16[4,512,128]{2,0,1:T(4,128)(2,1)S(1)}, u32[]{:S(2)}, u32[]{:S(2)}) %all-to-all-start.3) | async-done | bytes 524320 | tf_op jit(solution)/shard_map/all_to_all | solution.py:49
  64.2 6.3 %all-to-all-start.5 = ((bf16[4,512,128]{2,0,1:T(4,128)(2,1)}), bf16[4,512,128]{2,0,1:T(4,128)(2,1)S(1)}, u32[]{:S(2)}, u32[]{:S(2)}) async-start(bf16[4,512,128]{2,0,1:T(4,128)(2,1)} %copy.73), calls=%async_computation.5 | async-start | bytes 1048576 | tf_op jit(solution)/shard_map/all_to_all | solution.py:50
  70.5 6.7 %copy.57 = bf16[1,32,8192]{1,0,2:T(2,128)(2,1)} copy(bf16[1,32,8192]{2,1,0:T(8,128)(2,1)S(1)} %copy-done.2) | data formatting | bytes 1048576 | tf_op args[0]
  77.3 45.2 %reduce.3 = bf16[8192,32]{1,0:T(8,128)(2,1)S(1)} reduce(bf16[8192,1,32]{2,1,0:T(2,128)(2,1)} %bitcast.152, bf16[]{:T(256)} %broadcast.57), dimensions={1}, to_apply=%bitcast.108.reduce_sub_computation | reduce | bytes 1048578
  125.1 4.1 %all-to-all-start = ((bf16[8,2,16384]{2,1,0:T(2,128)(2,1)}), bf16[8,2,16384]{2,1,0:T(2,128)(2,1)}, u32[]{:S(2)}, u32[]{:S(2)}) async-start(bf16[8,2,16384]{2,1,0:T(2,128)(2,1)} %reshape.122), calls=%async_computation | async-start | bytes 1048576 | tf_op jit(solution)/shard_map/all_to_all | solution.py:53
  129.3 41.4 %all-gather = s32[64,1,8]{2,1,0:T(1,128)S(1)} all-gather(s32[1,1,8]{2,1,0:T(1,128)S(1)} %bitcast.180), channel_id=1, replica_groups=mesh['cache'=64,'tp'=8] {'cache'}, dimensions={0}, use_global_device_ids=true | all-gather | bytes 2080 | tf_op jit(solution)/shard_map/all_gather | solution.py:47
  176.4 34.8 %all_to_all.129 = bf16[64,8,8,128]{3,2,1,0:T(8,128)(2,1)S(1)} all-to-all(bf16[64,8,8,128]{3,2,1,0:T(8,128)(2,1)S(1)} %get-tuple-element.115), channel_id=1, replica_groups=mesh['cache'=64,'tp'=8] {'cache'}, dimensions={0} | all-to-all | bytes 2097152 | tf_op jit(solution)/shard_map/all_to_all | solution.py:72
  211.2 6.2 %all-to-all-start.4 = ((bf16[64,8,8,128]{3,2,1,0:T(8,128)(2,1)}), bf16[64,8,8,128]{3,2,1,0:T(8,128)(2,1)S(1)}, u32[]{:S(2)}, u32[]{:S(2)}) async-start(bf16[64,8,8,128]{3,2,1,0:T(8,128)(2,1)} %get-tuple-element.116), calls=%async_computation.4 | async-start | bytes 2097152 | tf_op jit(solution)/shard_map/all_to_all | solution.py:71
  218.9 6.2 %reshape.123 = bf16[8192,1,32]{2,1,0:T(2,128)(2,1)} reshape(bf16[8,2,16384]{2,1,0:T(2,128)(2,1)} %all-to-all-done) | data formatting | bytes 1048576
  225.0 8.0 %copy.58 = bf16[1,32,8192]{2,1,0:T(8,128)(2,1)S(1)} copy(bf16[1,32,8192]{1,0,2:T(2,128)(2,1)} %bitcast.151) | data formatting | bytes 1048576 | tf_op jit(solution)/shard_map/all_to_all | solution.py:53
  236.9 9.0 %all-to-all-done.4 = bf16[64,8,8,128]{3,2,1,0:T(8,128)(2,1)S(1)} async-done(((bf16[64,8,8,128]{3,2,1,0:T(8,128)(2,1)}), bf16[64,8,8,128]{3,2,1,0:T(8,128)(2,1)S(1)}, u32[]{:S(2)}, u32[]{:S(2)}) %all-to-all-start.4) | async-done | bytes 1048608 | tf_op jit(solution)/shard_map/all_to_all | solution.py:71
  246.1 33.7 %while.2 = (s32[]{:T(128)}, f32[8,1,8,256,128]{4,3,2,1,0:T(8,128)}, f32[8,1,8,256]{3,2,1,0:T(8,128)S(1)}, f32[8,1,8,256]{3,2,1,0:T(8,128)S(1)}, bf16[8,512,128]{...) while((s32[]{:T(128)}, ...), condition=%wide.region_4.6_spmd, body=%wide.region_1.5_spmd.sunk | while | flops 545255424 | bytes 14484573 | solution.py:74
  247.6 2.8 fusion.49
  251.8 2.8 fusion.49
  268.6 2.8 fusion.49
  272.8 2.8 fusion.49
  279.9 5.4 %multiply_reduce_fusion = f32[8,256,128]{2,1,0:T(8,128)S(1)} fusion(f32[8,1,8,256,128]{4,3,2,1,0:T(8,128)} %get-tuple-element.90, f32[8,8,256]{2,1,0:T(8,128)S(1)} %get-tuple-element.114), kind=kLoop, calls=%fused_computation.23 | loop fusion | flops 3932160 | bytes 9502720 | tf_op jit(solution)/shard_map/reduce_sum | solution.py:41
  291.8 3.7 %reduce.6 = bf16[256,1024]{1,0:T(8,128)(2,1)S(1)} reduce(bf16[256,1,1024]{2,1,0:T(2,128)(2,1)S(1)} %bitcast.156, bf16[]{:T(256)} %broadcast.57), dimensions={1}, to_apply=%bitcast.114.reduce_sub_computation | reduce | bytes 1048578
  295.9 24.5 %all_to_all.130 = bf16[8,2,16384]{2,1,0:T(2,128)(2,1)S(1)} all-to-all(bf16[8,2,16384]{2,1,0:T(2,128)(2,1)S(1)} %reshape.128), channel_id=1, replica_groups=mesh['cache'=64,'tp'=8] {'tp'}, dimensions={0} | all-to-all | bytes 1048576 | tf_op jit(solution)/shard_map/all_to_all | solution.py:77
  (95 shorter events, 57.1 us)
Async XLA Ops:
  0.0 46.9 %copy-start.3 = (bf16[4,512,128]{2,1,0:T(8,128)(2,1)S(1)}, bf16[4,512,128]{2,1,0:T(8,128)(2,1)}, u32[]{:S(2)}) copy-start(bf16[4,512,128]{2,1,0:T(8,128)(2,1)} %param.14) | copy-start | bytes 1572868
  0.0 70.5 %copy-start.2 = (bf16[1,32,8192]{2,1,0:T(8,128)(2,1)S(1)}, bf16[1,32,8192]{2,1,0:T(8,128)(2,1)}, u32[]{:S(2)}) copy-start(bf16[1,32,8192]{2,1,0:T(8,128)(2,1)} %param.10) | copy-start | bytes 1572868
  4.9 14.9 %all-to-all-start.1 = ((bf16[8,2,2048]{2,1,0:T(2,128)(2,1)}), bf16[8,2,2048]{2,1,0:T(2,128)(2,1)S(1)}, u32[]{:S(2)}, u32[]{:S(2)}) async-start(bf16[8,2,2048]{2,1,0:T(2,128)(2,1)} %reshape.124), calls=%async_computation.1 | async-start | bytes 131072 | tf_op jit(solution)/shard_map/all_to_all | solution.py:54
  19.8 10.9 %all-to-all-start.2 = ((bf16[8,2,2048]{2,1,0:T(2,128)(2,1)}), bf16[8,2,2048]{2,1,0:T(2,128)(2,1)S(1)}, u32[]{:S(2)}, u32[]{:S(2)}) async-start(bf16[8,2,2048]{2,1,0:T(2,128)(2,1)} %reshape.126), calls=%async_computation.2 | async-start | bytes 131072 | tf_op jit(solution)/shard_map/all_to_all | solution.py:55
  30.8 33.5 %all-to-all-start.3 = ((bf16[4,512,128]{2,0,1:T(4,128)(2,1)}), bf16[4,512,128]{2,0,1:T(4,128)(2,1)S(1)}, u32[]{:S(2)}, u32[]{:S(2)}) async-start(bf16[4,512,128]{2,0,1:T(4,128)(2,1)} %copy.69), calls=%async_computation.3 | async-start | bytes 1048576 | tf_op jit(solution)/shard_map/all_to_all | solution.py:49
  64.2 60.9 %all-to-all-start.5 = ((bf16[4,512,128]{2,0,1:T(4,128)(2,1)}), bf16[4,512,128]{2,0,1:T(4,128)(2,1)S(1)}, u32[]{:S(2)}, u32[]{:S(2)}) async-start(bf16[4,512,128]{2,0,1:T(4,128)(2,1)} %copy.73), calls=%async_computation.5 | async-start | bytes 1048576 | tf_op jit(solution)/shard_map/all_to_all | solution.py:50
  77.3 52.0 %copy-start.4 = (s32[1,8]{1,0:T(1,128)S(1)}, s32[1,8]{1,0:T(1,128)}, u32[]{:S(2)}) copy-start(s32[1,8]{1,0:T(1,128)} %param.15) | copy-start | bytes 100
  125.1 51.2 %all-to-all-start = ((bf16[8,2,16384]{2,1,0:T(2,128)(2,1)}), bf16[8,2,16384]{2,1,0:T(2,128)(2,1)}, u32[]{:S(2)}, u32[]{:S(2)}) async-start(bf16[8,2,16384]{2,1,0:T(2,128)(2,1)} %reshape.122), calls=%async_computation | async-start | bytes 1048576 | tf_op jit(solution)/shard_map/all_to_all | solution.py:53
  211.2 34.8 %all-to-all-start.4 = ((bf16[64,8,8,128]{3,2,1,0:T(8,128)(2,1)}), bf16[64,8,8,128]{3,2,1,0:T(8,128)(2,1)S(1)}, u32[]{:S(2)}, u32[]{:S(2)}) async-start(bf16[64,8,8,128]{3,2,1,0:T(8,128)(2,1)} %get-tuple-element.116), calls=%async_computation.4 | async-start | bytes 2097152 | tf_op jit(solution)/shard_map/all_to_all | solution.py:71
  234.3 1.4 copy-start
  279.9 6.8 %copy-start.1 = (f32[8,256,256]{1,2,0:T(8,128)S(1)}, f32[8,256,256]{1,2,0:T(8,128)}, u32[]{:S(2)}) copy-start(f32[8,256,256]{1,2,0:T(8,128)} %copy-done) | copy-start | bytes 6291460
where the time goes:
time: 324 us; the launch traced here: 322 us
  blocking collectives  101 us (31%)
  other arithmetic  66.5 us (21%)
  local copies, waits for them, and re-layouts  45.9 us (14%)
  starting transfers between devices  44.1 us (14%)
  waiting for transfers between devices  33.1 us (10%)
  matrix products  31 us (10%)
    unnamed x4, other arithmetic  53.4 us
    all_gather x1, blocking collectives, local(): all_lists = lax.all_gather(lists, 'cache', axis=0, tiled=True)  41.4 us
    all_to_all x1, blocking collectives, local(): lax.all_to_all(picked_v, 'cache', split_axis=0, concat_axis=2, tiled=True)  34.8 us
    unnamed x29, local copies, waits for them, and re-layouts  26.8 us
    dot_general x9, matrix products, one_head(): jnp.einsum('gqn,nd->gqd', rounded, value_h, preferred_element_type=jnp.fl...  24.8 us
    all_to_all x1, blocking collectives, local(): return lax.all_to_all(result, 'tp', split_axis=1, concat_axis=2, tiled=True)  24.5 us
    all_to_all x1, starting transfers between devices, local(): lax.all_to_all(cache_keys, 'cache', split_axis=1, concat_axis=0, tiled=True)  16.1 us
    all_to_all x1, waiting for transfers between devices, local(): lax.all_to_all(cache_keys, 'cache', split_axis=1, concat_axis=0, tiled=True)  16.1 us
  transfers between devices with their start and end apart: 6, of which 4 were waited for; matrix products, arithmetic and copies ran while one was open for 27% of the time, Pallas kernels for 0%

commit v1 on v0

v1 whole, which is shorter than its diff:
```python
import functools

import jax
import jax.numpy as jnp
from jax import lax
from jax.experimental import pallas as pl
from jax.experimental.pallas import tpu as pltpu
from jax.sharding import PartitionSpec as P

HD = 128
ROWS = 16
LOG2E = 1.4426950408889634
VMEM = pltpu.CompilerParams(vmem_limit_bytes=48 * 1024 * 1024)


def whole(shape):
    return pl.BlockSpec(shape, lambda *_: (0,) * len(shape))


def cut_bands(cache_keys, cache_values, parts):
    owned, plen, width = cache_keys.shape
    half = parts // 2

    def kernel(k_ref, v_ref, out_ref):
        for i in range(owned):
            out_ref[:half, i] = k_ref[i].reshape(half, ROWS, width)
            out_ref[half:, i] = v_ref[i].reshape(half, ROWS, width)

    return pl.pallas_call(
        kernel,
        out_shape=jax.ShapeDtypeStruct((parts, owned, ROWS, width), cache_keys.dtype),
        compiler_params=VMEM,
        name="cut_bands",
    )(cache_keys, cache_values)


def gather_lists(lists, parts):
    seen, step = lists, 1
    while step < parts:
        order = [((d + step) % parts, d) for d in range(parts)]
        seen = jnp.concatenate([seen, lax.ppermute(seen, "cache", order)], axis=0)
        step *= 2
    return seen


def pick_rows(band, lists, me):
    parts, top = lists.shape
    width = band.shape[2]
    steps = 4
    share = parts // steps

    def kernel(me_ref, lists_ref, band_ref, out_ref):
        first = pl.program_id(0) * share

        def one(d, carry):
            row = lax.rem(first + d - me_ref[0] + parts, parts)
            for j in range(top):
                out_ref[d, j] = band_ref[lists_ref[row, j]]
            return carry

        lax.fori_loop(0, share, one, 0, unroll=2)

    return pl.pallas_call(
        kernel,
        grid_spec=pltpu.PrefetchScalarGridSpec(
            num_scalar_prefetch=2,
            grid=(steps,),
            in_specs=[whole(band.shape)],
            out_specs=pl.BlockSpec((share, top, ROWS, width), lambda s, *_: (s, 0, 0, 0)),
        ),
        out_shape=jax.ShapeDtypeStruct((parts, top, ROWS, width), band.dtype),
        compiler_params=VMEM,
        name="pick_rows",
    )(me, lists, band)


def cut_heads(query, qkeys, qvalues, me, tp):
    tokens, width = query.shape[0], query.shape[1] // tp
    small = qkeys.shape[1] // tp

    def kernel(me_ref, q_ref, k_ref, v_ref, *outs):
        for k in range(tp):
            to = lax.rem(me_ref[0] + k, tp)
            big = pl.ds(pl.multiple_of(to * width, width), width)
            own = pl.ds(pl.multiple_of(to * small, small), small)
            outs[k][:, :width] = q_ref[:, big]
            outs[k][:, width : width + small] = k_ref[:, own]
            outs[k][:, width + small :] = v_ref[:, own]

    total = width + 2 * small
    return pl.pallas_call(
        kernel,
        grid_spec=pltpu.PrefetchScalarGridSpec(
            num_scalar_prefetch=1,
            grid=(1,),
            in_specs=[whole(query.shape), whole(qkeys.shape), whole(qvalues.shape)],
            out_specs=[whole((tokens, total))] * tp,
        ),
        out_shape=[jax.ShapeDtypeStruct((tokens, total), query.dtype)] * tp,
        compiler_params=VMEM,
        name="cut_heads",
    )(me, query, qkeys, qvalues)


def attend(parts_q, received, me, group):
    tp = len(parts_q)
    tokens, total = parts_q[0].shape
    qlen = tp * tokens
    width = group * HD
    bands, top, rows, _ = received.shape
    half = bands // 2
    keys_n = half * top * rows
    per = 2
    chunk = 512
    factor = HD ** (-0.5) * LOG2E

    def kernel(me_ref, *refs):
        q_refs = refs[:tp]
        k_ref, v_ref, out_ref, scores, weights, values = refs[tp:]
        mine = me_ref[0]

        @pl.when(pl.program_id(0) == 0)
        def _():
            values[:, HD:] = jnp.ones((keys_n + qlen, HD), values.dtype)
            values[:keys_n, :HD] = v_ref[...].reshape(keys_n, HD)
            for k in range(tp):
                values[keys_n + k * tokens : keys_n + (k + 1) * tokens, :HD] = q_refs[k][:, width + HD :]

        def position(axis):
            index = lax.broadcasted_iota(jnp.int32, (qlen, qlen), axis)
            owner = lax.bitwise_and(mine - index // tokens + tp, tp - 1)
            return owner * tokens + lax.rem(index, tokens)

        sees = position(0) >= position(1)
        own_keys = jnp.concatenate([q_refs[k][:, width : width + HD] for k in range(tp)], axis=0)
        dims = (((1,), (1,)), ((), ()))
        for p in range(per):
            at = pl.ds(pl.multiple_of((pl.program_id(0) * per + p) * HD, HD), HD)
            q = jnp.concatenate([q_refs[k][:, at] for k in range(tp)], axis=0)
            s = lax.dot_general(q, own_keys, dims, preferred_element_type=jnp.float32)
            s = jnp.where(sees, s, -jnp.inf)
            scores[p, :, keys_n:] = s
            most = functools.reduce(jnp.maximum, [s[:, i : i + HD] for i in range(0, qlen, HD)])
            for c in range(0, keys_n, chunk):
                keys = k_ref[c // (top * rows) : (c + chunk) // (top * rows)].reshape(chunk, HD)
                s = lax.dot_general(q, keys, dims, preferred_element_type=jnp.float32)
                scores[p, :, c : c + chunk] = s
                most = functools.reduce(jnp.maximum, [s[:, i : i + HD] for i in range(0, chunk, HD)], most)
            m = jnp.max(most, axis=1, keepdims=True)
            for c in range(0, keys_n + qlen, 256):
                s = scores[p, :, c : c + 256]
                weights[p, :, c : c + 256] = jnp.exp2((s - m) * factor).astype(weights.dtype)
            o = jnp.dot(weights[p], values[...], preferred_element_type=jnp.float32)
            o = (o[:, :HD] / o[:, HD:]).astype(out_ref.dtype)
            for k in range(tp):
                owner = lax.bitwise_and(mine - k + tp, tp - 1)
                out_ref[owner, :, p * HD : (p + 1) * HD] = o[k * tokens : (k + 1) * tokens]

    return pl.pallas_call(
        kernel,
        grid_spec=pltpu.PrefetchScalarGridSpec(
            num_scalar_prefetch=1,
            grid=(group // per,),
            in_specs=[whole((tokens, total))] * tp
            + [
                pl.BlockSpec((half, top, rows, HD), lambda s, *_: (0, 0, 0, 0)),
                pl.BlockSpec((half, top, rows, HD), lambda s, *_: (1, 0, 0, 0)),
            ],
            out_specs=pl.BlockSpec((tp, tokens, per * HD), lambda s, *_: (0, 0, s)),
            scratch_shapes=[
                pltpu.VMEM((per, qlen, keys_n + qlen), jnp.float32),
                pltpu.VMEM((per, qlen, keys_n + qlen), jnp.bfloat16),
                pltpu.VMEM((keys_n + qlen, 2 * HD), jnp.bfloat16),
            ],
        ),
        out_shape=jax.ShapeDtypeStruct((tp, tokens, width), jnp.bfloat16),
        compiler_params=VMEM,
        cost_estimate=pl.CostEstimate(
            flops=4 * group * qlen * (keys_n + qlen) * HD,
            bytes_accessed=2 * keys_n * HD * 2,
            transcendentals=group * qlen * (keys_n + qlen),
        ),
        name="attend",
    )(me, *parts_q, received, received)


def solution(mesh):
    parts, tp = mesh.shape["cache"], mesh.shape["tp"]

    def local(query, qkeys, qvalues, cache_keys, cache_values, lists):
        at_cache = lax.axis_index("cache").reshape(1).astype(jnp.int32)
        at_tp = lax.axis_index("tp").reshape(1).astype(jnp.int32)
        owned = cache_keys.shape[0]
        group = query.shape[2] // qkeys.shape[2]

        banded = lax.all_to_all(
            cut_bands(cache_keys, cache_values, parts), "cache", split_axis=0, concat_axis=0, tiled=True
        )
        seen = gather_lists(lists, parts)
        cuts = cut_heads(query[0], qkeys[0], qvalues[0], at_tp, tp)
        parts_q = [cuts[0]] + [
            lax.ppermute(cuts[k], "tp", [(d, (d + k) % tp) for d in range(tp)]) for k in range(1, tp)
        ]
        picked = pick_rows(banded.reshape(parts * owned, ROWS, HD), seen, at_cache)
        received = lax.all_to_all(picked, "cache", split_axis=0, concat_axis=0, tiled=True)
        result = attend(parts_q, received, at_tp, group)
        back = lax.all_to_all(result, "tp", split_axis=0, concat_axis=0, tiled=True)
        tokens = back.shape[1]
        return back.transpose(1, 0, 2).reshape(1, tokens, tp * group * HD)

    return jax.shard_map(
        local,
        mesh=mesh,
        in_specs=(
            P("cache", "tp", None),
            P("cache", "tp", None),
            P("cache", "tp", None),
            P("cache", None, "tp"),
            P("cache", None, "tp"),
            P("cache", None),
        ),
        out_specs=P("cache", "tp", None),
        check_vma=False,
    )
```

time: 324 us -> 189 us (0.58)
  blocking collectives: 101 us -> 23.2 us
  other arithmetic: 66.5 us -> 0.03 us
  starting transfers between devices: 44.1 us -> 87.3 us
  local copies, waits for them, and re-layouts: 45.9 us -> 3.49 us
  matrix products: 31 us -> 0 us
  Pallas kernels: 0 us -> 20.9 us
  waiting for transfers between devices: 33.1 us -> 52.4 us
    unnamed x4 -> x0, other arithmetic: 53.4 us -> none
    ppermute x0 -> x13, starting transfers between devices: none -> 53.4 us  [the longest x7 28.4 us: local(): lax.ppermute(cuts[k], 'tp', [(d, (d + k) % tp) for d in range(tp)])]
    all_gather x1 -> x0, blocking collectives: 41.4 us -> none  [local(): all_lists = lax.all_gather(lists, 'cache', axis=0, tiled=True)]
    all_to_all x2 -> x1, blocking collectives: 59.3 us -> 23.2 us  [local(): back = lax.all_to_all(result, 'tp', split_axis=0, concat_axis=0, tiled=True)]
    ppermute x0 -> x13, waiting for transfers between devices: none -> 34.8 us  [the longest x6 29.8 us: gather_lists(): seen = jnp.concatenate([seen, lax.ppermute(seen, 'cache', order)], axis=0)]
    dot_general x18 -> x0, matrix products: 31 us -> none  [the longest x9 24.8 us: one_head(): jnp.einsum('gqn,nd->gqd', rounded, value_h, preferred_element_type=jnp.fl...]
    unnamed x29 -> x12, local copies, waits for them, and re-layouts: 26.8 us -> 2.1 us
    pallas_call x0 -> x4, Pallas kernels: none -> 20.9 us  [the longest x1 16.2 us: attend(): pl.pallas_call(kernel, grid_spec=pltpu.PrefetchScalarGridSpec(num_scalar_...]
  transfers between devices with their start and end apart: 6 -> 15, of which waited for: 4 -> 9; matrix products, arithmetic and copies ran while one was open for 27% -> 0% of each run, Pallas kernels for 0% -> 0%
where the time goes in v1:
time: 189 us; the launch traced here: 188 us
  starting transfers between devices  87.3 us (46%)
  waiting for transfers between devices  52.4 us (28%)
  blocking collectives  23.2 us (12%)
  Pallas kernels  20.9 us (11%)
  local copies, waits for them, and re-layouts  3.49 us (2%)
    ppermute x6, waiting for transfers between devices, gather_lists(): seen = jnp.concatenate([seen, lax.ppermute(seen, 'cache', order)], axis=0)  29.8 us
    ppermute x7, starting transfers between devices, local(): lax.ppermute(cuts[k], 'tp', [(d, (d + k) % tp) for d in range(tp)])  28.4 us
    ppermute x6, starting transfers between devices, gather_lists(): seen = jnp.concatenate([seen, lax.ppermute(seen, 'cache', order)], axis=0)  25 us
    all_to_all x1, blocking collectives, local(): back = lax.all_to_all(result, 'tp', split_axis=0, concat_axis=0, tiled=True)  23.2 us
    all_to_all x1, starting transfers between devices, local(): lax.all_to_all(picked, 'cache', split_axis=0, concat_axis=0, tiled=True)  19.1 us
    all_to_all x1, waiting for transfers between devices, local(): lax.all_to_all(picked, 'cache', split_axis=0, concat_axis=0, tiled=True)  17.6 us
    pallas_call x1, Pallas kernels, attend(): pl.pallas_call(kernel, grid_spec=pltpu.PrefetchScalarGridSpec(num_scalar_...  16.2 us
    all_to_all x1, starting transfers between devices, local(): lax.all_to_all(cut_bands(cache_keys, cache_values, parts), 'cache', split...  14.8 us
  transfers between devices with their start and end apart: 15, of which 9 were waited for; matrix products, arithmetic and copies ran while one was open for 0% of the time, Pallas kernels for 0%

profile of v1, /device:TPU:1, one launch (start us, length us, event | category | flops | bytes accessed | tf_op | source)
XLA Modules:
  0.0 187.5 jit_solution(16427752227337955068)
XLA Ops:
  3.2 14.8 %all-to-all-start = ((bf16[64,4,16,128]{3,2,1,0:T(8,128)(2,1)}), bf16[64,4,16,128]{3,2,1,0:T(8,128)(2,1)S(1)}, u32[]{:S(2)}, u32[]{:S(2)}) async-start(bf16[64,4,16,128]{3,2,1,0:T(8,128)(2,1)} %cut_bands.1), calls=%async_computation | async-start | bytes 2097152 | tf_op jit(solution)/shard_map/all_to_all | solution.py:196
  18.1 2.4 %collective-permute-start.7 = (s32[1,8]{1,0:T(1,128)S(1)}, s32[1,8]{1,0:T(1,128)S(1)}, u32[]{:S(2)}, u32[]{:S(2)}) collective-permute-start(s32[1,8]{1,0:T(1,128)S(1)} %copy-done.5), channel_id=1, source_target_pairs={{8,0},{16,8},{24,16},{32,24},{40,32},{48,40},{56,48},{64,56},{72,6... | collective-permute-start | bytes 104 | tf_op jit(solution)/shard_map/ppermute | solution.py:41
  20.4 22.5 %collective-permute-done.7 = s32[1,8]{1,0:T(1,128)S(1)} collective-permute-done((s32[1,8]{1,0:T(1,128)S(1)}, s32[1,8]{1,0:T(1,128)S(1)}, u32[]{:S(2)}, u32[]{:S(2)}) %collective-permute-start.7) | collective-permute-done | bytes 64 | tf_op jit(solution)/shard_map/ppermute | solution.py:41
  43.0 2.9 %collective-permute-start.8 = (s32[2,8]{1,0:T(2,128)S(1)}, s32[2,8]{1,0:T(2,128)S(1)}, u32[]{:S(2)}, u32[]{:S(2)}) collective-permute-start(s32[2,8]{1,0:T(2,128)S(1)} %pad_add_fusion.2), channel_id=1, source_target_pairs={{16,0},{24,8},{32,16},{40,24},{48,32},{56,40},{64,48},{72,56},{80,... | collective-permute-start | bytes 200 | tf_op jit(solution)/shard_map/ppermute | solution.py:41
  45.9 1.4 collective-permute-done.8
  47.3 6.3 %collective-permute-start.9 = (s32[4,8]{1,0:T(4,128)S(1)}, s32[4,8]{1,0:T(4,128)S(1)}, u32[]{:S(2)}, u32[]{:S(2)}) collective-permute-start(s32[4,8]{1,0:T(4,128)S(1)} %pad_add_fusion.1), channel_id=1, source_target_pairs={{32,0},{40,8},{48,16},{56,24},{64,32},{72,40},{80,48},{88,56},{96,... | collective-permute-start | bytes 392 | tf_op jit(solution)/shard_map/ppermute | solution.py:41
  54.3 7.0 %collective-permute-start.10 = (s32[8,8]{1,0:T(8,128)S(1)}, s32[8,8]{1,0:T(8,128)S(1)}, u32[]{:S(2)}, u32[]{:S(2)}) collective-permute-start(s32[8,8]{1,0:T(8,128)S(1)} %pad_add_fusion), channel_id=1, source_target_pairs={{64,0},{72,8},{80,16},{88,24},{96,32},{104,40},{112,48},{120,56},{... | collective-permute-start | bytes 776 | tf_op jit(solution)/shard_map/ppermute | solution.py:41
  62.6 3.0 %collective-permute-start.11 = (s32[16,8]{1,0:T(8,128)S(1)}, s32[16,8]{1,0:T(8,128)S(1)}, u32[]{:S(2)}, u32[]{:S(2)}) collective-permute-start(s32[16,8]{1,0:T(8,128)S(1)} %concatenate.26), channel_id=1, source_target_pairs={{128,0},{136,8},{144,16},{152,24},{160,32},{168,40},{176,48},{184,... | collective-permute-start | bytes 1544 | tf_op jit(solution)/shard_map/ppermute | solution.py:41
  65.7 1.3 collective-permute-done.11
  67.0 3.4 %collective-permute-start.12 = (s32[32,8]{1,0:T(8,128)S(1)}, s32[32,8]{1,0:T(8,128)S(1)}, u32[]{:S(2)}, u32[]{:S(2)}) collective-permute-start(s32[32,8]{1,0:T(8,128)S(1)} %concatenate.27), channel_id=1, source_target_pairs={{256,0},{264,8},{272,16},{280,24},{288,32},{296,40},{304,48},{312,... | collective-permute-start | bytes 3080 | tf_op jit(solution)/shard_map/ppermute | solution.py:41
  70.4 2.6 %collective-permute-done.12 = s32[32,8]{1,0:T(8,128)S(1)} collective-permute-done((s32[32,8]{1,0:T(8,128)S(1)}, s32[32,8]{1,0:T(8,128)S(1)}, u32[]{:S(2)}, u32[]{:S(2)}) %collective-permute-start.12) | collective-permute-done | bytes 1056 | tf_op jit(solution)/shard_map/ppermute | solution.py:41
  73.0 3.4 %pick_rows.1 = bf16[64,8,16,128]{3,2,1,0:T(8,128)(2,1)} custom-call(s32[1]{0:T(128)} %bitcast.4.me_ref, s32[64,8]{1,0:T(8,128)S(1)} %concatenate.28.lists_ref, bf16[256,16,128]{2,1,0:T(8,128)(2,1)S(1)} %bitcast.7), custom_call_target="tpu_custom_call" | custom-call | tf_op jit(solution)/shard_map/pick_rows/pallas_call | solution.py:63
  76.4 19.1 %all-to-all-start.1 = ((bf16[64,8,16,128]{3,2,1,0:T(8,128)(2,1)}), bf16[64,8,16,128]{3,2,1,0:T(8,128)(2,1)S(1)}, u32[]{:S(2)}, u32[]{:S(2)}) async-start(bf16[64,8,16,128]{3,2,1,0:T(8,128)(2,1)} %pick_rows.1), calls=%async_computation.1 | async-start | bytes 4194304 | tf_op jit(solution)/shard_map/all_to_all | solution.py:205
  95.6 3.2 %collective-permute-start = (bf16[32,1280]{1,0:T(8,128)(2,1)S(1)}, bf16[32,1280]{1,0:T(8,128)(2,1)S(1)}, u32[]{:S(2)}, u32[]{:S(2)}) collective-permute-start(bf16[32,1280]{1,0:T(8,128)(2,1)S(1)} %get-tuple-element.14), channel_id=1, source_target_pairs={{0,1},{1,2},{2,3},{3,4},{4,5},{5,6},{6,7},{7,0},{8,9},{9,10},{10,1... | collective-permute-start | bytes 245768 | tf_op jit(solution)/shard_map/ppermute | solution.py:202
  98.8 4.2 %collective-permute-start.1 = (bf16[32,1280]{1,0:T(8,128)(2,1)S(1)}, bf16[32,1280]{1,0:T(8,128)(2,1)S(1)}, u32[]{:S(2)}, u32[]{:S(2)}) collective-permute-start(bf16[32,1280]{1,0:T(8,128)(2,1)S(1)} %get-tuple-element.15), channel_id=1, source_target_pairs={{0,2},{1,3},{2,4},{3,5},{4,6},{5,7},{6,0},{7,1},{8,10},{9,11},{10,... | collective-permute-start | bytes 245768 | tf_op jit(solution)/shard_map/ppermute | solution.py:202
  103.1 4.6 %collective-permute-start.2 = (bf16[32,1280]{1,0:T(8,128)(2,1)S(1)}, bf16[32,1280]{1,0:T(8,128)(2,1)S(1)}, u32[]{:S(2)}, u32[]{:S(2)}) collective-permute-start(bf16[32,1280]{1,0:T(8,128)(2,1)S(1)} %get-tuple-element.16), channel_id=1, source_target_pairs={{0,3},{1,4},{2,5},{3,6},{4,7},{5,0},{6,1},{7,2},{8,11},{9,12},{10,... | collective-permute-start | bytes 245768 | tf_op jit(solution)/shard_map/ppermute | solution.py:202
  107.7 3.5 %collective-permute-start.3 = (bf16[32,1280]{1,0:T(8,128)(2,1)S(1)}, bf16[32,1280]{1,0:T(8,128)(2,1)S(1)}, u32[]{:S(2)}, u32[]{:S(2)}) collective-permute-start(bf16[32,1280]{1,0:T(8,128)(2,1)S(1)} %get-tuple-element.17), channel_id=1, source_target_pairs={{0,4},{1,5},{2,6},{3,7},{4,0},{5,1},{6,2},{7,3},{8,12},{9,13},{10,... | collective-permute-start | bytes 245768 | tf_op jit(solution)/shard_map/ppermute | solution.py:202
  111.3 4.9 %collective-permute-start.4 = (bf16[32,1280]{1,0:T(8,128)(2,1)S(1)}, bf16[32,1280]{1,0:T(8,128)(2,1)S(1)}, u32[]{:S(2)}, u32[]{:S(2)}) collective-permute-start(bf16[32,1280]{1,0:T(8,128)(2,1)S(1)} %get-tuple-element.18), channel_id=1, source_target_pairs={{0,5},{1,6},{2,7},{3,0},{4,1},{5,2},{6,3},{7,4},{8,13},{9,14},{10,... | collective-permute-start | bytes 245768 | tf_op jit(solution)/shard_map/ppermute | solution.py:202
  116.1 5.0 %collective-permute-start.5 = (bf16[32,1280]{1,0:T(8,128)(2,1)S(1)}, bf16[32,1280]{1,0:T(8,128)(2,1)S(1)}, u32[]{:S(2)}, u32[]{:S(2)}) collective-permute-start(bf16[32,1280]{1,0:T(8,128)(2,1)S(1)} %get-tuple-element.19), channel_id=1, source_target_pairs={{0,6},{1,7},{2,0},{3,1},{4,2},{5,3},{6,4},{7,5},{8,14},{9,15},{10,... | collective-permute-start | bytes 245768 | tf_op jit(solution)/shard_map/ppermute | solution.py:202
  121.1 3.0 %collective-permute-start.6 = (bf16[32,1280]{1,0:T(8,128)(2,1)S(1)}, bf16[32,1280]{1,0:T(8,128)(2,1)S(1)}, u32[]{:S(2)}, u32[]{:S(2)}) collective-permute-start(bf16[32,1280]{1,0:T(8,128)(2,1)S(1)} %get-tuple-element.20), channel_id=1, source_target_pairs={{0,7},{1,0},{2,1},{3,2},{4,3},{5,4},{6,5},{7,6},{8,15},{9,8},{10,9... | collective-permute-start | bytes 245768 | tf_op jit(solution)/shard_map/ppermute | solution.py:202
  124.2 4.0 %collective-permute-done.5.refs_6_ = bf16[32,1280]{1,0:T(8,128)(2,1)S(1)} collective-permute-done((bf16[32,1280]{1,0:T(8,128)(2,1)S(1)}, bf16[32,1280]{1,0:T(8,128)(2,1)S(1)}, u32[]{:S(2)}, u32[]{:S(2)}) %collective-permute-start.5) | collective-permute-done | bytes 81952 | tf_op jit(solution)/shard_map/ppermute | solution.py:202
  129.1 17.6 %all-to-all-done.1.refs_8_.refs_9_ = bf16[64,8,16,128]{3,2,1,0:T(8,128)(2,1)S(1)} async-done(((bf16[64,8,16,128]{3,2,1,0:T(8,128)(2,1)}), bf16[64,8,16,128]{3,2,1,0:T(8,128)(2,1)S(1)}, u32[]{:S(2)}, u32[]{:S(2)}) %all-to-all-start.1) | async-done | bytes 2097184 | tf_op jit(solution)/shard_map/all_to_all | solution.py:205
  146.8 16.2 %attend.1 = bf16[8,32,1024]{2,1,0:T(8,128)(2,1)S(1)} custom-call(s32[1]{0:T(128)} %bitcast.me_ref, bf16[32,1280]{1,0:T(8,128)(2,1)S(1)} %get-tuple-element.13.refs_0_, bf16[32,1280]{1,0:T(8,128)(2,1)S(1)} %collective-permute-done.refs_1_, bf16[32,1280]{1,0:T(8,128)(2,1)S(1)} %collective-permute-done.1.refs_2_, ...), custom_call_target="tpu_custom_call" | custom-call | flops 4563402752 | bytes 2097152 | tf_op jit(solution)/shard_map/attend/pallas_call | solution.py:159
  163.0 23.2 %all_to_all.15 = bf16[8,32,1024]{2,1,0:T(8,128)(2,1)S(1)} all-to-all(bf16[8,32,1024]{2,1,0:T(8,128)(2,1)S(1)} %attend.1), channel_id=1, replica_groups=mesh['cache'=64,'tp'=8] {'tp'}, dimensions={0} | all-to-all | bytes 1048576 | tf_op jit(solution)/shard_map/all_to_all | solution.py:207
  (31 shorter events, 7.7 us)
Async XLA Ops:
  0.0 1.0 copy-start.1
  1.0 1.0 copy-start.2
  2.1 16.0 %copy-start.5 = (s32[1,8]{1,0:T(1,128)S(1)}, s32[1,8]{1,0:T(1,128)}, u32[]{:S(2)}) copy-start(s32[1,8]{1,0:T(1,128)} %param.11) | copy-start | bytes 100
  3.2 69.8 %all-to-all-start = ((bf16[64,4,16,128]{3,2,1,0:T(8,128)(2,1)}), bf16[64,4,16,128]{3,2,1,0:T(8,128)(2,1)S(1)}, u32[]{:S(2)}, u32[]{:S(2)}) async-start(bf16[64,4,16,128]{3,2,1,0:T(8,128)(2,1)} %cut_bands.1), calls=%async_computation | async-start | bytes 2097152 | tf_op jit(solution)/shard_map/all_to_all | solution.py:196
  18.1 24.9 %collective-permute-start.7 = (s32[1,8]{1,0:T(1,128)S(1)}, s32[1,8]{1,0:T(1,128)S(1)}, u32[]{:S(2)}, u32[]{:S(2)}) collective-permute-start(s32[1,8]{1,0:T(1,128)S(1)} %copy-done.5), channel_id=1, source_target_pairs={{8,0},{16,8},{24,16},{32,24},{40,32},{48,40},{56,48},{64,56},{72,6... | collective-permute-start | bytes 104 | tf_op jit(solution)/shard_map/ppermute | solution.py:41
  43.0 4.3 %collective-permute-start.8 = (s32[2,8]{1,0:T(2,128)S(1)}, s32[2,8]{1,0:T(2,128)S(1)}, u32[]{:S(2)}, u32[]{:S(2)}) collective-permute-start(s32[2,8]{1,0:T(2,128)S(1)} %pad_add_fusion.2), channel_id=1, source_target_pairs={{16,0},{24,8},{32,16},{40,24},{48,32},{56,40},{64,48},{72,56},{80,... | collective-permute-start | bytes 200 | tf_op jit(solution)/shard_map/ppermute | solution.py:41
  47.3 7.0 %collective-permute-start.9 = (s32[4,8]{1,0:T(4,128)S(1)}, s32[4,8]{1,0:T(4,128)S(1)}, u32[]{:S(2)}, u32[]{:S(2)}) collective-permute-start(s32[4,8]{1,0:T(4,128)S(1)} %pad_add_fusion.1), channel_id=1, source_target_pairs={{32,0},{40,8},{48,16},{56,24},{64,32},{72,40},{80,48},{88,56},{96,... | collective-permute-start | bytes 392 | tf_op jit(solution)/shard_map/ppermute | solution.py:41
  54.3 8.3 %collective-permute-start.10 = (s32[8,8]{1,0:T(8,128)S(1)}, s32[8,8]{1,0:T(8,128)S(1)}, u32[]{:S(2)}, u32[]{:S(2)}) collective-permute-start(s32[8,8]{1,0:T(8,128)S(1)} %pad_add_fusion), channel_id=1, source_target_pairs={{64,0},{72,8},{80,16},{88,24},{96,32},{104,40},{112,48},{120,56},{... | collective-permute-start | bytes 776 | tf_op jit(solution)/shard_map/ppermute | solution.py:41
  62.6 4.4 %collective-permute-start.11 = (s32[16,8]{1,0:T(8,128)S(1)}, s32[16,8]{1,0:T(8,128)S(1)}, u32[]{:S(2)}, u32[]{:S(2)}) collective-permute-start(s32[16,8]{1,0:T(8,128)S(1)} %concatenate.26), channel_id=1, source_target_pairs={{128,0},{136,8},{144,16},{152,24},{160,32},{168,40},{176,48},{184,... | collective-permute-start | bytes 1544 | tf_op jit(solution)/shard_map/ppermute | solution.py:41
  67.0 6.0 %collective-permute-start.12 = (s32[32,8]{1,0:T(8,128)S(1)}, s32[32,8]{1,0:T(8,128)S(1)}, u32[]{:S(2)}, u32[]{:S(2)}) collective-permute-start(s32[32,8]{1,0:T(8,128)S(1)} %concatenate.27), channel_id=1, source_target_pairs={{256,0},{264,8},{272,16},{280,24},{288,32},{296,40},{304,48},{312,... | collective-permute-start | bytes 3080 | tf_op jit(solution)/shard_map/ppermute | solution.py:41
  76.4 19.1 %copy-start = (bf16[1,32,8192]{2,1,0:T(8,128)(2,1)S(1)}, bf16[1,32,8192]{2,1,0:T(8,128)(2,1)}, u32[]{:S(2)}) copy-start(bf16[1,32,8192]{2,1,0:T(8,128)(2,1)} %param.6) | copy-start | bytes 1572868
  76.4 19.1 %copy-start.3 = (bf16[1,32,1024]{2,1,0:T(8,128)(2,1)S(1)}, bf16[1,32,1024]{2,1,0:T(8,128)(2,1)}, u32[]{:S(2)}) copy-start(bf16[1,32,1024]{2,1,0:T(8,128)(2,1)} %param.7) | copy-start | bytes 196612
  76.4 19.1 %copy-start.4 = (bf16[1,32,1024]{2,1,0:T(8,128)(2,1)S(1)}, bf16[1,32,1024]{2,1,0:T(8,128)(2,1)}, u32[]{:S(2)}) copy-start(bf16[1,32,1024]{2,1,0:T(8,128)(2,1)} %param.8) | copy-start | bytes 196612
  76.4 70.3 %all-to-all-start.1 = ((bf16[64,8,16,128]{3,2,1,0:T(8,128)(2,1)}), bf16[64,8,16,128]{3,2,1,0:T(8,128)(2,1)S(1)}, u32[]{:S(2)}, u32[]{:S(2)}) async-start(bf16[64,8,16,128]{3,2,1,0:T(8,128)(2,1)} %pick_rows.1), calls=%async_computation.1 | async-start | bytes 4194304 | tf_op jit(solution)/shard_map/all_to_all | solution.py:205
  95.6 20.5 %collective-permute-start = (bf16[32,1280]{1,0:T(8,128)(2,1)S(1)}, bf16[32,1280]{1,0:T(8,128)(2,1)S(1)}, u32[]{:S(2)}, u32[]{:S(2)}) collective-permute-start(bf16[32,1280]{1,0:T(8,128)(2,1)S(1)} %get-tuple-element.14), channel_id=1, source_target_pairs={{0,1},{1,2},{2,3},{3,4},{4,5},{5,6},{6,7},{7,0},{8,9},{9,10},{10,1... | collective-permute-start | bytes 245768 | tf_op jit(solution)/shard_map/ppermute | solution.py:202
  98.8 22.3 %collective-permute-start.1 = (bf16[32,1280]{1,0:T(8,128)(2,1)S(1)}, bf16[32,1280]{1,0:T(8,128)(2,1)S(1)}, u32[]{:S(2)}, u32[]{:S(2)}) collective-permute-start(bf16[32,1280]{1,0:T(8,128)(2,1)S(1)} %get-tuple-element.15), channel_id=1, source_target_pairs={{0,2},{1,3},{2,4},{3,5},{4,6},{5,7},{6,0},{7,1},{8,10},{9,11},{10,... | collective-permute-start | bytes 245768 | tf_op jit(solution)/shard_map/ppermute | solution.py:202
  103.1 21.1 %collective-permute-start.2 = (bf16[32,1280]{1,0:T(8,128)(2,1)S(1)}, bf16[32,1280]{1,0:T(8,128)(2,1)S(1)}, u32[]{:S(2)}, u32[]{:S(2)}) collective-permute-start(bf16[32,1280]{1,0:T(8,128)(2,1)S(1)} %get-tuple-element.16), channel_id=1, source_target_pairs={{0,3},{1,4},{2,5},{3,6},{4,7},{5,0},{6,1},{7,2},{8,11},{9,12},{10,... | collective-permute-start | bytes 245768 | tf_op jit(solution)/shard_map/ppermute | solution.py:202
  107.7 16.4 %collective-permute-start.3 = (bf16[32,1280]{1,0:T(8,128)(2,1)S(1)}, bf16[32,1280]{1,0:T(8,128)(2,1)S(1)}, u32[]{:S(2)}, u32[]{:S(2)}) collective-permute-start(bf16[32,1280]{1,0:T(8,128)(2,1)S(1)} %get-tuple-element.17), channel_id=1, source_target_pairs={{0,4},{1,5},{2,6},{3,7},{4,0},{5,1},{6,2},{7,3},{8,12},{9,13},{10,... | collective-permute-start | bytes 245768 | tf_op jit(solution)/shard_map/ppermute | solution.py:202
  111.3 12.9 %collective-permute-start.4 = (bf16[32,1280]{1,0:T(8,128)(2,1)S(1)}, bf16[32,1280]{1,0:T(8,128)(2,1)S(1)}, u32[]{:S(2)}, u32[]{:S(2)}) collective-permute-start(bf16[32,1280]{1,0:T(8,128)(2,1)S(1)} %get-tuple-element.18), channel_id=1, source_target_pairs={{0,5},{1,6},{2,7},{3,0},{4,1},{5,2},{6,3},{7,4},{8,13},{9,14},{10,... | collective-permute-start | bytes 245768 | tf_op jit(solution)/shard_map/ppermute | solution.py:202
  116.1 12.0 %collective-permute-start.5 = (bf16[32,1280]{1,0:T(8,128)(2,1)S(1)}, bf16[32,1280]{1,0:T(8,128)(2,1)S(1)}, u32[]{:S(2)}, u32[]{:S(2)}) collective-permute-start(bf16[32,1280]{1,0:T(8,128)(2,1)S(1)} %get-tuple-element.19), channel_id=1, source_target_pairs={{0,6},{1,7},{2,0},{3,1},{4,2},{5,3},{6,4},{7,5},{8,14},{9,15},{10,... | collective-permute-start | bytes 245768 | tf_op jit(solution)/shard_map/ppermute | solution.py:202
  121.1 8.0 %collective-permute-start.6 = (bf16[32,1280]{1,0:T(8,128)(2,1)S(1)}, bf16[32,1280]{1,0:T(8,128)(2,1)S(1)}, u32[]{:S(2)}, u32[]{:S(2)}) collective-permute-start(bf16[32,1280]{1,0:T(8,128)(2,1)S(1)} %get-tuple-element.20), channel_id=1, source_target_pairs={{0,7},{1,0},{2,1},{3,2},{4,3},{5,4},{6,5},{7,6},{8,15},{9,8},{10,9... | collective-permute-start | bytes 245768 | tf_op jit(solution)/shard_map/ppermute | solution.py:202

commit v2 on v1

--- a/solution.py
+++ b/solution.py
@@ -8,6 +8,7 @@
 from jax.sharding import PartitionSpec as P
 
 HD = 128
+EXTRA = 8
 ROWS = 16
 LOG2E = 1.4426950408889634
 VMEM = pltpu.CompilerParams(vmem_limit_bytes=48 * 1024 * 1024)
@@ -20,42 +21,39 @@
 def cut_bands(cache_keys, cache_values, parts):
     owned, plen, width = cache_keys.shape
     half = parts // 2
+    rows = owned * ROWS
 
     def kernel(k_ref, v_ref, out_ref):
         for i in range(owned):
-            out_ref[:half, i] = k_ref[i].reshape(half, ROWS, width)
-            out_ref[half:, i] = v_ref[i].reshape(half, ROWS, width)
-
-    return pl.pallas_call(
-        kernel,
-        out_shape=jax.ShapeDtypeStruct((parts, owned, ROWS, width), cache_keys.dtype),
+            at = slice(i * ROWS, (i + 1) * ROWS)
+            out_ref[:half, at] = k_ref[i].reshape(half, ROWS, width)
+            out_ref[half:, at] = v_ref[i].reshape(half, ROWS, width)
+
+    return pl.pallas_call(
+        kernel,
+        grid=(1,),
+        in_specs=[whole(cache_keys.shape), whole(cache_values.shape)],
+        out_specs=whole((parts, rows, width)),
+        out_shape=jax.ShapeDtypeStruct((parts, rows + EXTRA, width), cache_keys.dtype),
         compiler_params=VMEM,
         name="cut_bands",
     )(cache_keys, cache_values)
 
 
-def gather_lists(lists, parts):
-    seen, step = lists, 1
-    while step < parts:
-        order = [((d + step) % parts, d) for d in range(parts)]
-        seen = jnp.concatenate([seen, lax.ppermute(seen, "cache", order)], axis=0)
-        step *= 2
-    return seen
-
-
-def pick_rows(band, lists, me):
+def pick_rows(bands, lists, owned):
     parts, top = lists.shape
-    width = band.shape[2]
+    width = bands.shape[2]
     steps = 4
     share = parts // steps
 
-    def kernel(me_ref, lists_ref, band_ref, out_ref):
+    def kernel(lists_ref, bands_ref, out_ref):
         first = pl.program_id(0) * share
 
         def one(d, carry):
-            row = lax.rem(first + d - me_ref[0] + parts, parts)
             for j in range(top):
-                out_ref[d, j] = band_ref[lists_ref[row, j]]
+                passage = lists_ref[first + d, j]
+                at = pl.multiple_of(lax.rem(passage, owned) * ROWS, ROWS)
+                out_ref[d, j] = bands_ref[lax.div(passage, owned), pl.ds(at, ROWS)]
             return carry
 
         lax.fori_loop(0, share, one, 0, unroll=2)
@@ -63,15 +61,15 @@
     return pl.pallas_call(
         kernel,
         grid_spec=pltpu.PrefetchScalarGridSpec(
-            num_scalar_prefetch=2,
+            num_scalar_prefetch=1,
             grid=(steps,),
-            in_specs=[whole(band.shape)],
+            in_specs=[whole((parts, owned * ROWS, width))],
             out_specs=pl.BlockSpec((share, top, ROWS, width), lambda s, *_: (s, 0, 0, 0)),
         ),
-        out_shape=jax.ShapeDtypeStruct((parts, top, ROWS, width), band.dtype),
+        out_shape=jax.ShapeDtypeStruct((parts, top, ROWS, width), bands.dtype),
         compiler_params=VMEM,
         name="pick_rows",
-    )(me, lists, band)
+    )(lists, bands)
 
 
 def cut_heads(query, qkeys, qvalues, me, tp):
@@ -188,20 +186,21 @@
     parts, tp = mesh.shape["cache"], mesh.shape["tp"]
 
     def local(query, qkeys, qvalues, cache_keys, cache_values, lists):
-        at_cache = lax.axis_index("cache").reshape(1).astype(jnp.int32)
         at_tp = lax.axis_index("tp").reshape(1).astype(jnp.int32)
         owned = cache_keys.shape[0]
         group = query.shape[2] // qkeys.shape[2]
 
-        banded = lax.all_to_all(
-            cut_bands(cache_keys, cache_values, parts), "cache", split_axis=0, concat_axis=0, tiled=True
-        )
-        seen = gather_lists(lists, parts)
+        bands = cut_bands(cache_keys, cache_values, parts)
+        top = lists.shape[1]
+        note = jnp.pad(lists.astype(bands.dtype), ((0, EXTRA - 1), (0, bands.shape[2] - top)))
+        bands = bands.at[:, owned * ROWS :].set(note[None])
+        bands = lax.all_to_all(bands, "cache", split_axis=0, concat_axis=0, tiled=True)
+        seen = bands[:, owned * ROWS, :top].astype(jnp.int32)
         cuts = cut_heads(query[0], qkeys[0], qvalues[0], at_tp, tp)
         parts_q = [cuts[0]] + [
             lax.ppermute(cuts[k], "tp", [(d, (d + k) % tp) for d in range(tp)]) for k in range(1, tp)
         ]
-        picked = pick_rows(banded.reshape(parts * owned, ROWS, HD), seen, at_cache)
+        picked = pick_rows(bands, seen, owned)
         received = lax.all_to_all(picked, "cache", split_axis=0, concat_axis=0, tiled=True)
         result = attend(parts_q, received, at_tp, group)
         back = lax.all_to_all(result, "tp", split_axis=0, concat_axis=0, tiled=True)

time: 189 us -> 153 us (0.81)
  starting transfers between devices: 87.3 us -> 34.7 us
  blocking collectives: 23.2 us -> 69.2 us
  waiting for transfers between devices: 52.4 us -> 22.6 us
    all_to_all x0 -> x1, blocking collectives: none -> 46 us  [local(): lax.all_to_all(bands, 'cache', split_axis=0, concat_axis=0, tiled=True)]
    ppermute x6 -> x0, waiting for transfers between devices: 29.8 us -> none  [gather_lists(): seen = jnp.concatenate([seen, lax.ppermute(seen, 'cache', order)], axis=0)]
    ppermute x6 -> x0, starting transfers between devices: 25 us -> none  [gather_lists(): seen = jnp.concatenate([seen, lax.ppermute(seen, 'cache', order)], axis=0)]
    all_to_all x1 -> x0, starting transfers between devices: 14.8 us -> none  [local(): lax.all_to_all(cut_bands(cache_keys, cache_values, parts), 'cache', split...]
    all_to_all x1, starting transfers between devices: 19.1 us -> 6.32 us  [local(): lax.all_to_all(picked, 'cache', split_axis=0, concat_axis=0, tiled=True)]
  transfers between devices with their start and end apart: 15 -> 8, of which waited for: 9 -> 3; matrix products, arithmetic and copies ran while one was open for 0% -> 0% of each run, Pallas kernels for 0% -> 0%
where the time goes in v2:
time: 153 us; the launch traced here: 152 us
  blocking collectives  69.2 us (45%)
  starting transfers between devices  34.7 us (23%)
  waiting for transfers between devices  22.6 us (15%)
  Pallas kernels  21.2 us (14%)
  local copies, waits for them, and re-layouts  3.47 us (2%)
    all_to_all x1, blocking collectives, local(): lax.all_to_all(bands, 'cache', split_axis=0, concat_axis=0, tiled=True)  46 us
    ppermute x7, starting transfers between devices, local(): lax.ppermute(cuts[k], 'tp', [(d, (d + k) % tp) for d in range(tp)])  28.4 us
    all_to_all x1, blocking collectives, local(): back = lax.all_to_all(result, 'tp', split_axis=0, concat_axis=0, tiled=True)  23.2 us
    all_to_all x1, waiting for transfers between devices, local(): lax.all_to_all(picked, 'cache', split_axis=0, concat_axis=0, tiled=True)  17.6 us
    pallas_call x1, Pallas kernels, attend(): pl.pallas_call(kernel, grid_spec=pltpu.PrefetchScalarGridSpec(num_scalar_...  16.2 us
    all_to_all x1, starting transfers between devices, local(): lax.all_to_all(picked, 'cache', split_axis=0, concat_axis=0, tiled=True)  6.32 us
    ppermute x7, waiting for transfers between devices, local(): lax.ppermute(cuts[k], 'tp', [(d, (d + k) % tp) for d in range(tp)])  4.98 us
    pallas_call x1, Pallas kernels, pick_rows(): pl.pallas_call(kernel, grid_spec=pltpu.PrefetchScalarGridSpec(num_scalar_...  4.65 us
  transfers between devices with their start and end apart: 8, of which 3 were waited for; matrix products, arithmetic and copies ran while one was open for 0% of the time, Pallas kernels for 0%

profile of v2, /device:TPU:1, one launch (start us, length us, event | category | flops | bytes accessed | tf_op | source)
XLA Modules:
  0.0 152.0 jit_solution(14775128949113117242)
XLA Ops:
  0.0 0.7 convert_element_type.10
  0.7 1.0 copy-done
  1.7 1.0 copy-done.1
  2.8 0.2 cut_bands.1
  3.0 46.0 %all_to_all.15.bands_ref = bf16[64,72,128]{2,1,0:T(8,128)(2,1)S(1)} all-to-all(bf16[64,72,128]{2,1,0:T(8,128)(2,1)S(1)} %broadcast_dynamic-update-slice_fusion), channel_id=1, replica_groups=mesh['cache'=64,'tp'=8] {'cache'}, dimensions={0} | all-to-all | bytes 2359296 | tf_op jit(solution)/shard_map/all_to_all | solution.py:197
  49.0 4.6 %pick_rows.1 = bf16[64,8,16,128]{3,2,1,0:T(8,128)(2,1)} custom-call(s32[64,8]{1,0:T(8,128)S(1)} %bitcast.7, bf16[64,72,128]{2,1,0:T(8,128)(2,1)S(1)} %all_to_all.15.bands_ref), custom_call_target="tpu_custom_call" | custom-call | tf_op jit(solution)/shard_map/pick_rows/pallas_call | solution.py:61
  53.7 6.3 %all-to-all-start.1 = ((bf16[64,8,16,128]{3,2,1,0:T(8,128)(2,1)}), bf16[64,8,16,128]{3,2,1,0:T(8,128)(2,1)S(1)}, u32[]{:S(2)}, u32[]{:S(2)}) async-start(bf16[64,8,16,128]{3,2,1,0:T(8,128)(2,1)} %pick_rows.1), calls=%async_computation.1 | async-start | bytes 4194304 | tf_op jit(solution)/shard_map/all_to_all | solution.py:204
  60.1 0.1 cut_heads.1
  60.1 3.2 %collective-permute-start = (bf16[32,1280]{1,0:T(8,128)(2,1)S(1)}, bf16[32,1280]{1,0:T(8,128)(2,1)S(1)}, u32[]{:S(2)}, u32[]{:S(2)}) collective-permute-start(bf16[32,1280]{1,0:T(8,128)(2,1)S(1)} %get-tuple-element.26), channel_id=1, source_target_pairs={{0,1},{1,2},{2,3},{3,4},{4,5},{5,6},{6,7},{7,0},{8,9},{9,10},{10,1... | collective-permute-start | bytes 245768 | tf_op jit(solution)/shard_map/ppermute | solution.py:201
  63.4 4.2 %collective-permute-start.1 = (bf16[32,1280]{1,0:T(8,128)(2,1)S(1)}, bf16[32,1280]{1,0:T(8,128)(2,1)S(1)}, u32[]{:S(2)}, u32[]{:S(2)}) collective-permute-start(bf16[32,1280]{1,0:T(8,128)(2,1)S(1)} %get-tuple-element.27), channel_id=1, source_target_pairs={{0,2},{1,3},{2,4},{3,5},{4,6},{5,7},{6,0},{7,1},{8,10},{9,11},{10,... | collective-permute-start | bytes 245768 | tf_op jit(solution)/shard_map/ppermute | solution.py:201
  67.6 4.6 %collective-permute-start.2 = (bf16[32,1280]{1,0:T(8,128)(2,1)S(1)}, bf16[32,1280]{1,0:T(8,128)(2,1)S(1)}, u32[]{:S(2)}, u32[]{:S(2)}) collective-permute-start(bf16[32,1280]{1,0:T(8,128)(2,1)S(1)} %get-tuple-element.28), channel_id=1, source_target_pairs={{0,3},{1,4},{2,5},{3,6},{4,7},{5,0},{6,1},{7,2},{8,11},{9,12},{10,... | collective-permute-start | bytes 245768 | tf_op jit(solution)/shard_map/ppermute | solution.py:201
  72.2 3.5 %collective-permute-start.3 = (bf16[32,1280]{1,0:T(8,128)(2,1)S(1)}, bf16[32,1280]{1,0:T(8,128)(2,1)S(1)}, u32[]{:S(2)}, u32[]{:S(2)}) collective-permute-start(bf16[32,1280]{1,0:T(8,128)(2,1)S(1)} %get-tuple-element.29), channel_id=1, source_target_pairs={{0,4},{1,5},{2,6},{3,7},{4,0},{5,1},{6,2},{7,3},{8,12},{9,13},{10,... | collective-permute-start | bytes 245768 | tf_op jit(solution)/shard_map/ppermute | solution.py:201
  75.8 4.9 %collective-permute-start.4 = (bf16[32,1280]{1,0:T(8,128)(2,1)S(1)}, bf16[32,1280]{1,0:T(8,128)(2,1)S(1)}, u32[]{:S(2)}, u32[]{:S(2)}) collective-permute-start(bf16[32,1280]{1,0:T(8,128)(2,1)S(1)} %get-tuple-element.30), channel_id=1, source_target_pairs={{0,5},{1,6},{2,7},{3,0},{4,1},{5,2},{6,3},{7,4},{8,13},{9,14},{10,... | collective-permute-start | bytes 245768 | tf_op jit(solution)/shard_map/ppermute | solution.py:201
  80.6 0.0 collective-permute-done.refs_1_
  80.7 5.0 %collective-permute-start.5 = (bf16[32,1280]{1,0:T(8,128)(2,1)S(1)}, bf16[32,1280]{1,0:T(8,128)(2,1)S(1)}, u32[]{:S(2)}, u32[]{:S(2)}) collective-permute-start(bf16[32,1280]{1,0:T(8,128)(2,1)S(1)} %get-tuple-element.31), channel_id=1, source_target_pairs={{0,6},{1,7},{2,0},{3,1},{4,2},{5,3},{6,4},{7,5},{8,14},{9,15},{10,... | collective-permute-start | bytes 245768 | tf_op jit(solution)/shard_map/ppermute | solution.py:201
  85.6 3.0 %collective-permute-start.6 = (bf16[32,1280]{1,0:T(8,128)(2,1)S(1)}, bf16[32,1280]{1,0:T(8,128)(2,1)S(1)}, u32[]{:S(2)}, u32[]{:S(2)}) collective-permute-start(bf16[32,1280]{1,0:T(8,128)(2,1)S(1)} %get-tuple-element.32), channel_id=1, source_target_pairs={{0,7},{1,0},{2,1},{3,2},{4,3},{5,4},{6,5},{7,6},{8,15},{9,8},{10,9... | collective-permute-start | bytes 245768 | tf_op jit(solution)/shard_map/ppermute | solution.py:201
  88.6 0.0 collective-permute-done.3.refs_4_
  88.7 4.0 %collective-permute-done.5.refs_6_ = bf16[32,1280]{1,0:T(8,128)(2,1)S(1)} collective-permute-done((bf16[32,1280]{1,0:T(8,128)(2,1)S(1)}, bf16[32,1280]{1,0:T(8,128)(2,1)S(1)}, u32[]{:S(2)}, u32[]{:S(2)}) %collective-permute-start.5) | collective-permute-done | bytes 81952 | tf_op jit(solution)/shard_map/ppermute | solution.py:201
  92.7 1.0 collective-permute-done.6.refs_7_
  93.6 17.6 %all-to-all-done.1.refs_8_.refs_9_ = bf16[64,8,16,128]{3,2,1,0:T(8,128)(2,1)S(1)} async-done(((bf16[64,8,16,128]{3,2,1,0:T(8,128)(2,1)}), bf16[64,8,16,128]{3,2,1,0:T(8,128)(2,1)S(1)}, u32[]{:S(2)}, u32[]{:S(2)}) %all-to-all-start.1) | async-done | bytes 2097184 | tf_op jit(solution)/shard_map/all_to_all | solution.py:204
  111.3 16.2 %attend.1 = bf16[8,32,1024]{2,1,0:T(8,128)(2,1)S(1)} custom-call(s32[1]{0:T(128)} %bitcast.me_ref, bf16[32,1280]{1,0:T(8,128)(2,1)S(1)} %get-tuple-element.25.refs_0_, bf16[32,1280]{1,0:T(8,128)(2,1)S(1)} %collective-permute-done.refs_1_, bf16[32,1280]{1,0:T(8,128)(2,1)S(1)} %collective-permute-done.1.refs_2_, ...), custom_call_target="tpu_custom_call" | custom-call | flops 4563402752 | bytes 2097152 | tf_op jit(solution)/shard_map/attend/pallas_call | solution.py:157
  127.5 23.2 %all_to_all.16 = bf16[8,32,1024]{2,1,0:T(8,128)(2,1)S(1)} all-to-all(bf16[8,32,1024]{2,1,0:T(8,128)(2,1)S(1)} %attend.1), channel_id=1, replica_groups=mesh['cache'=64,'tp'=8] {'tp'}, dimensions={0} | all-to-all | bytes 1048576 | tf_op jit(solution)/shard_map/all_to_all | solution.py:206
  150.7 0.3 copy.7
  151.0 1.0 reshape.39
  (14 shorter events, 0.1 us)
Async XLA Ops:
  0.7 1.0 copy-start
  1.7 1.0 copy-start.1
  53.7 6.3 %copy-start.2 = (bf16[1,32,8192]{2,1,0:T(8,128)(2,1)S(1)}, bf16[1,32,8192]{2,1,0:T(8,128)(2,1)}, u32[]{:S(2)}) copy-start(bf16[1,32,8192]{2,1,0:T(8,128)(2,1)} %param.8) | copy-start | bytes 1572868
  53.7 6.3 %copy-start.3 = (bf16[1,32,1024]{2,1,0:T(8,128)(2,1)S(1)}, bf16[1,32,1024]{2,1,0:T(8,128)(2,1)}, u32[]{:S(2)}) copy-start(bf16[1,32,1024]{2,1,0:T(8,128)(2,1)} %param.9) | copy-start | bytes 196612
  53.7 6.4 %copy-start.4 = (bf16[1,32,1024]{2,1,0:T(8,128)(2,1)S(1)}, bf16[1,32,1024]{2,1,0:T(8,128)(2,1)}, u32[]{:S(2)}) copy-start(bf16[1,32,1024]{2,1,0:T(8,128)(2,1)} %param.10) | copy-start | bytes 196612
  53.7 57.6 %all-to-all-start.1 = ((bf16[64,8,16,128]{3,2,1,0:T(8,128)(2,1)}), bf16[64,8,16,128]{3,2,1,0:T(8,128)(2,1)S(1)}, u32[]{:S(2)}, u32[]{:S(2)}) async-start(bf16[64,8,16,128]{3,2,1,0:T(8,128)(2,1)} %pick_rows.1), calls=%async_computation.1 | async-start | bytes 4194304 | tf_op jit(solution)/shard_map/all_to_all | solution.py:204
  60.1 20.5 %collective-permute-start = (bf16[32,1280]{1,0:T(8,128)(2,1)S(1)}, bf16[32,1280]{1,0:T(8,128)(2,1)S(1)}, u32[]{:S(2)}, u32[]{:S(2)}) collective-permute-start(bf16[32,1280]{1,0:T(8,128)(2,1)S(1)} %get-tuple-element.26), channel_id=1, source_target_pairs={{0,1},{1,2},{2,3},{3,4},{4,5},{5,6},{6,7},{7,0},{8,9},{9,10},{10,1... | collective-permute-start | bytes 245768 | tf_op jit(solution)/shard_map/ppermute | solution.py:201
  63.4 22.3 %collective-permute-start.1 = (bf16[32,1280]{1,0:T(8,128)(2,1)S(1)}, bf16[32,1280]{1,0:T(8,128)(2,1)S(1)}, u32[]{:S(2)}, u32[]{:S(2)}) collective-permute-start(bf16[32,1280]{1,0:T(8,128)(2,1)S(1)} %get-tuple-element.27), channel_id=1, source_target_pairs={{0,2},{1,3},{2,4},{3,5},{4,6},{5,7},{6,0},{7,1},{8,10},{9,11},{10,... | collective-permute-start | bytes 245768 | tf_op jit(solution)/shard_map/ppermute | solution.py:201
  67.6 21.1 %collective-permute-start.2 = (bf16[32,1280]{1,0:T(8,128)(2,1)S(1)}, bf16[32,1280]{1,0:T(8,128)(2,1)S(1)}, u32[]{:S(2)}, u32[]{:S(2)}) collective-permute-start(bf16[32,1280]{1,0:T(8,128)(2,1)S(1)} %get-tuple-element.28), channel_id=1, source_target_pairs={{0,3},{1,4},{2,5},{3,6},{4,7},{5,0},{6,1},{7,2},{8,11},{9,12},{10,... | collective-permute-start | bytes 245768 | tf_op jit(solution)/shard_map/ppermute | solution.py:201
  72.2 16.4 %collective-permute-start.3 = (bf16[32,1280]{1,0:T(8,128)(2,1)S(1)}, bf16[32,1280]{1,0:T(8,128)(2,1)S(1)}, u32[]{:S(2)}, u32[]{:S(2)}) collective-permute-start(bf16[32,1280]{1,0:T(8,128)(2,1)S(1)} %get-tuple-element.29), channel_id=1, source_target_pairs={{0,4},{1,5},{2,6},{3,7},{4,0},{5,1},{6,2},{7,3},{8,12},{9,13},{10,... | collective-permute-start | bytes 245768 | tf_op jit(solution)/shard_map/ppermute | solution.py:201
  75.8 12.9 %collective-permute-start.4 = (bf16[32,1280]{1,0:T(8,128)(2,1)S(1)}, bf16[32,1280]{1,0:T(8,128)(2,1)S(1)}, u32[]{:S(2)}, u32[]{:S(2)}) collective-permute-start(bf16[32,1280]{1,0:T(8,128)(2,1)S(1)} %get-tuple-element.30), channel_id=1, source_target_pairs={{0,5},{1,6},{2,7},{3,0},{4,1},{5,2},{6,3},{7,4},{8,13},{9,14},{10,... | collective-permute-start | bytes 245768 | tf_op jit(solution)/shard_map/ppermute | solution.py:201
  80.7 12.0 %collective-permute-start.5 = (bf16[32,1280]{1,0:T(8,128)(2,1)S(1)}, bf16[32,1280]{1,0:T(8,128)(2,1)S(1)}, u32[]{:S(2)}, u32[]{:S(2)}) collective-permute-start(bf16[32,1280]{1,0:T(8,128)(2,1)S(1)} %get-tuple-element.31), channel_id=1, source_target_pairs={{0,6},{1,7},{2,0},{3,1},{4,2},{5,3},{6,4},{7,5},{8,14},{9,15},{10,... | collective-permute-start | bytes 245768 | tf_op jit(solution)/shard_map/ppermute | solution.py:201
  85.6 8.0 %collective-permute-start.6 = (bf16[32,1280]{1,0:T(8,128)(2,1)S(1)}, bf16[32,1280]{1,0:T(8,128)(2,1)S(1)}, u32[]{:S(2)}, u32[]{:S(2)}) collective-permute-start(bf16[32,1280]{1,0:T(8,128)(2,1)S(1)} %get-tuple-element.32), channel_id=1, source_target_pairs={{0,7},{1,0},{2,1},{3,2},{4,3},{5,4},{6,5},{7,6},{8,15},{9,8},{10,9... | collective-permute-start | bytes 245768 | tf_op jit(solution)/shard_map/ppermute | solution.py:201

commit v3 on v2

v3 whole, which is shorter than its diff:
```python
import functools

import jax
import jax.numpy as jnp
from jax import lax
from jax.experimental import pallas as pl
from jax.experimental.pallas import tpu as pltpu
from jax.sharding import PartitionSpec as P

HD = 128
EXTRA = 8
ROWS = 16
LOG2E = 1.4426950408889634
VMEM = pltpu.CompilerParams(vmem_limit_bytes=48 * 1024 * 1024)


def whole(shape):
    return pl.BlockSpec(shape, lambda *_: (0,) * len(shape))


def cut_bands(cache_keys, cache_values, parts):
    owned, plen, width = cache_keys.shape
    half = parts // 2
    rows = owned * ROWS

    def kernel(k_ref, v_ref, out_ref, sems):
        copies = []
        for i in range(owned):
            at = pl.ds(i * ROWS, ROWS)
            copies.append(pltpu.make_async_copy(k_ref.at[i], out_ref.at[pl.ds(0, half), at], sems.at[0, i]))
            copies.append(pltpu.make_async_copy(v_ref.at[i], out_ref.at[pl.ds(half, half), at], sems.at[1, i]))
        for copy in copies:
            copy.start()
        for copy in copies:
            copy.wait()

    return pl.pallas_call(
        kernel,
        in_specs=[pl.BlockSpec(memory_space=pl.ANY)] * 2,
        out_specs=pl.BlockSpec(memory_space=pltpu.VMEM),
        scratch_shapes=[pltpu.SemaphoreType.DMA((2, owned))],
        out_shape=jax.ShapeDtypeStruct((parts, rows + EXTRA, width), cache_keys.dtype),
        name="cut_bands",
    )(
        cache_keys.reshape(owned, half, ROWS, width),
        cache_values.reshape(owned, half, ROWS, width),
    )


def pick_rows(bands, lists, owned):
    parts, top = lists.shape
    width = bands.shape[2]
    assert owned & (owned - 1) == 0
    shift = owned.bit_length() - 1

    def kernel(lists_ref, bands_ref, out_ref):
        def one(d, carry):
            for j in range(top):
                passage = lists_ref[d, j]
                at = pl.multiple_of(lax.bitwise_and(passage, owned - 1) * ROWS, ROWS)
                out_ref[d, j] = bands_ref[lax.shift_right_logical(passage, shift), pl.ds(at, ROWS)]
            return carry

        lax.fori_loop(0, parts, one, 0, unroll=4)

    return pl.pallas_call(
        kernel,
        in_specs=[pl.BlockSpec(memory_space=pltpu.SMEM), pl.BlockSpec(memory_space=pltpu.VMEM)],
        out_specs=pl.BlockSpec(memory_space=pltpu.VMEM),
        out_shape=jax.ShapeDtypeStruct((parts, top, ROWS, width), bands.dtype),
        compiler_params=VMEM,
        name="pick_rows",
    )(lists, bands)


def cut_heads(query, qkeys, qvalues, me, tp):
    tokens, width = query.shape[0], query.shape[1] // tp
    small = qkeys.shape[1] // tp

    def kernel(me_ref, q_ref, k_ref, v_ref, *outs):
        for k in range(tp):
            to = lax.rem(me_ref[0] + k, tp)
            big = pl.ds(pl.multiple_of(to * width, width), width)
            own = pl.ds(pl.multiple_of(to * small, small), small)
            outs[k][:, :width] = q_ref[:, big]
            outs[k][:, width : width + small] = k_ref[:, own]
            outs[k][:, width + small :] = v_ref[:, own]

    total = width + 2 * small
    return pl.pallas_call(
        kernel,
        grid_spec=pltpu.PrefetchScalarGridSpec(
            num_scalar_prefetch=1,
            grid=(1,),
            in_specs=[whole(query.shape), whole(qkeys.shape), whole(qvalues.shape)],
            out_specs=[whole((tokens, total))] * tp,
        ),
        out_shape=[jax.ShapeDtypeStruct((tokens, total), query.dtype)] * tp,
        compiler_params=VMEM,
        name="cut_heads",
    )(me, query, qkeys, qvalues)


def attend(parts_q, received, me, group):
    tp = len(parts_q)
    tokens, total = parts_q[0].shape
    qlen = tp * tokens
    width = group * HD
    bands, top, rows, _ = received.shape
    half = bands // 2
    keys_n = half * top * rows
    all_n = keys_n + qlen
    per = 2
    chunk = 512
    span = 1024
    factor = HD ** (-0.5) * LOG2E
    dims = (((1,), (1,)), ((), ()))

    def lane_max(s, most):
        pieces = [s[:, i : i + HD] for i in range(0, s.shape[1], HD)]
        return functools.reduce(jnp.maximum, pieces if most is None else [most] + pieces)

    def kernel(me_ref, *refs):
        q_refs = refs[:tp]
        k_ref, v_ref, out_ref, scores, values = refs[tp:]
        mine = me_ref[0]
        values[:, HD:] = jnp.ones((all_n, HD), values.dtype)
        values[:keys_n, :HD] = v_ref[...].reshape(keys_n, HD)
        for k in range(tp):
            values[keys_n + k * tokens : keys_n + (k + 1) * tokens, :HD] = q_refs[k][:, width + HD :]

        def position(axis):
            index = lax.broadcasted_iota(jnp.int32, (qlen, qlen), axis)
            owner = lax.bitwise_and(mine - index // tokens + tp, tp - 1)
            return owner * tokens + lax.rem(index, tokens)

        sees = jnp.concatenate([position(0) >= position(1)] * per, axis=0)
        own_keys = jnp.concatenate([q_refs[k][:, width : width + HD] for k in range(tp)], axis=0)

        def score_steps(g):
            heads = [slice((g * per + p) * HD, (g * per + p + 1) * HD) for p in range(per)]
            q = jnp.concatenate([q_refs[k][:, at] for at in heads for k in range(tp)], axis=0)

            def own_step(most):
                s = lax.dot_general(q, own_keys, dims, preferred_element_type=jnp.float32)
                s = jnp.where(sees, s, -jnp.inf)
                scores[g % 2, :, keys_n:] = s
                return lane_max(s, most)

            def step(c, most):
                keys = k_ref[c // (top * rows) : (c + chunk) // (top * rows)].reshape(chunk, HD)
                s = lax.dot_general(q, keys, dims, preferred_element_type=jnp.float32)
                scores[g % 2, :, c : c + chunk] = s
                return lane_max(s, most)

            return [own_step] + [functools.partial(step, c) for c in range(0, keys_n, chunk)]

        most = None
        for step in score_steps(0):
            most = step(most)
        spans = [(c, min(c + span, all_n)) for c in range(0, all_n, span)]
        groups = group // per
        for g in range(groups):
            m = jnp.max(most, axis=1, keepdims=True)
            steps = score_steps(g + 1) if g + 1 < groups else []
            most, total_o, done = None, None, 0
            for i, (lo, hi) in enumerate(spans):
                upto = -(-len(steps) * (i + 1) // len(spans))
                for step in steps[done:upto]:
                    most = step(most)
                done = upto
                w = jnp.exp2((scores[g % 2, :, lo:hi] - m) * factor).astype(values.dtype)
                o = jnp.dot(w, values[lo:hi], preferred_element_type=jnp.float32)
                total_o = o if total_o is None else total_o + o
            o = (total_o[:, :HD] / total_o[:, HD:]).astype(out_ref.dtype)
            for p in range(per):
                for k in range(tp):
                    owner = lax.bitwise_and(mine - k + tp, tp - 1)
                    at = p * qlen + k * tokens
                    out_ref[owner, :, (g * per + p) * HD : (g * per + p + 1) * HD] = o[at : at + tokens]

    return pl.pallas_call(
        kernel,
        grid_spec=pltpu.PrefetchScalarGridSpec(
            num_scalar_prefetch=1,
            grid=(1,),
            in_specs=[whole((tokens, total))] * tp
            + [
                pl.BlockSpec((half, top, rows, HD), lambda s, *_: (0, 0, 0, 0)),
                pl.BlockSpec((half, top, rows, HD), lambda s, *_: (1, 0, 0, 0)),
            ],
            out_specs=whole((tp, tokens, width)),
            scratch_shapes=[
                pltpu.VMEM((2, per * qlen, all_n), jnp.float32),
                pltpu.VMEM((all_n, 2 * HD), jnp.bfloat16),
            ],
        ),
        out_shape=jax.ShapeDtypeStruct((tp, tokens, width), jnp.bfloat16),
        compiler_params=VMEM,
        cost_estimate=pl.CostEstimate(
            flops=4 * group * qlen * all_n * HD,
            bytes_accessed=2 * keys_n * HD * 2,
            transcendentals=group * qlen * all_n,
        ),
        name="attend",
    )(me, *parts_q, received, received)


def solution(mesh):
    parts, tp = mesh.shape["cache"], mesh.shape["tp"]

    def local(query, qkeys, qvalues, cache_keys, cache_values, lists):
        at_tp = lax.axis_index("tp").reshape(1).astype(jnp.int32)
        owned = cache_keys.shape[0]
        group = query.shape[2] // qkeys.shape[2]

        bands = cut_bands(cache_keys, cache_values, parts)
        top = lists.shape[1]
        note = jnp.pad(lists.astype(bands.dtype), ((0, EXTRA - 1), (0, bands.shape[2] - top)))
        bands = bands.at[:, owned * ROWS :].set(note[None])
        bands = lax.all_to_all(bands, "cache", split_axis=0, concat_axis=0, tiled=True)
        seen = bands[:, owned * ROWS, :top].astype(jnp.int32)
        cuts = cut_heads(query[0], qkeys[0], qvalues[0], at_tp, tp)
        parts_q = [cuts[0]] + [
            lax.ppermute(cuts[k], "tp", [(d, (d + k) % tp) for d in range(tp)]) for k in range(1, tp)
        ]
        picked = pick_rows(bands, seen, owned)
        received = lax.all_to_all(picked, "cache", split_axis=0, concat_axis=0, tiled=True)
        result = attend(parts_q, received, at_tp, group)
        back = lax.all_to_all(result, "tp", split_axis=0, concat_axis=0, tiled=True)
        tokens = back.shape[1]
        return back.transpose(1, 0, 2).reshape(1, tokens, tp * group * HD)

    return jax.shard_map(
        local,
        mesh=mesh,
        in_specs=(
            P("cache", "tp", None),
            P("cache", "tp", None),
            P("cache", "tp", None),
            P("cache", None, "tp"),
            P("cache", None, "tp"),
            P("cache", None),
        ),
        out_specs=P("cache", "tp", None),
        check_vma=False,
    )
```

time: 153 us -> 147 us (0.961)
  Pallas kernels: 21.2 us -> 16.9 us
    pallas_call x1, Pallas kernels: 16.2 us -> 10.7 us  [attend(): pl.pallas_call(kernel, grid_spec=pltpu.PrefetchScalarGridSpec(num_scalar_...]
    unnamed x10 -> x6, local copies, waits for them, and re-layouts: 2.09 us -> 0.01 us
where the time goes in v3:
time: 147 us
  blocking collectives  69.4 us (47%)
  starting transfers between devices  34.9 us (24%)
  waiting for transfers between devices  22.4 us (15%)
  Pallas kernels  16.9 us (11%)
  local copies, waits for them, and re-layouts  2.03 us (1%)
    all_to_all x1, blocking collectives, local(): lax.all_to_all(bands, 'cache', split_axis=0, concat_axis=0, tiled=True)  46.2 us
    ppermute x7, starting transfers between devices, local(): lax.ppermute(cuts[k], 'tp', [(d, (d + k) % tp) for d in range(tp)])  28.6 us
    all_to_all x1, blocking collectives, local(): back = lax.all_to_all(result, 'tp', split_axis=0, concat_axis=0, tiled=True)  23.2 us
    all_to_all x1, waiting for transfers between devices, local(): lax.all_to_all(picked, 'cache', split_axis=0, concat_axis=0, tiled=True)  17.6 us
    pallas_call x1, Pallas kernels, attend(): pl.pallas_call(kernel, grid_spec=pltpu.PrefetchScalarGridSpec(num_scalar_...  10.7 us
    all_to_all x1, starting transfers between devices, local(): lax.all_to_all(picked, 'cache', split_axis=0, concat_axis=0, tiled=True)  6.32 us
    ppermute x7, waiting for transfers between devices, local(): lax.ppermute(cuts[k], 'tp', [(d, (d + k) % tp) for d in range(tp)])  4.8 us
    pallas_call x1, Pallas kernels, pick_rows(): pl.pallas_call(kernel, in_specs=[pl.BlockSpec(memory_space=pltpu.SMEM), p...  3.83 us
  transfers between devices with their start and end apart: 8, of which 3 were waited for; matrix products, arithmetic and copies ran while one was open for 0% of the time, Pallas kernels for 0%

profile of v3, /device:TPU:1, one launch (start us, length us, event | category | flops | bytes accessed | tf_op | source)
XLA Modules:
  0.0 146.6 jit_solution(18430756633312241051)
XLA Ops:
  0.0 0.7 convert_element_type.10
  0.7 2.4 %cut_bands.1 = bf16[64,72,128]{2,1,0:T(8,128)(2,1)} custom-call(bf16[4,32,16,128]{3,2,1,0:T(8,128)(2,1)} %bitcast.13, bf16[4,32,16,128]{3,2,1,0:T(8,128)(2,1)} %bitcast.14), custom_call_target="tpu_custom_call" | custom-call | tf_op jit(solution)/shard_map/cut_bands/pallas_call | solution.py:37
  3.1 0.7 broadcast_dynamic-update-slice_fusion
  3.7 46.2 %all_to_all.15.bands_ref = bf16[64,72,128]{2,1,0:T(8,128)(2,1)S(1)} all-to-all(bf16[64,72,128]{2,1,0:T(8,128)(2,1)} %broadcast_dynamic-update-slice_fusion), channel_id=1, replica_groups=mesh['cache'=64,'tp'=8] {'cache'}, dimensions={0} | all-to-all | bytes 2359296 | tf_op jit(solution)/shard_map/all_to_all | solution.py:221
  50.0 3.8 %pick_rows.1 = bf16[64,8,16,128]{3,2,1,0:T(8,128)(2,1)} custom-call(s32[64,8]{1,0:T(8,128)S(1)} %bitcast.9, bf16[64,72,128]{2,1,0:T(8,128)(2,1)S(1)} %all_to_all.15.bands_ref), custom_call_target="tpu_custom_call" | custom-call | tf_op jit(solution)/shard_map/pick_rows/pallas_call | solution.py:66
  53.8 6.3 %all-to-all-start.1 = ((bf16[64,8,16,128]{3,2,1,0:T(8,128)(2,1)}), bf16[64,8,16,128]{3,2,1,0:T(8,128)(2,1)S(1)}, u32[]{:S(2)}, u32[]{:S(2)}) async-start(bf16[64,8,16,128]{3,2,1,0:T(8,128)(2,1)} %pick_rows.1), calls=%async_computation.1 | async-start | bytes 4194304 | tf_op jit(solution)/shard_map/all_to_all | solution.py:228
  60.2 0.1 cut_heads.1
  60.2 3.2 %collective-permute-start = (bf16[32,1280]{1,0:T(8,128)(2,1)S(1)}, bf16[32,1280]{1,0:T(8,128)(2,1)S(1)}, u32[]{:S(2)}, u32[]{:S(2)}) collective-permute-start(bf16[32,1280]{1,0:T(8,128)(2,1)S(1)} %get-tuple-element.26), channel_id=1, source_target_pairs={{0,1},{1,2},{2,3},{3,4},{4,5},{5,6},{6,7},{7,0},{8,9},{9,10},{10,1... | collective-permute-start | bytes 245768 | tf_op jit(solution)/shard_map/ppermute | solution.py:225
  63.5 4.2 %collective-permute-start.1 = (bf16[32,1280]{1,0:T(8,128)(2,1)S(1)}, bf16[32,1280]{1,0:T(8,128)(2,1)S(1)}, u32[]{:S(2)}, u32[]{:S(2)}) collective-permute-start(bf16[32,1280]{1,0:T(8,128)(2,1)S(1)} %get-tuple-element.27), channel_id=1, source_target_pairs={{0,2},{1,3},{2,4},{3,5},{4,6},{5,7},{6,0},{7,1},{8,10},{9,11},{10,... | collective-permute-start | bytes 245768 | tf_op jit(solution)/shard_map/ppermute | solution.py:225
  67.7 4.6 %collective-permute-start.2 = (bf16[32,1280]{1,0:T(8,128)(2,1)S(1)}, bf16[32,1280]{1,0:T(8,128)(2,1)S(1)}, u32[]{:S(2)}, u32[]{:S(2)}) collective-permute-start(bf16[32,1280]{1,0:T(8,128)(2,1)S(1)} %get-tuple-element.28), channel_id=1, source_target_pairs={{0,3},{1,4},{2,5},{3,6},{4,7},{5,0},{6,1},{7,2},{8,11},{9,12},{10,... | collective-permute-start | bytes 245768 | tf_op jit(solution)/shard_map/ppermute | solution.py:225
  72.3 3.5 %collective-permute-start.3 = (bf16[32,1280]{1,0:T(8,128)(2,1)S(1)}, bf16[32,1280]{1,0:T(8,128)(2,1)S(1)}, u32[]{:S(2)}, u32[]{:S(2)}) collective-permute-start(bf16[32,1280]{1,0:T(8,128)(2,1)S(1)} %get-tuple-element.29), channel_id=1, source_target_pairs={{0,4},{1,5},{2,6},{3,7},{4,0},{5,1},{6,2},{7,3},{8,12},{9,13},{10,... | collective-permute-start | bytes 245768 | tf_op jit(solution)/shard_map/ppermute | solution.py:225
  75.9 4.9 %collective-permute-start.4 = (bf16[32,1280]{1,0:T(8,128)(2,1)S(1)}, bf16[32,1280]{1,0:T(8,128)(2,1)S(1)}, u32[]{:S(2)}, u32[]{:S(2)}) collective-permute-start(bf16[32,1280]{1,0:T(8,128)(2,1)S(1)} %get-tuple-element.30), channel_id=1, source_target_pairs={{0,5},{1,6},{2,7},{3,0},{4,1},{5,2},{6,3},{7,4},{8,13},{9,14},{10,... | collective-permute-start | bytes 245768 | tf_op jit(solution)/shard_map/ppermute | solution.py:225
  80.7 0.0 collective-permute-done.refs_1_
  80.8 5.0 %collective-permute-start.5 = (bf16[32,1280]{1,0:T(8,128)(2,1)S(1)}, bf16[32,1280]{1,0:T(8,128)(2,1)S(1)}, u32[]{:S(2)}, u32[]{:S(2)}) collective-permute-start(bf16[32,1280]{1,0:T(8,128)(2,1)S(1)} %get-tuple-element.31), channel_id=1, source_target_pairs={{0,6},{1,7},{2,0},{3,1},{4,2},{5,3},{6,4},{7,5},{8,14},{9,15},{10,... | collective-permute-start | bytes 245768 | tf_op jit(solution)/shard_map/ppermute | solution.py:225
  85.7 0.0 collective-permute-done.1.refs_2_
  85.7 3.2 %collective-permute-start.6 = (bf16[32,1280]{1,0:T(8,128)(2,1)S(1)}, bf16[32,1280]{1,0:T(8,128)(2,1)S(1)}, u32[]{:S(2)}, u32[]{:S(2)}) collective-permute-start(bf16[32,1280]{1,0:T(8,128)(2,1)S(1)} %get-tuple-element.32), channel_id=1, source_target_pairs={{0,7},{1,0},{2,1},{3,2},{4,3},{5,4},{6,5},{7,6},{8,15},{9,8},{10,9... | collective-permute-start | bytes 245768 | tf_op jit(solution)/shard_map/ppermute | solution.py:225
  88.9 0.0 collective-permute-done.4.refs_5_
  88.9 3.8 %collective-permute-done.5.refs_6_ = bf16[32,1280]{1,0:T(8,128)(2,1)S(1)} collective-permute-done((bf16[32,1280]{1,0:T(8,128)(2,1)S(1)}, bf16[32,1280]{1,0:T(8,128)(2,1)S(1)}, u32[]{:S(2)}, u32[]{:S(2)}) %collective-permute-start.5) | collective-permute-done | bytes 81952 | tf_op jit(solution)/shard_map/ppermute | solution.py:225
  92.8 1.0 collective-permute-done.6.refs_7_
  93.7 17.6 %all-to-all-done.1.refs_8_.refs_9_ = bf16[64,8,16,128]{3,2,1,0:T(8,128)(2,1)S(1)} async-done(((bf16[64,8,16,128]{3,2,1,0:T(8,128)(2,1)}), bf16[64,8,16,128]{3,2,1,0:T(8,128)(2,1)S(1)}, u32[]{:S(2)}, u32[]{:S(2)}) %all-to-all-start.1) | async-done | bytes 2097184 | tf_op jit(solution)/shard_map/all_to_all | solution.py:228
  111.4 10.7 %attend.1 = bf16[8,32,1024]{2,1,0:T(8,128)(2,1)S(1)} custom-call(s32[1]{0:T(128)} %bitcast.me_ref, bf16[32,1280]{1,0:T(8,128)(2,1)S(1)} %get-tuple-element.25.refs_0_, bf16[32,1280]{1,0:T(8,128)(2,1)S(1)} %collective-permute-done.refs_1_, bf16[32,1280]{1,0:T(8,128)(2,1)S(1)} %collective-permute-done.1.refs_2_, ...), custom_call_target="tpu_custom_call" | custom-call | flops 4563402752 | bytes 2097152 | tf_op jit(solution)/shard_map/attend/pallas_call | solution.py:182
  122.1 23.2 %all_to_all.16 = bf16[8,32,1024]{2,1,0:T(8,128)(2,1)S(1)} all-to-all(bf16[8,32,1024]{2,1,0:T(8,128)(2,1)S(1)} %attend.1), channel_id=1, replica_groups=mesh['cache'=64,'tp'=8] {'tp'}, dimensions={0} | all-to-all | bytes 1048576 | tf_op jit(solution)/shard_map/all_to_all | solution.py:230
  145.3 0.3 copy.7
  145.5 1.0 reshape.47
  (10 shorter events, 0.1 us)
Async XLA Ops:
  53.8 6.3 %copy-start = (bf16[1,32,8192]{2,1,0:T(8,128)(2,1)S(1)}, bf16[1,32,8192]{2,1,0:T(8,128)(2,1)}, u32[]{:S(2)}) copy-start(bf16[1,32,8192]{2,1,0:T(8,128)(2,1)} %param.8) | copy-start | bytes 1572868
  53.8 6.3 %copy-start.1 = (bf16[1,32,1024]{2,1,0:T(8,128)(2,1)S(1)}, bf16[1,32,1024]{2,1,0:T(8,128)(2,1)}, u32[]{:S(2)}) copy-start(bf16[1,32,1024]{2,1,0:T(8,128)(2,1)} %param.9) | copy-start | bytes 196612
  53.8 6.4 %copy-start.2 = (bf16[1,32,1024]{2,1,0:T(8,128)(2,1)S(1)}, bf16[1,32,1024]{2,1,0:T(8,128)(2,1)}, u32[]{:S(2)}) copy-start(bf16[1,32,1024]{2,1,0:T(8,128)(2,1)} %param.10) | copy-start | bytes 196612
  53.8 57.6 %all-to-all-start.1 = ((bf16[64,8,16,128]{3,2,1,0:T(8,128)(2,1)}), bf16[64,8,16,128]{3,2,1,0:T(8,128)(2,1)S(1)}, u32[]{:S(2)}, u32[]{:S(2)}) async-start(bf16[64,8,16,128]{3,2,1,0:T(8,128)(2,1)} %pick_rows.1), calls=%async_computation.1 | async-start | bytes 4194304 | tf_op jit(solution)/shard_map/all_to_all | solution.py:228
  60.2 20.5 %collective-permute-start = (bf16[32,1280]{1,0:T(8,128)(2,1)S(1)}, bf16[32,1280]{1,0:T(8,128)(2,1)S(1)}, u32[]{:S(2)}, u32[]{:S(2)}) collective-permute-start(bf16[32,1280]{1,0:T(8,128)(2,1)S(1)} %get-tuple-element.26), channel_id=1, source_target_pairs={{0,1},{1,2},{2,3},{3,4},{4,5},{5,6},{6,7},{7,0},{8,9},{9,10},{10,1... | collective-permute-start | bytes 245768 | tf_op jit(solution)/shard_map/ppermute | solution.py:225
  63.5 22.3 %collective-permute-start.1 = (bf16[32,1280]{1,0:T(8,128)(2,1)S(1)}, bf16[32,1280]{1,0:T(8,128)(2,1)S(1)}, u32[]{:S(2)}, u32[]{:S(2)}) collective-permute-start(bf16[32,1280]{1,0:T(8,128)(2,1)S(1)} %get-tuple-element.27), channel_id=1, source_target_pairs={{0,2},{1,3},{2,4},{3,5},{4,6},{5,7},{6,0},{7,1},{8,10},{9,11},{10,... | collective-permute-start | bytes 245768 | tf_op jit(solution)/shard_map/ppermute | solution.py:225
  67.7 21.2 %collective-permute-start.2 = (bf16[32,1280]{1,0:T(8,128)(2,1)S(1)}, bf16[32,1280]{1,0:T(8,128)(2,1)S(1)}, u32[]{:S(2)}, u32[]{:S(2)}) collective-permute-start(bf16[32,1280]{1,0:T(8,128)(2,1)S(1)} %get-tuple-element.28), channel_id=1, source_target_pairs={{0,3},{1,4},{2,5},{3,6},{4,7},{5,0},{6,1},{7,2},{8,11},{9,12},{10,... | collective-permute-start | bytes 245768 | tf_op jit(solution)/shard_map/ppermute | solution.py:225
  72.3 16.6 %collective-permute-start.3 = (bf16[32,1280]{1,0:T(8,128)(2,1)S(1)}, bf16[32,1280]{1,0:T(8,128)(2,1)S(1)}, u32[]{:S(2)}, u32[]{:S(2)}) collective-permute-start(bf16[32,1280]{1,0:T(8,128)(2,1)S(1)} %get-tuple-element.29), channel_id=1, source_target_pairs={{0,4},{1,5},{2,6},{3,7},{4,0},{5,1},{6,2},{7,3},{8,12},{9,13},{10,... | collective-permute-start | bytes 245768 | tf_op jit(solution)/shard_map/ppermute | solution.py:225
  75.9 13.1 %collective-permute-start.4 = (bf16[32,1280]{1,0:T(8,128)(2,1)S(1)}, bf16[32,1280]{1,0:T(8,128)(2,1)S(1)}, u32[]{:S(2)}, u32[]{:S(2)}) collective-permute-start(bf16[32,1280]{1,0:T(8,128)(2,1)S(1)} %get-tuple-element.30), channel_id=1, source_target_pairs={{0,5},{1,6},{2,7},{3,0},{4,1},{5,2},{6,3},{7,4},{8,13},{9,14},{10,... | collective-permute-start | bytes 245768 | tf_op jit(solution)/shard_map/ppermute | solution.py:225
  80.8 12.0 %collective-permute-start.5 = (bf16[32,1280]{1,0:T(8,128)(2,1)S(1)}, bf16[32,1280]{1,0:T(8,128)(2,1)S(1)}, u32[]{:S(2)}, u32[]{:S(2)}) collective-permute-start(bf16[32,1280]{1,0:T(8,128)(2,1)S(1)} %get-tuple-element.31), channel_id=1, source_target_pairs={{0,6},{1,7},{2,0},{3,1},{4,2},{5,3},{6,4},{7,5},{8,14},{9,15},{10,... | collective-permute-start | bytes 245768 | tf_op jit(solution)/shard_map/ppermute | solution.py:225
  85.7 8.0 %collective-permute-start.6 = (bf16[32,1280]{1,0:T(8,128)(2,1)S(1)}, bf16[32,1280]{1,0:T(8,128)(2,1)S(1)}, u32[]{:S(2)}, u32[]{:S(2)}) collective-permute-start(bf16[32,1280]{1,0:T(8,128)(2,1)S(1)} %get-tuple-element.32), channel_id=1, source_target_pairs={{0,7},{1,0},{2,1},{3,2},{4,3},{5,4},{6,5},{7,6},{8,15},{9,8},{10,9... | collective-permute-start | bytes 245768 | tf_op jit(solution)/shard_map/ppermute | solution.py:225

commit v4 on v3

--- a/solution.py
+++ b/solution.py
@@ -18,33 +18,39 @@
     return pl.BlockSpec(shape, lambda *_: (0,) * len(shape))
 
 
-def cut_bands(cache_keys, cache_values, parts):
+def cut_bands(cache_keys, cache_values, lists, parts):
     owned, plen, width = cache_keys.shape
     half = parts // 2
     rows = owned * ROWS
-
-    def kernel(k_ref, v_ref, out_ref, sems):
-        copies = []
+    top = lists.shape[1]
+
+    def kernel(lists_ref, k_ref, v_ref, out_ref, note_ref):
         for i in range(owned):
-            at = pl.ds(i * ROWS, ROWS)
-            copies.append(pltpu.make_async_copy(k_ref.at[i], out_ref.at[pl.ds(0, half), at], sems.at[0, i]))
-            copies.append(pltpu.make_async_copy(v_ref.at[i], out_ref.at[pl.ds(half, half), at], sems.at[1, i]))
-        for copy in copies:
-            copy.start()
-        for copy in copies:
-            copy.wait()
-
-    return pl.pallas_call(
-        kernel,
-        in_specs=[pl.BlockSpec(memory_space=pl.ANY)] * 2,
-        out_specs=pl.BlockSpec(memory_space=pltpu.VMEM),
-        scratch_shapes=[pltpu.SemaphoreType.DMA((2, owned))],
-        out_shape=jax.ShapeDtypeStruct((parts, rows + EXTRA, width), cache_keys.dtype),
+            at = slice(i * ROWS, (i + 1) * ROWS)
+            out_ref[:half, at] = k_ref[i].reshape(half, ROWS, width)
+            out_ref[half:, at] = v_ref[i].reshape(half, ROWS, width)
+        lane = lax.broadcasted_iota(jnp.int32, (EXTRA, width), 1)
+        note = jnp.zeros((EXTRA, width), jnp.int32)
+        for j in range(top):
+            note = jnp.where(lane == j, lists_ref[0, j], note)
+        note_ref[...] = note.astype(jnp.float32).astype(note_ref.dtype)
+
+    return pl.pallas_call(
+        kernel,
+        grid=(1,),
+        in_specs=[
+            pl.BlockSpec(memory_space=pltpu.SMEM),
+            whole(cache_keys.shape),
+            whole(cache_values.shape),
+        ],
+        out_specs=[whole((parts, rows, width)), whole((EXTRA, width))],
+        out_shape=[
+            jax.ShapeDtypeStruct((parts, rows + EXTRA, width), cache_keys.dtype),
+            jax.ShapeDtypeStruct((EXTRA, width), cache_keys.dtype),
+        ],
+        compiler_params=VMEM,
         name="cut_bands",
-    )(
-        cache_keys.reshape(owned, half, ROWS, width),
-        cache_values.reshape(owned, half, ROWS, width),
-    )
+    )(lists, cache_keys, cache_values)
 
 
 def pick_rows(bands, lists, owned):
@@ -55,13 +61,16 @@
 
     def kernel(lists_ref, bands_ref, out_ref):
         def one(d, carry):
-            for j in range(top):
-                passage = lists_ref[d, j]
+            found = []
+            for j in range(2 * top):
+                passage = lists_ref[2 * d + j // top, j % top]
                 at = pl.multiple_of(lax.bitwise_and(passage, owned - 1) * ROWS, ROWS)
-                out_ref[d, j] = bands_ref[lax.shift_right_logical(passage, shift), pl.ds(at, ROWS)]
+                found.append(bands_ref[lax.shift_right_logical(passage, shift), pl.ds(at, ROWS)])
+            for j in range(2 * top):
+                out_ref[2 * d + j // top, j % top] = found[j]
             return carry
 
-        lax.fori_loop(0, parts, one, 0, unroll=4)
+        lax.fori_loop(0, parts // 2, one, 0, unroll=2)
 
     return pl.pallas_call(
         kernel,
@@ -206,6 +215,30 @@
     )(me, *parts_q, received, received)
 
 
+def join_heads(back):
+    groups, tokens, width = back.shape
+
+    def kernel(in_ref, out_ref, sems):
+        copies = [
+            pltpu.make_async_copy(in_ref.at[g], out_ref.at[0, :, pl.ds(g * width, width)], sems.at[g])
+            for g in range(groups)
+        ]
+        for copy in copies:
+            copy.start()
+        for copy in copies:
+            copy.wait()
+
+    return pl.pallas_call(
+        kernel,
+        in_specs=[pl.BlockSpec(memory_space=pltpu.VMEM)],
+        out_specs=pl.BlockSpec(memory_space=pl.ANY),
+        scratch_shapes=[pltpu.SemaphoreType.DMA((groups,))],
+        out_shape=jax.ShapeDtypeStruct((1, tokens, groups * width), back.dtype),
+        compiler_params=VMEM,
+        name="join_heads",
+    )(back)
+
+
 def solution(mesh):
     parts, tp = mesh.shape["cache"], mesh.shape["tp"]
 
@@ -214,9 +247,8 @@
         owned = cache_keys.shape[0]
         group = query.shape[2] // qkeys.shape[2]
 
-        bands = cut_bands(cache_keys, cache_values, parts)
         top = lists.shape[1]
-        note = jnp.pad(lists.astype(bands.dtype), ((0, EXTRA - 1), (0, bands.shape[2] - top)))
+        bands, note = cut_bands(cache_keys, cache_values, lists, parts)
         bands = bands.at[:, owned * ROWS :].set(note[None])
         bands = lax.all_to_all(bands, "cache", split_axis=0, concat_axis=0, tiled=True)
         seen = bands[:, owned * ROWS, :top].astype(jnp.int32)
@@ -228,8 +260,7 @@
         received = lax.all_to_all(picked, "cache", split_axis=0, concat_axis=0, tiled=True)
         result = attend(parts_q, received, at_tp, group)
         back = lax.all_to_all(result, "tp", split_axis=0, concat_axis=0, tiled=True)
-        tokens = back.shape[1]
-        return back.transpose(1, 0, 2).reshape(1, tokens, tp * group * HD)
+        return join_heads(back)
 
     return jax.shard_map(
         local,

time: 147 us -> 147 us (level)
    unnamed x6 -> x12, local copies, waits for them, and re-layouts: 0.01 us -> 2.75 us
where the time goes in v4:
time: 147 us; the launch traced here: 146 us
  blocking collectives  69.2 us (47%)
  starting transfers between devices  34.9 us (24%)
  waiting for transfers between devices  22.4 us (15%)
  Pallas kernels  16.2 us (11%)
  local copies, waits for them, and re-layouts  2.79 us (2%)
    all_to_all x1, blocking collectives, local(): lax.all_to_all(bands, 'cache', split_axis=0, concat_axis=0, tiled=True)  46 us
    ppermute x7, starting transfers between devices, local(): lax.ppermute(cuts[k], 'tp', [(d, (d + k) % tp) for d in range(tp)])  28.6 us
    all_to_all x1, blocking collectives, local(): back = lax.all_to_all(result, 'tp', split_axis=0, concat_axis=0, tiled=True)  23.2 us
    all_to_all x1, waiting for transfers between devices, local(): lax.all_to_all(picked, 'cache', split_axis=0, concat_axis=0, tiled=True)  17.6 us
    pallas_call x1, Pallas kernels, attend(): pl.pallas_call(kernel, grid_spec=pltpu.PrefetchScalarGridSpec(num_scalar_...  10.7 us
    all_to_all x1, starting transfers between devices, local(): lax.all_to_all(picked, 'cache', split_axis=0, concat_axis=0, tiled=True)  6.32 us
    ppermute x7, waiting for transfers between devices, local(): lax.ppermute(cuts[k], 'tp', [(d, (d + k) % tp) for d in range(tp)])  4.8 us
    pallas_call x1, Pallas kernels, pick_rows(): pl.pallas_call(kernel, in_specs=[pl.BlockSpec(memory_space=pltpu.SMEM), p...  3.82 us
  transfers between devices with their start and end apart: 8, of which 3 were waited for; matrix products, arithmetic and copies ran while one was open for 0% of the time, Pallas kernels for 0%

profile of v4, /device:TPU:1, one launch (start us, length us, event | category | flops | bytes accessed | tf_op | source)
XLA Modules:
  0.0 145.8 jit_solution(14353406509814832575)
XLA Ops:
  0.0 1.0 copy-done.1
  1.0 1.0 copy-done.2
  2.1 0.7 copy-done.5
  2.7 0.7 cut_bands.1
  3.5 46.0 %all_to_all.15.bands_ref = bf16[64,72,128]{2,1,0:T(8,128)(2,1)S(1)} all-to-all(bf16[64,72,128]{2,1,0:T(8,128)(2,1)S(1)} %broadcast_dynamic-update-slice_fusion), channel_id=1, replica_groups=mesh['cache'=64,'tp'=8] {'cache'}, dimensions={0} | all-to-all | bytes 2359296 | tf_op jit(solution)/shard_map/all_to_all | solution.py:253
  49.6 3.8 %pick_rows.1 = bf16[64,8,16,128]{3,2,1,0:T(8,128)(2,1)} custom-call(s32[64,8]{1,0:T(8,128)S(1)} %bitcast.6, bf16[64,72,128]{2,1,0:T(8,128)(2,1)S(1)} %all_to_all.15.bands_ref), custom_call_target="tpu_custom_call" | custom-call | tf_op jit(solution)/shard_map/pick_rows/pallas_call | solution.py:75
  53.4 6.3 %all-to-all-start.1 = ((bf16[64,8,16,128]{3,2,1,0:T(8,128)(2,1)}), bf16[64,8,16,128]{3,2,1,0:T(8,128)(2,1)S(1)}, u32[]{:S(2)}, u32[]{:S(2)}) async-start(bf16[64,8,16,128]{3,2,1,0:T(8,128)(2,1)} %pick_rows.1), calls=%async_computation.1 | async-start | bytes 4194304 | tf_op jit(solution)/shard_map/all_to_all | solution.py:260
  59.8 0.1 cut_heads.1
  59.8 3.2 %collective-permute-start = (bf16[32,1280]{1,0:T(8,128)(2,1)S(1)}, bf16[32,1280]{1,0:T(8,128)(2,1)S(1)}, u32[]{:S(2)}, u32[]{:S(2)}) collective-permute-start(bf16[32,1280]{1,0:T(8,128)(2,1)S(1)} %get-tuple-element.28), channel_id=1, source_target_pairs={{0,1},{1,2},{2,3},{3,4},{4,5},{5,6},{6,7},{7,0},{8,9},{9,10},{10,1... | collective-permute-start | bytes 245768 | tf_op jit(solution)/shard_map/ppermute | solution.py:257
  63.1 4.2 %collective-permute-start.1 = (bf16[32,1280]{1,0:T(8,128)(2,1)S(1)}, bf16[32,1280]{1,0:T(8,128)(2,1)S(1)}, u32[]{:S(2)}, u32[]{:S(2)}) collective-permute-start(bf16[32,1280]{1,0:T(8,128)(2,1)S(1)} %get-tuple-element.29), channel_id=1, source_target_pairs={{0,2},{1,3},{2,4},{3,5},{4,6},{5,7},{6,0},{7,1},{8,10},{9,11},{10,... | collective-permute-start | bytes 245768 | tf_op jit(solution)/shard_map/ppermute | solution.py:257
  67.3 4.6 %collective-permute-start.2 = (bf16[32,1280]{1,0:T(8,128)(2,1)S(1)}, bf16[32,1280]{1,0:T(8,128)(2,1)S(1)}, u32[]{:S(2)}, u32[]{:S(2)}) collective-permute-start(bf16[32,1280]{1,0:T(8,128)(2,1)S(1)} %get-tuple-element.30), channel_id=1, source_target_pairs={{0,3},{1,4},{2,5},{3,6},{4,7},{5,0},{6,1},{7,2},{8,11},{9,12},{10,... | collective-permute-start | bytes 245768 | tf_op jit(solution)/shard_map/ppermute | solution.py:257
  71.9 3.5 %collective-permute-start.3 = (bf16[32,1280]{1,0:T(8,128)(2,1)S(1)}, bf16[32,1280]{1,0:T(8,128)(2,1)S(1)}, u32[]{:S(2)}, u32[]{:S(2)}) collective-permute-start(bf16[32,1280]{1,0:T(8,128)(2,1)S(1)} %get-tuple-element.31), channel_id=1, source_target_pairs={{0,4},{1,5},{2,6},{3,7},{4,0},{5,1},{6,2},{7,3},{8,12},{9,13},{10,... | collective-permute-start | bytes 245768 | tf_op jit(solution)/shard_map/ppermute | solution.py:257
  75.5 4.9 %collective-permute-start.4 = (bf16[32,1280]{1,0:T(8,128)(2,1)S(1)}, bf16[32,1280]{1,0:T(8,128)(2,1)S(1)}, u32[]{:S(2)}, u32[]{:S(2)}) collective-permute-start(bf16[32,1280]{1,0:T(8,128)(2,1)S(1)} %get-tuple-element.32), channel_id=1, source_target_pairs={{0,5},{1,6},{2,7},{3,0},{4,1},{5,2},{6,3},{7,4},{8,13},{9,14},{10,... | collective-permute-start | bytes 245768 | tf_op jit(solution)/shard_map/ppermute | solution.py:257
  80.3 0.0 collective-permute-done.refs_1_
  80.4 5.0 %collective-permute-start.5 = (bf16[32,1280]{1,0:T(8,128)(2,1)S(1)}, bf16[32,1280]{1,0:T(8,128)(2,1)S(1)}, u32[]{:S(2)}, u32[]{:S(2)}) collective-permute-start(bf16[32,1280]{1,0:T(8,128)(2,1)S(1)} %get-tuple-element.33), channel_id=1, source_target_pairs={{0,6},{1,7},{2,0},{3,1},{4,2},{5,3},{6,4},{7,5},{8,14},{9,15},{10,... | collective-permute-start | bytes 245768 | tf_op jit(solution)/shard_map/ppermute | solution.py:257
  85.4 3.2 %collective-permute-start.6 = (bf16[32,1280]{1,0:T(8,128)(2,1)S(1)}, bf16[32,1280]{1,0:T(8,128)(2,1)S(1)}, u32[]{:S(2)}, u32[]{:S(2)}) collective-permute-start(bf16[32,1280]{1,0:T(8,128)(2,1)S(1)} %get-tuple-element.34), channel_id=1, source_target_pairs={{0,7},{1,0},{2,1},{3,2},{4,3},{5,4},{6,5},{7,6},{8,15},{9,8},{10,9... | collective-permute-start | bytes 245768 | tf_op jit(solution)/shard_map/ppermute | solution.py:257
  88.5 0.0 collective-permute-done.2.refs_3_
  88.5 0.0 collective-permute-done.3.refs_4_
  88.5 3.8 %collective-permute-done.5.refs_6_ = bf16[32,1280]{1,0:T(8,128)(2,1)S(1)} collective-permute-done((bf16[32,1280]{1,0:T(8,128)(2,1)S(1)}, bf16[32,1280]{1,0:T(8,128)(2,1)S(1)}, u32[]{:S(2)}, u32[]{:S(2)}) %collective-permute-start.5) | collective-permute-done | bytes 81952 | tf_op jit(solution)/shard_map/ppermute | solution.py:257
  92.4 1.0 collective-permute-done.6.refs_7_
  93.3 17.6 %all-to-all-done.1.refs_8_.refs_9_ = bf16[64,8,16,128]{3,2,1,0:T(8,128)(2,1)S(1)} async-done(((bf16[64,8,16,128]{3,2,1,0:T(8,128)(2,1)}), bf16[64,8,16,128]{3,2,1,0:T(8,128)(2,1)S(1)}, u32[]{:S(2)}, u32[]{:S(2)}) %all-to-all-start.1) | async-done | bytes 2097184 | tf_op jit(solution)/shard_map/all_to_all | solution.py:260
  111.0 10.7 %attend.1 = bf16[8,32,1024]{2,1,0:T(8,128)(2,1)S(1)} custom-call(s32[1]{0:T(128)} %bitcast.me_ref, bf16[32,1280]{1,0:T(8,128)(2,1)S(1)} %get-tuple-element.27.refs_0_, bf16[32,1280]{1,0:T(8,128)(2,1)S(1)} %collective-permute-done.refs_1_, bf16[32,1280]{1,0:T(8,128)(2,1)S(1)} %collective-permute-done.1.refs_2_, ...), custom_call_target="tpu_custom_call" | custom-call | flops 4563402752 | bytes 2097152 | tf_op jit(solution)/shard_map/attend/pallas_call | solution.py:191
  121.6 23.2 %all_to_all.16.in_ref = bf16[8,32,1024]{2,1,0:T(8,128)(2,1)S(1)} all-to-all(bf16[8,32,1024]{2,1,0:T(8,128)(2,1)S(1)} %attend.1), channel_id=1, replica_groups=mesh['cache'=64,'tp'=8] {'tp'}, dimensions={0} | all-to-all | bytes 1048576 | tf_op jit(solution)/shard_map/all_to_all | solution.py:262
  144.8 0.8 join_heads.1
  (13 shorter events, 0.1 us)
Async XLA Ops:
  0.0 1.0 copy-start.1
  1.0 1.0 copy-start.2
  2.1 0.7 copy-start.5
  53.4 6.3 %copy-start = (bf16[1,32,8192]{2,1,0:T(8,128)(2,1)S(1)}, bf16[1,32,8192]{2,1,0:T(8,128)(2,1)}, u32[]{:S(2)}) copy-start(bf16[1,32,8192]{2,1,0:T(8,128)(2,1)} %param.8) | copy-start | bytes 1572868
  53.4 6.3 %copy-start.3 = (bf16[1,32,1024]{2,1,0:T(8,128)(2,1)S(1)}, bf16[1,32,1024]{2,1,0:T(8,128)(2,1)}, u32[]{:S(2)}) copy-start(bf16[1,32,1024]{2,1,0:T(8,128)(2,1)} %param.9) | copy-start | bytes 196612
  53.4 6.4 %copy-start.4 = (bf16[1,32,1024]{2,1,0:T(8,128)(2,1)S(1)}, bf16[1,32,1024]{2,1,0:T(8,128)(2,1)}, u32[]{:S(2)}) copy-start(bf16[1,32,1024]{2,1,0:T(8,128)(2,1)} %param.10) | copy-start | bytes 196612
  53.4 57.6 %all-to-all-start.1 = ((bf16[64,8,16,128]{3,2,1,0:T(8,128)(2,1)}), bf16[64,8,16,128]{3,2,1,0:T(8,128)(2,1)S(1)}, u32[]{:S(2)}, u32[]{:S(2)}) async-start(bf16[64,8,16,128]{3,2,1,0:T(8,128)(2,1)} %pick_rows.1), calls=%async_computation.1 | async-start | bytes 4194304 | tf_op jit(solution)/shard_map/all_to_all | solution.py:260
  59.8 20.5 %collective-permute-start = (bf16[32,1280]{1,0:T(8,128)(2,1)S(1)}, bf16[32,1280]{1,0:T(8,128)(2,1)S(1)}, u32[]{:S(2)}, u32[]{:S(2)}) collective-permute-start(bf16[32,1280]{1,0:T(8,128)(2,1)S(1)} %get-tuple-element.28), channel_id=1, source_target_pairs={{0,1},{1,2},{2,3},{3,4},{4,5},{5,6},{6,7},{7,0},{8,9},{9,10},{10,1... | collective-permute-start | bytes 245768 | tf_op jit(solution)/shard_map/ppermute | solution.py:257
  63.1 22.3 %collective-permute-start.1 = (bf16[32,1280]{1,0:T(8,128)(2,1)S(1)}, bf16[32,1280]{1,0:T(8,128)(2,1)S(1)}, u32[]{:S(2)}, u32[]{:S(2)}) collective-permute-start(bf16[32,1280]{1,0:T(8,128)(2,1)S(1)} %get-tuple-element.29), channel_id=1, source_target_pairs={{0,2},{1,3},{2,4},{3,5},{4,6},{5,7},{6,0},{7,1},{8,10},{9,11},{10,... | collective-permute-start | bytes 245768 | tf_op jit(solution)/shard_map/ppermute | solution.py:257
  67.3 21.2 %collective-permute-start.2 = (bf16[32,1280]{1,0:T(8,128)(2,1)S(1)}, bf16[32,1280]{1,0:T(8,128)(2,1)S(1)}, u32[]{:S(2)}, u32[]{:S(2)}) collective-permute-start(bf16[32,1280]{1,0:T(8,128)(2,1)S(1)} %get-tuple-element.30), channel_id=1, source_target_pairs={{0,3},{1,4},{2,5},{3,6},{4,7},{5,0},{6,1},{7,2},{8,11},{9,12},{10,... | collective-permute-start | bytes 245768 | tf_op jit(solution)/shard_map/ppermute | solution.py:257
  71.9 16.6 %collective-permute-start.3 = (bf16[32,1280]{1,0:T(8,128)(2,1)S(1)}, bf16[32,1280]{1,0:T(8,128)(2,1)S(1)}, u32[]{:S(2)}, u32[]{:S(2)}) collective-permute-start(bf16[32,1280]{1,0:T(8,128)(2,1)S(1)} %get-tuple-element.31), channel_id=1, source_target_pairs={{0,4},{1,5},{2,6},{3,7},{4,0},{5,1},{6,2},{7,3},{8,12},{9,13},{10,... | collective-permute-start | bytes 245768 | tf_op jit(solution)/shard_map/ppermute | solution.py:257
  75.5 13.1 %collective-permute-start.4 = (bf16[32,1280]{1,0:T(8,128)(2,1)S(1)}, bf16[32,1280]{1,0:T(8,128)(2,1)S(1)}, u32[]{:S(2)}, u32[]{:S(2)}) collective-permute-start(bf16[32,1280]{1,0:T(8,128)(2,1)S(1)} %get-tuple-element.32), channel_id=1, source_target_pairs={{0,5},{1,6},{2,7},{3,0},{4,1},{5,2},{6,3},{7,4},{8,13},{9,14},{10,... | collective-permute-start | bytes 245768 | tf_op jit(solution)/shard_map/ppermute | solution.py:257
  80.4 12.0 %collective-permute-start.5 = (bf16[32,1280]{1,0:T(8,128)(2,1)S(1)}, bf16[32,1280]{1,0:T(8,128)(2,1)S(1)}, u32[]{:S(2)}, u32[]{:S(2)}) collective-permute-start(bf16[32,1280]{1,0:T(8,128)(2,1)S(1)} %get-tuple-element.33), channel_id=1, source_target_pairs={{0,6},{1,7},{2,0},{3,1},{4,2},{5,3},{6,4},{7,5},{8,14},{9,15},{10,... | collective-permute-start | bytes 245768 | tf_op jit(solution)/shard_map/ppermute | solution.py:257
  85.4 8.0 %collective-permute-start.6 = (bf16[32,1280]{1,0:T(8,128)(2,1)S(1)}, bf16[32,1280]{1,0:T(8,128)(2,1)S(1)}, u32[]{:S(2)}, u32[]{:S(2)}) collective-permute-start(bf16[32,1280]{1,0:T(8,128)(2,1)S(1)} %get-tuple-element.34), channel_id=1, source_target_pairs={{0,7},{1,0},{2,1},{3,2},{4,3},{5,4},{6,5},{7,6},{8,15},{9,8},{10,9... | collective-permute-start | bytes 245768 | tf_op jit(solution)/shard_map/ppermute | solution.py:257

commit v5 on v4

--- a/solution.py
+++ b/solution.py
@@ -11,6 +11,7 @@
 EXTRA = 8
 ROWS = 16
 LOG2E = 1.4426950408889634
+LIMIT = 62 * 1024 * 1024 + 512 * 1024
 VMEM = pltpu.CompilerParams(vmem_limit_bytes=48 * 1024 * 1024)
 
 
@@ -23,32 +24,45 @@
     half = parts // 2
     rows = owned * ROWS
     top = lists.shape[1]
-
-    def kernel(lists_ref, k_ref, v_ref, out_ref, note_ref):
+    pieces = 2
+    part = plen // pieces
+
+    def kernel(lists_ref, k_ref, v_ref, out_ref, list_buf, bufs, list_sem, sems):
+        list_copy = pltpu.make_async_copy(lists_ref, list_buf, list_sem)
+        list_copy.start()
+        copies = {}
+        for i in range(owned):
+            for side, ref in enumerate((k_ref, v_ref)):
+                for n in range(pieces):
+                    at = pl.ds(n * part, part)
+                    copy = pltpu.make_async_copy(ref.at[i, at], bufs.at[side, i, at], sems.at[side, i, n])
+                    copy.start()
+                    copies[side, i, n] = copy
+        list_copy.wait()
+        spread = lax.broadcasted_iota(jnp.int32, (top, width), 0) == lax.broadcasted_iota(jnp.int32, (top, width), 1)
+        note = jnp.dot(
+            list_buf[...].astype(jnp.bfloat16), spread.astype(jnp.bfloat16), preferred_element_type=jnp.float32
+        )
+        out_ref[:, rows:] = jnp.broadcast_to(note.astype(out_ref.dtype)[None], (parts, EXTRA, width))
         for i in range(owned):
             at = slice(i * ROWS, (i + 1) * ROWS)
-            out_ref[:half, at] = k_ref[i].reshape(half, ROWS, width)
-            out_ref[half:, at] = v_ref[i].reshape(half, ROWS, width)
-        lane = lax.broadcasted_iota(jnp.int32, (EXTRA, width), 1)
-        note = jnp.zeros((EXTRA, width), jnp.int32)
-        for j in range(top):
-            note = jnp.where(lane == j, lists_ref[0, j], note)
-        note_ref[...] = note.astype(jnp.float32).astype(note_ref.dtype)
-
-    return pl.pallas_call(
-        kernel,
-        grid=(1,),
-        in_specs=[
-            pl.BlockSpec(memory_space=pltpu.SMEM),
-            whole(cache_keys.shape),
-            whole(cache_values.shape),
+            for side in range(2):
+                for n in range(pieces):
+                    copies[side, i, n].wait()
+                out_ref[side * half : (side + 1) * half, at] = bufs[side, i].reshape(half, ROWS, width)
+
+    return pl.pallas_call(
+        kernel,
+        in_specs=[pl.BlockSpec(memory_space=pl.ANY)] * 3,
+        out_specs=pl.BlockSpec(memory_space=pltpu.VMEM),
+        scratch_shapes=[
+            pltpu.VMEM(lists.shape, lists.dtype),
+            pltpu.VMEM((2, owned, plen, width), cache_keys.dtype),
+            pltpu.SemaphoreType.DMA,
+            pltpu.SemaphoreType.DMA((2, owned, pieces)),
         ],
-        out_specs=[whole((parts, rows, width)), whole((EXTRA, width))],
-        out_shape=[
-            jax.ShapeDtypeStruct((parts, rows + EXTRA, width), cache_keys.dtype),
-            jax.ShapeDtypeStruct((EXTRA, width), cache_keys.dtype),
-        ],
-        compiler_params=VMEM,
+        out_shape=jax.ShapeDtypeStruct((parts, rows + EXTRA, width), cache_keys.dtype),
+        compiler_params=pltpu.CompilerParams(vmem_limit_bytes=LIMIT),
         name="cut_bands",
     )(lists, cache_keys, cache_values)
 
@@ -59,23 +73,37 @@
     assert owned & (owned - 1) == 0
     shift = owned.bit_length() - 1
 
-    def kernel(lists_ref, bands_ref, out_ref):
+    steps = 16
+    share = parts // steps
+
+    def kernel(lists_ref, bands_ref, out_ref, buf, sems):
         def one(d, carry):
             found = []
-            for j in range(2 * top):
-                passage = lists_ref[2 * d + j // top, j % top]
+            for j in range(top):
+                passage = lists_ref[d, j]
                 at = pl.multiple_of(lax.bitwise_and(passage, owned - 1) * ROWS, ROWS)
                 found.append(bands_ref[lax.shift_right_logical(passage, shift), pl.ds(at, ROWS)])
-            for j in range(2 * top):
-                out_ref[2 * d + j // top, j % top] = found[j]
+            for j in range(top):
+                buf[d, j] = found[j]
             return carry
 
-        lax.fori_loop(0, parts // 2, one, 0, unroll=2)
+        copies = []
+        for step in range(steps):
+            lax.fori_loop(step * share, (step + 1) * share, one, 0, unroll=4)
+            at = pl.ds(step * share, share)
+            copies.append(pltpu.make_async_copy(buf.at[at], out_ref.at[at], sems.at[step]))
+            copies[-1].start()
+        for copy in copies:
+            copy.wait()
 
     return pl.pallas_call(
         kernel,
         in_specs=[pl.BlockSpec(memory_space=pltpu.SMEM), pl.BlockSpec(memory_space=pltpu.VMEM)],
-        out_specs=pl.BlockSpec(memory_space=pltpu.VMEM),
+        out_specs=pl.BlockSpec(memory_space=pl.ANY),
+        scratch_shapes=[
+            pltpu.VMEM((parts, top, ROWS, width), bands.dtype),
+            pltpu.SemaphoreType.DMA((steps,)),
+        ],
         out_shape=jax.ShapeDtypeStruct((parts, top, ROWS, width), bands.dtype),
         compiler_params=VMEM,
         name="pick_rows",
@@ -248,8 +276,7 @@
         group = query.shape[2] // qkeys.shape[2]
 
         top = lists.shape[1]
-        bands, note = cut_bands(cache_keys, cache_values, lists, parts)
-        bands = bands.at[:, owned * ROWS :].set(note[None])
+        bands = cut_bands(cache_keys, cache_values, lists, parts)
         bands = lax.all_to_all(bands, "cache", split_axis=0, concat_axis=0, tiled=True)
         seen = bands[:, owned * ROWS, :top].astype(jnp.int32)
         cuts = cut_heads(query[0], qkeys[0], qvalues[0], at_tp, tp)

time: 147 us -> 145 us (0.986)
  local copies, waits for them, and re-layouts: 2.79 us -> 0.02 us
    unnamed x12 -> x6, local copies, waits for them, and re-layouts: 2.75 us -> 0.02 us
    pallas_call x1, Pallas kernels: 0.75 us -> 2.45 us  [cut_bands(): pl.pallas_call(kernel, in_specs=[pl.BlockSpec(memory_space=pl.ANY)] * 3,...]
where the time goes in v5:
time: 145 us; the launch traced here: 144 us
  blocking collectives  69.4 us (48%)
  starting transfers between devices  34.9 us (24%)
  waiting for transfers between devices  22.4 us (15%)
  Pallas kernels  17.1 us (12%)
    all_to_all x1, blocking collectives, local(): lax.all_to_all(bands, 'cache', split_axis=0, concat_axis=0, tiled=True)  46.2 us
    ppermute x7, starting transfers between devices, local(): lax.ppermute(cuts[k], 'tp', [(d, (d + k) % tp) for d in range(tp)])  28.6 us
    all_to_all x1, blocking collectives, local(): back = lax.all_to_all(result, 'tp', split_axis=0, concat_axis=0, tiled=True)  23.2 us
    all_to_all x1, waiting for transfers between devices, local(): lax.all_to_all(picked, 'cache', split_axis=0, concat_axis=0, tiled=True)  17.6 us
    pallas_call x1, Pallas kernels, attend(): pl.pallas_call(kernel, grid_spec=pltpu.PrefetchScalarGridSpec(num_scalar_...  10.7 us
    all_to_all x1, starting transfers between devices, local(): lax.all_to_all(picked, 'cache', split_axis=0, concat_axis=0, tiled=True)  6.33 us
    ppermute x7, waiting for transfers between devices, local(): lax.ppermute(cuts[k], 'tp', [(d, (d + k) % tp) for d in range(tp)])  4.8 us
    pallas_call x1, Pallas kernels, pick_rows(): pl.pallas_call(kernel, in_specs=[pl.BlockSpec(memory_space=pltpu.SMEM), p...  3.11 us
  transfers between devices with their start and end apart: 8, of which 3 were waited for; matrix products, arithmetic and copies ran while one was open for 0% of the time, Pallas kernels for 0%

profile of v5, /device:TPU:1, one launch (start us, length us, event | category | flops | bytes accessed | tf_op | source)
XLA Modules:
  0.0 144.3 jit_solution(16565549015050579655)
XLA Ops:
  0.0 2.5 %cut_bands.1 = bf16[64,72,128]{2,1,0:T(8,128)(2,1)} custom-call(s32[1,8]{1,0:T(1,128)} %lists_ref.1, bf16[4,512,128]{2,1,0:T(8,128)(2,1)} %k_ref.1, bf16[4,512,128]{2,1,0:T(8,128)(2,1)} %v_ref.1), custom_call_target="tpu_custom_call" | custom-call | tf_op jit(solution)/shard_map/cut_bands/pallas_call | solution.py:54
  2.5 46.2 %all_to_all.15.bands_ref = bf16[64,72,128]{2,1,0:T(8,128)(2,1)S(1)} all-to-all(bf16[64,72,128]{2,1,0:T(8,128)(2,1)} %cut_bands.1), channel_id=1, replica_groups=mesh['cache'=64,'tp'=8] {'cache'}, dimensions={0} | all-to-all | bytes 2359296 | tf_op jit(solution)/shard_map/all_to_all | solution.py:280
  48.7 3.1 %pick_rows.1 = bf16[64,8,16,128]{3,2,1,0:T(8,128)(2,1)} custom-call(s32[64,8]{1,0:T(8,128)S(1)} %bitcast.6, bf16[64,72,128]{2,1,0:T(8,128)(2,1)S(1)} %all_to_all.15.bands_ref), custom_call_target="tpu_custom_call" | custom-call | tf_op jit(solution)/shard_map/pick_rows/pallas_call | solution.py:99
  51.8 0.0 copy-start
  51.8 0.0 copy-start.1
  51.8 0.0 copy-start.2
  51.9 6.3 %all-to-all-start.1 = ((bf16[64,8,16,128]{3,2,1,0:T(8,128)(2,1)}), bf16[64,8,16,128]{3,2,1,0:T(8,128)(2,1)S(1)}, u32[]{:S(2)}, u32[]{:S(2)}) async-start(bf16[64,8,16,128]{3,2,1,0:T(8,128)(2,1)} %pick_rows.1), calls=%async_computation.1 | async-start | bytes 4194304 | tf_op jit(solution)/shard_map/all_to_all | solution.py:287
  58.2 0.1 cut_heads.1
  58.3 3.2 %collective-permute-start = (bf16[32,1280]{1,0:T(8,128)(2,1)S(1)}, bf16[32,1280]{1,0:T(8,128)(2,1)S(1)}, u32[]{:S(2)}, u32[]{:S(2)}) collective-permute-start(bf16[32,1280]{1,0:T(8,128)(2,1)S(1)} %get-tuple-element.14), channel_id=1, source_target_pairs={{0,1},{1,2},{2,3},{3,4},{4,5},{5,6},{6,7},{7,0},{8,9},{9,10},{10,1... | collective-permute-start | bytes 245768 | tf_op jit(solution)/shard_map/ppermute | solution.py:284
  61.5 4.2 %collective-permute-start.1 = (bf16[32,1280]{1,0:T(8,128)(2,1)S(1)}, bf16[32,1280]{1,0:T(8,128)(2,1)S(1)}, u32[]{:S(2)}, u32[]{:S(2)}) collective-permute-start(bf16[32,1280]{1,0:T(8,128)(2,1)S(1)} %get-tuple-element.15), channel_id=1, source_target_pairs={{0,2},{1,3},{2,4},{3,5},{4,6},{5,7},{6,0},{7,1},{8,10},{9,11},{10,... | collective-permute-start | bytes 245768 | tf_op jit(solution)/shard_map/ppermute | solution.py:284
  65.7 4.6 %collective-permute-start.2 = (bf16[32,1280]{1,0:T(8,128)(2,1)S(1)}, bf16[32,1280]{1,0:T(8,128)(2,1)S(1)}, u32[]{:S(2)}, u32[]{:S(2)}) collective-permute-start(bf16[32,1280]{1,0:T(8,128)(2,1)S(1)} %get-tuple-element.16), channel_id=1, source_target_pairs={{0,3},{1,4},{2,5},{3,6},{4,7},{5,0},{6,1},{7,2},{8,11},{9,12},{10,... | collective-permute-start | bytes 245768 | tf_op jit(solution)/shard_map/ppermute | solution.py:284
  70.4 3.5 %collective-permute-start.3 = (bf16[32,1280]{1,0:T(8,128)(2,1)S(1)}, bf16[32,1280]{1,0:T(8,128)(2,1)S(1)}, u32[]{:S(2)}, u32[]{:S(2)}) collective-permute-start(bf16[32,1280]{1,0:T(8,128)(2,1)S(1)} %get-tuple-element.17), channel_id=1, source_target_pairs={{0,4},{1,5},{2,6},{3,7},{4,0},{5,1},{6,2},{7,3},{8,12},{9,13},{10,... | collective-permute-start | bytes 245768 | tf_op jit(solution)/shard_map/ppermute | solution.py:284
  73.9 4.9 %collective-permute-start.4 = (bf16[32,1280]{1,0:T(8,128)(2,1)S(1)}, bf16[32,1280]{1,0:T(8,128)(2,1)S(1)}, u32[]{:S(2)}, u32[]{:S(2)}) collective-permute-start(bf16[32,1280]{1,0:T(8,128)(2,1)S(1)} %get-tuple-element.18), channel_id=1, source_target_pairs={{0,5},{1,6},{2,7},{3,0},{4,1},{5,2},{6,3},{7,4},{8,13},{9,14},{10,... | collective-permute-start | bytes 245768 | tf_op jit(solution)/shard_map/ppermute | solution.py:284
  78.8 0.0 collective-permute-done.refs_1_
  78.8 5.0 %collective-permute-start.5 = (bf16[32,1280]{1,0:T(8,128)(2,1)S(1)}, bf16[32,1280]{1,0:T(8,128)(2,1)S(1)}, u32[]{:S(2)}, u32[]{:S(2)}) collective-permute-start(bf16[32,1280]{1,0:T(8,128)(2,1)S(1)} %get-tuple-element.19), channel_id=1, source_target_pairs={{0,6},{1,7},{2,0},{3,1},{4,2},{5,3},{6,4},{7,5},{8,14},{9,15},{10,... | collective-permute-start | bytes 245768 | tf_op jit(solution)/shard_map/ppermute | solution.py:284
  83.8 3.2 %collective-permute-start.6 = (bf16[32,1280]{1,0:T(8,128)(2,1)S(1)}, bf16[32,1280]{1,0:T(8,128)(2,1)S(1)}, u32[]{:S(2)}, u32[]{:S(2)}) collective-permute-start(bf16[32,1280]{1,0:T(8,128)(2,1)S(1)} %get-tuple-element.20), channel_id=1, source_target_pairs={{0,7},{1,0},{2,1},{3,2},{4,3},{5,4},{6,5},{7,6},{8,15},{9,8},{10,9... | collective-permute-start | bytes 245768 | tf_op jit(solution)/shard_map/ppermute | solution.py:284
  87.0 0.0 collective-permute-done.2.refs_3_
  87.0 0.0 collective-permute-done.3.refs_4_
  87.0 3.8 %collective-permute-done.5.refs_6_ = bf16[32,1280]{1,0:T(8,128)(2,1)S(1)} collective-permute-done((bf16[32,1280]{1,0:T(8,128)(2,1)S(1)}, bf16[32,1280]{1,0:T(8,128)(2,1)S(1)}, u32[]{:S(2)}, u32[]{:S(2)}) %collective-permute-start.5) | collective-permute-done | bytes 81952 | tf_op jit(solution)/shard_map/ppermute | solution.py:284
  90.8 1.0 collective-permute-done.6.refs_7_
  91.8 17.6 %all-to-all-done.1.refs_8_.refs_9_ = bf16[64,8,16,128]{3,2,1,0:T(8,128)(2,1)S(1)} async-done(((bf16[64,8,16,128]{3,2,1,0:T(8,128)(2,1)}), bf16[64,8,16,128]{3,2,1,0:T(8,128)(2,1)S(1)}, u32[]{:S(2)}, u32[]{:S(2)}) %all-to-all-start.1) | async-done | bytes 2097184 | tf_op jit(solution)/shard_map/all_to_all | solution.py:287
  109.4 10.7 %attend.1 = bf16[8,32,1024]{2,1,0:T(8,128)(2,1)S(1)} custom-call(s32[1]{0:T(128)} %bitcast.me_ref, bf16[32,1280]{1,0:T(8,128)(2,1)S(1)} %get-tuple-element.13.refs_0_, bf16[32,1280]{1,0:T(8,128)(2,1)S(1)} %collective-permute-done.refs_1_, bf16[32,1280]{1,0:T(8,128)(2,1)S(1)} %collective-permute-done.1.refs_2_, ...), custom_call_target="tpu_custom_call" | custom-call | flops 4563402752 | bytes 2097152 | tf_op jit(solution)/shard_map/attend/pallas_call | solution.py:219
  120.1 23.2 %all_to_all.16.in_ref = bf16[8,32,1024]{2,1,0:T(8,128)(2,1)S(1)} all-to-all(bf16[8,32,1024]{2,1,0:T(8,128)(2,1)S(1)} %attend.1), channel_id=1, replica_groups=mesh['cache'=64,'tp'=8] {'tp'}, dimensions={0} | all-to-all | bytes 1048576 | tf_op jit(solution)/shard_map/all_to_all | solution.py:289
  143.3 0.8 join_heads.1
  (6 shorter events, 0.0 us)
Async XLA Ops:
  51.8 6.4 %copy-start = (bf16[1,32,8192]{2,1,0:T(8,128)(2,1)S(1)}, bf16[1,32,8192]{2,1,0:T(8,128)(2,1)}, u32[]{:S(2)}) copy-start(bf16[1,32,8192]{2,1,0:T(8,128)(2,1)} %param.6) | copy-start | bytes 1572868
  51.8 6.4 %copy-start.1 = (bf16[1,32,1024]{2,1,0:T(8,128)(2,1)S(1)}, bf16[1,32,1024]{2,1,0:T(8,128)(2,1)}, u32[]{:S(2)}) copy-start(bf16[1,32,1024]{2,1,0:T(8,128)(2,1)} %param.7) | copy-start | bytes 196612
  51.8 6.4 %copy-start.2 = (bf16[1,32,1024]{2,1,0:T(8,128)(2,1)S(1)}, bf16[1,32,1024]{2,1,0:T(8,128)(2,1)}, u32[]{:S(2)}) copy-start(bf16[1,32,1024]{2,1,0:T(8,128)(2,1)} %param.8) | copy-start | bytes 196612
  51.9 57.6 %all-to-all-start.1 = ((bf16[64,8,16,128]{3,2,1,0:T(8,128)(2,1)}), bf16[64,8,16,128]{3,2,1,0:T(8,128)(2,1)S(1)}, u32[]{:S(2)}, u32[]{:S(2)}) async-start(bf16[64,8,16,128]{3,2,1,0:T(8,128)(2,1)} %pick_rows.1), calls=%async_computation.1 | async-start | bytes 4194304 | tf_op jit(solution)/shard_map/all_to_all | solution.py:287
  58.3 20.5 %collective-permute-start = (bf16[32,1280]{1,0:T(8,128)(2,1)S(1)}, bf16[32,1280]{1,0:T(8,128)(2,1)S(1)}, u32[]{:S(2)}, u32[]{:S(2)}) collective-permute-start(bf16[32,1280]{1,0:T(8,128)(2,1)S(1)} %get-tuple-element.14), channel_id=1, source_target_pairs={{0,1},{1,2},{2,3},{3,4},{4,5},{5,6},{6,7},{7,0},{8,9},{9,10},{10,1... | collective-permute-start | bytes 245768 | tf_op jit(solution)/shard_map/ppermute | solution.py:284
  61.5 22.3 %collective-permute-start.1 = (bf16[32,1280]{1,0:T(8,128)(2,1)S(1)}, bf16[32,1280]{1,0:T(8,128)(2,1)S(1)}, u32[]{:S(2)}, u32[]{:S(2)}) collective-permute-start(bf16[32,1280]{1,0:T(8,128)(2,1)S(1)} %get-tuple-element.15), channel_id=1, source_target_pairs={{0,2},{1,3},{2,4},{3,5},{4,6},{5,7},{6,0},{7,1},{8,10},{9,11},{10,... | collective-permute-start | bytes 245768 | tf_op jit(solution)/shard_map/ppermute | solution.py:284
  65.7 21.2 %collective-permute-start.2 = (bf16[32,1280]{1,0:T(8,128)(2,1)S(1)}, bf16[32,1280]{1,0:T(8,128)(2,1)S(1)}, u32[]{:S(2)}, u32[]{:S(2)}) collective-permute-start(bf16[32,1280]{1,0:T(8,128)(2,1)S(1)} %get-tuple-element.16), channel_id=1, source_target_pairs={{0,3},{1,4},{2,5},{3,6},{4,7},{5,0},{6,1},{7,2},{8,11},{9,12},{10,... | collective-permute-start | bytes 245768 | tf_op jit(solution)/shard_map/ppermute | solution.py:284
  70.4 16.6 %collective-permute-start.3 = (bf16[32,1280]{1,0:T(8,128)(2,1)S(1)}, bf16[32,1280]{1,0:T(8,128)(2,1)S(1)}, u32[]{:S(2)}, u32[]{:S(2)}) collective-permute-start(bf16[32,1280]{1,0:T(8,128)(2,1)S(1)} %get-tuple-element.17), channel_id=1, source_target_pairs={{0,4},{1,5},{2,6},{3,7},{4,0},{5,1},{6,2},{7,3},{8,12},{9,13},{10,... | collective-permute-start | bytes 245768 | tf_op jit(solution)/shard_map/ppermute | solution.py:284
  73.9 13.1 %collective-permute-start.4 = (bf16[32,1280]{1,0:T(8,128)(2,1)S(1)}, bf16[32,1280]{1,0:T(8,128)(2,1)S(1)}, u32[]{:S(2)}, u32[]{:S(2)}) collective-permute-start(bf16[32,1280]{1,0:T(8,128)(2,1)S(1)} %get-tuple-element.18), channel_id=1, source_target_pairs={{0,5},{1,6},{2,7},{3,0},{4,1},{5,2},{6,3},{7,4},{8,13},{9,14},{10,... | collective-permute-start | bytes 245768 | tf_op jit(solution)/shard_map/ppermute | solution.py:284
  78.8 12.0 %collective-permute-start.5 = (bf16[32,1280]{1,0:T(8,128)(2,1)S(1)}, bf16[32,1280]{1,0:T(8,128)(2,1)S(1)}, u32[]{:S(2)}, u32[]{:S(2)}) collective-permute-start(bf16[32,1280]{1,0:T(8,128)(2,1)S(1)} %get-tuple-element.19), channel_id=1, source_target_pairs={{0,6},{1,7},{2,0},{3,1},{4,2},{5,3},{6,4},{7,5},{8,14},{9,15},{10,... | collective-permute-start | bytes 245768 | tf_op jit(solution)/shard_map/ppermute | solution.py:284
  83.8 8.0 %collective-permute-start.6 = (bf16[32,1280]{1,0:T(8,128)(2,1)S(1)}, bf16[32,1280]{1,0:T(8,128)(2,1)S(1)}, u32[]{:S(2)}, u32[]{:S(2)}) collective-permute-start(bf16[32,1280]{1,0:T(8,128)(2,1)S(1)} %get-tuple-element.20), channel_id=1, source_target_pairs={{0,7},{1,0},{2,1},{3,2},{4,3},{5,4},{6,5},{7,6},{8,15},{9,8},{10,9... | collective-permute-start | bytes 245768 | tf_op jit(solution)/shard_map/ppermute | solution.py:284

commit v6 on v5

--- a/solution.py
+++ b/solution.py
@@ -11,7 +11,6 @@
 EXTRA = 8
 ROWS = 16
 LOG2E = 1.4426950408889634
-LIMIT = 62 * 1024 * 1024 + 512 * 1024
 VMEM = pltpu.CompilerParams(vmem_limit_bytes=48 * 1024 * 1024)
 
 
@@ -24,7 +23,7 @@
     half = parts // 2
     rows = owned * ROWS
     top = lists.shape[1]
-    pieces = 2
+    pieces = 4
     part = plen // pieces
 
     def kernel(lists_ref, k_ref, v_ref, out_ref, list_buf, bufs, list_sem, sems):
@@ -53,7 +52,7 @@
 
     return pl.pallas_call(
         kernel,
-        in_specs=[pl.BlockSpec(memory_space=pl.ANY)] * 3,
+        in_specs=[pl.BlockSpec(memory_space=pltpu.HBM)] * 3,
         out_specs=pl.BlockSpec(memory_space=pltpu.VMEM),
         scratch_shapes=[
             pltpu.VMEM(lists.shape, lists.dtype),
@@ -62,9 +61,13 @@
             pltpu.SemaphoreType.DMA((2, owned, pieces)),
         ],
         out_shape=jax.ShapeDtypeStruct((parts, rows + EXTRA, width), cache_keys.dtype),
-        compiler_params=pltpu.CompilerParams(vmem_limit_bytes=LIMIT),
+        compiler_params=pltpu.CompilerParams(vmem_limit_bytes=40 * 1024 * 1024),
         name="cut_bands",
-    )(lists, cache_keys, cache_values)
+    )(
+        pltpu.with_memory_space_constraint(lists, pltpu.HBM),
+        pltpu.with_memory_space_constraint(cache_keys, pltpu.HBM),
+        pltpu.with_memory_space_constraint(cache_values, pltpu.HBM),
+    )
 
 
 def pick_rows(bands, lists, owned):

time: 145 us -> 144 us (level)
  no operation moved by 1% of the time
where the time goes in v6:
time: 144 us; the launch traced here: 143 us
  blocking collectives  69.2 us (48%)
  starting transfers between devices  34.9 us (24%)
  waiting for transfers between devices  22.4 us (16%)
  Pallas kernels  16.3 us (11%)
    all_to_all x1, blocking collectives, local(): lax.all_to_all(bands, 'cache', split_axis=0, concat_axis=0, tiled=True)  46 us
    ppermute x7, starting transfers between devices, local(): lax.ppermute(cuts[k], 'tp', [(d, (d + k) % tp) for d in range(tp)])  28.6 us
    all_to_all x1, blocking collectives, local(): back = lax.all_to_all(result, 'tp', split_axis=0, concat_axis=0, tiled=True)  23.2 us
    all_to_all x1, waiting for transfers between devices, local(): lax.all_to_all(picked, 'cache', split_axis=0, concat_axis=0, tiled=True)  17.6 us
    pallas_call x1, Pallas kernels, attend(): pl.pallas_call(kernel, grid_spec=pltpu.PrefetchScalarGridSpec(num_scalar_...  10.7 us
    all_to_all x1, starting transfers between devices, local(): lax.all_to_all(picked, 'cache', split_axis=0, concat_axis=0, tiled=True)  6.33 us
    ppermute x7, waiting for transfers between devices, local(): lax.ppermute(cuts[k], 'tp', [(d, (d + k) % tp) for d in range(tp)])  4.8 us
    pallas_call x1, Pallas kernels, pick_rows(): pl.pallas_call(kernel, in_specs=[pl.BlockSpec(memory_space=pltpu.SMEM), p...  3.11 us
  transfers between devices with their start and end apart: 8, of which 3 were waited for; matrix products, arithmetic and copies ran while one was open for 0% of the time, Pallas kernels for 0%

profile of v6, /device:TPU:1, one launch (start us, length us, event | category | flops | bytes accessed | tf_op | source)
XLA Modules:
  0.0 143.2 jit_solution(2805241858285365762)
XLA Ops:
  0.0 1.6 %cut_bands.1 = bf16[64,72,128]{2,1,0:T(8,128)(2,1)S(1)} custom-call(s32[1,8]{1,0:T(1,128)} %lists_ref.1, bf16[4,512,128]{2,1,0:T(8,128)(2,1)} %k_ref.1, bf16[4,512,128]{2,1,0:T(8,128)(2,1)} %v_ref.1), custom_call_target="tpu_custom_call" | custom-call | tf_op jit(solution)/shard_map/cut_bands/pallas_call | solution.py:53
  1.6 46.0 %all_to_all.15.bands_ref = bf16[64,72,128]{2,1,0:T(8,128)(2,1)S(1)} all-to-all(bf16[64,72,128]{2,1,0:T(8,128)(2,1)S(1)} %cut_bands.1), channel_id=1, replica_groups=mesh['cache'=64,'tp'=8] {'cache'}, dimensions={0} | all-to-all | bytes 2359296 | tf_op jit(solution)/shard_map/all_to_all | solution.py:283
  47.6 3.1 %pick_rows.1 = bf16[64,8,16,128]{3,2,1,0:T(8,128)(2,1)} custom-call(s32[64,8]{1,0:T(8,128)S(1)} %bitcast.6, bf16[64,72,128]{2,1,0:T(8,128)(2,1)S(1)} %all_to_all.15.bands_ref), custom_call_target="tpu_custom_call" | custom-call | tf_op jit(solution)/shard_map/pick_rows/pallas_call | solution.py:102
  50.8 0.0 copy-start
  50.8 0.0 copy-start.1
  50.8 0.0 copy-start.2
  50.8 6.3 %all-to-all-start.1 = ((bf16[64,8,16,128]{3,2,1,0:T(8,128)(2,1)}), bf16[64,8,16,128]{3,2,1,0:T(8,128)(2,1)S(1)}, u32[]{:S(2)}, u32[]{:S(2)}) async-start(bf16[64,8,16,128]{3,2,1,0:T(8,128)(2,1)} %pick_rows.1), calls=%async_computation.1 | async-start | bytes 4194304 | tf_op jit(solution)/shard_map/all_to_all | solution.py:290
  57.2 0.1 cut_heads.1
  57.2 3.2 %collective-permute-start = (bf16[32,1280]{1,0:T(8,128)(2,1)S(1)}, bf16[32,1280]{1,0:T(8,128)(2,1)S(1)}, u32[]{:S(2)}, u32[]{:S(2)}) collective-permute-start(bf16[32,1280]{1,0:T(8,128)(2,1)S(1)} %get-tuple-element.14), channel_id=1, source_target_pairs={{0,1},{1,2},{2,3},{3,4},{4,5},{5,6},{6,7},{7,0},{8,9},{9,10},{10,1... | collective-permute-start | bytes 245768 | tf_op jit(solution)/shard_map/ppermute | solution.py:287
  60.5 4.2 %collective-permute-start.1 = (bf16[32,1280]{1,0:T(8,128)(2,1)S(1)}, bf16[32,1280]{1,0:T(8,128)(2,1)S(1)}, u32[]{:S(2)}, u32[]{:S(2)}) collective-permute-start(bf16[32,1280]{1,0:T(8,128)(2,1)S(1)} %get-tuple-element.15), channel_id=1, source_target_pairs={{0,2},{1,3},{2,4},{3,5},{4,6},{5,7},{6,0},{7,1},{8,10},{9,11},{10,... | collective-permute-start | bytes 245768 | tf_op jit(solution)/shard_map/ppermute | solution.py:287
  64.7 4.6 %collective-permute-start.2 = (bf16[32,1280]{1,0:T(8,128)(2,1)S(1)}, bf16[32,1280]{1,0:T(8,128)(2,1)S(1)}, u32[]{:S(2)}, u32[]{:S(2)}) collective-permute-start(bf16[32,1280]{1,0:T(8,128)(2,1)S(1)} %get-tuple-element.16), channel_id=1, source_target_pairs={{0,3},{1,4},{2,5},{3,6},{4,7},{5,0},{6,1},{7,2},{8,11},{9,12},{10,... | collective-permute-start | bytes 245768 | tf_op jit(solution)/shard_map/ppermute | solution.py:287
  69.3 3.5 %collective-permute-start.3 = (bf16[32,1280]{1,0:T(8,128)(2,1)S(1)}, bf16[32,1280]{1,0:T(8,128)(2,1)S(1)}, u32[]{:S(2)}, u32[]{:S(2)}) collective-permute-start(bf16[32,1280]{1,0:T(8,128)(2,1)S(1)} %get-tuple-element.17), channel_id=1, source_target_pairs={{0,4},{1,5},{2,6},{3,7},{4,0},{5,1},{6,2},{7,3},{8,12},{9,13},{10,... | collective-permute-start | bytes 245768 | tf_op jit(solution)/shard_map/ppermute | solution.py:287
  72.9 4.9 %collective-permute-start.4 = (bf16[32,1280]{1,0:T(8,128)(2,1)S(1)}, bf16[32,1280]{1,0:T(8,128)(2,1)S(1)}, u32[]{:S(2)}, u32[]{:S(2)}) collective-permute-start(bf16[32,1280]{1,0:T(8,128)(2,1)S(1)} %get-tuple-element.18), channel_id=1, source_target_pairs={{0,5},{1,6},{2,7},{3,0},{4,1},{5,2},{6,3},{7,4},{8,13},{9,14},{10,... | collective-permute-start | bytes 245768 | tf_op jit(solution)/shard_map/ppermute | solution.py:287
  77.7 0.0 collective-permute-done.refs_1_
  77.8 5.0 %collective-permute-start.5 = (bf16[32,1280]{1,0:T(8,128)(2,1)S(1)}, bf16[32,1280]{1,0:T(8,128)(2,1)S(1)}, u32[]{:S(2)}, u32[]{:S(2)}) collective-permute-start(bf16[32,1280]{1,0:T(8,128)(2,1)S(1)} %get-tuple-element.19), channel_id=1, source_target_pairs={{0,6},{1,7},{2,0},{3,1},{4,2},{5,3},{6,4},{7,5},{8,14},{9,15},{10,... | collective-permute-start | bytes 245768 | tf_op jit(solution)/shard_map/ppermute | solution.py:287
  82.7 0.0 collective-permute-done.1.refs_2_
  82.8 3.2 %collective-permute-start.6 = (bf16[32,1280]{1,0:T(8,128)(2,1)S(1)}, bf16[32,1280]{1,0:T(8,128)(2,1)S(1)}, u32[]{:S(2)}, u32[]{:S(2)}) collective-permute-start(bf16[32,1280]{1,0:T(8,128)(2,1)S(1)} %get-tuple-element.20), channel_id=1, source_target_pairs={{0,7},{1,0},{2,1},{3,2},{4,3},{5,4},{6,5},{7,6},{8,15},{9,8},{10,9... | collective-permute-start | bytes 245768 | tf_op jit(solution)/shard_map/ppermute | solution.py:287
  85.9 0.0 collective-permute-done.2.refs_3_
  85.9 3.8 %collective-permute-done.5.refs_6_ = bf16[32,1280]{1,0:T(8,128)(2,1)S(1)} collective-permute-done((bf16[32,1280]{1,0:T(8,128)(2,1)S(1)}, bf16[32,1280]{1,0:T(8,128)(2,1)S(1)}, u32[]{:S(2)}, u32[]{:S(2)}) %collective-permute-start.5) | collective-permute-done | bytes 81952 | tf_op jit(solution)/shard_map/ppermute | solution.py:287
  89.8 1.0 collective-permute-done.6.refs_7_
  90.7 17.6 %all-to-all-done.1.refs_8_.refs_9_ = bf16[64,8,16,128]{3,2,1,0:T(8,128)(2,1)S(1)} async-done(((bf16[64,8,16,128]{3,2,1,0:T(8,128)(2,1)}), bf16[64,8,16,128]{3,2,1,0:T(8,128)(2,1)S(1)}, u32[]{:S(2)}, u32[]{:S(2)}) %all-to-all-start.1) | async-done | bytes 2097184 | tf_op jit(solution)/shard_map/all_to_all | solution.py:290
  108.4 10.7 %attend.1 = bf16[8,32,1024]{2,1,0:T(8,128)(2,1)S(1)} custom-call(s32[1]{0:T(128)} %bitcast.me_ref, bf16[32,1280]{1,0:T(8,128)(2,1)S(1)} %get-tuple-element.13.refs_0_, bf16[32,1280]{1,0:T(8,128)(2,1)S(1)} %collective-permute-done.refs_1_, bf16[32,1280]{1,0:T(8,128)(2,1)S(1)} %collective-permute-done.1.refs_2_, ...), custom_call_target="tpu_custom_call" | custom-call | flops 4563402752 | bytes 2097152 | tf_op jit(solution)/shard_map/attend/pallas_call | solution.py:222
  119.0 23.2 %all_to_all.16.in_ref = bf16[8,32,1024]{2,1,0:T(8,128)(2,1)S(1)} all-to-all(bf16[8,32,1024]{2,1,0:T(8,128)(2,1)S(1)} %attend.1), channel_id=1, replica_groups=mesh['cache'=64,'tp'=8] {'tp'}, dimensions={0} | all-to-all | bytes 1048576 | tf_op jit(solution)/shard_map/all_to_all | solution.py:292
  142.2 0.8 join_heads.1
  (6 shorter events, 0.0 us)
Async XLA Ops:
  50.8 6.4 %copy-start = (bf16[1,32,8192]{2,1,0:T(8,128)(2,1)S(1)}, bf16[1,32,8192]{2,1,0:T(8,128)(2,1)}, u32[]{:S(2)}) copy-start(bf16[1,32,8192]{2,1,0:T(8,128)(2,1)} %param.6) | copy-start | bytes 1572868
  50.8 6.4 %copy-start.1 = (bf16[1,32,1024]{2,1,0:T(8,128)(2,1)S(1)}, bf16[1,32,1024]{2,1,0:T(8,128)(2,1)}, u32[]{:S(2)}) copy-start(bf16[1,32,1024]{2,1,0:T(8,128)(2,1)} %param.7) | copy-start | bytes 196612
  50.8 6.4 %copy-start.2 = (bf16[1,32,1024]{2,1,0:T(8,128)(2,1)S(1)}, bf16[1,32,1024]{2,1,0:T(8,128)(2,1)}, u32[]{:S(2)}) copy-start(bf16[1,32,1024]{2,1,0:T(8,128)(2,1)} %param.8) | copy-start | bytes 196612
  50.8 57.6 %all-to-all-start.1 = ((bf16[64,8,16,128]{3,2,1,0:T(8,128)(2,1)}), bf16[64,8,16,128]{3,2,1,0:T(8,128)(2,1)S(1)}, u32[]{:S(2)}, u32[]{:S(2)}) async-start(bf16[64,8,16,128]{3,2,1,0:T(8,128)(2,1)} %pick_rows.1), calls=%async_computation.1 | async-start | bytes 4194304 | tf_op jit(solution)/shard_map/all_to_all | solution.py:290
  57.2 20.5 %collective-permute-start = (bf16[32,1280]{1,0:T(8,128)(2,1)S(1)}, bf16[32,1280]{1,0:T(8,128)(2,1)S(1)}, u32[]{:S(2)}, u32[]{:S(2)}) collective-permute-start(bf16[32,1280]{1,0:T(8,128)(2,1)S(1)} %get-tuple-element.14), channel_id=1, source_target_pairs={{0,1},{1,2},{2,3},{3,4},{4,5},{5,6},{6,7},{7,0},{8,9},{9,10},{10,1... | collective-permute-start | bytes 245768 | tf_op jit(solution)/shard_map/ppermute | solution.py:287
  60.5 22.3 %collective-permute-start.1 = (bf16[32,1280]{1,0:T(8,128)(2,1)S(1)}, bf16[32,1280]{1,0:T(8,128)(2,1)S(1)}, u32[]{:S(2)}, u32[]{:S(2)}) collective-permute-start(bf16[32,1280]{1,0:T(8,128)(2,1)S(1)} %get-tuple-element.15), channel_id=1, source_target_pairs={{0,2},{1,3},{2,4},{3,5},{4,6},{5,7},{6,0},{7,1},{8,10},{9,11},{10,... | collective-permute-start | bytes 245768 | tf_op jit(solution)/shard_map/ppermute | solution.py:287
  64.7 21.2 %collective-permute-start.2 = (bf16[32,1280]{1,0:T(8,128)(2,1)S(1)}, bf16[32,1280]{1,0:T(8,128)(2,1)S(1)}, u32[]{:S(2)}, u32[]{:S(2)}) collective-permute-start(bf16[32,1280]{1,0:T(8,128)(2,1)S(1)} %get-tuple-element.16), channel_id=1, source_target_pairs={{0,3},{1,4},{2,5},{3,6},{4,7},{5,0},{6,1},{7,2},{8,11},{9,12},{10,... | collective-permute-start | bytes 245768 | tf_op jit(solution)/shard_map/ppermute | solution.py:287
  69.3 16.6 %collective-permute-start.3 = (bf16[32,1280]{1,0:T(8,128)(2,1)S(1)}, bf16[32,1280]{1,0:T(8,128)(2,1)S(1)}, u32[]{:S(2)}, u32[]{:S(2)}) collective-permute-start(bf16[32,1280]{1,0:T(8,128)(2,1)S(1)} %get-tuple-element.17), channel_id=1, source_target_pairs={{0,4},{1,5},{2,6},{3,7},{4,0},{5,1},{6,2},{7,3},{8,12},{9,13},{10,... | collective-permute-start | bytes 245768 | tf_op jit(solution)/shard_map/ppermute | solution.py:287
  72.9 13.1 %collective-permute-start.4 = (bf16[32,1280]{1,0:T(8,128)(2,1)S(1)}, bf16[32,1280]{1,0:T(8,128)(2,1)S(1)}, u32[]{:S(2)}, u32[]{:S(2)}) collective-permute-start(bf16[32,1280]{1,0:T(8,128)(2,1)S(1)} %get-tuple-element.18), channel_id=1, source_target_pairs={{0,5},{1,6},{2,7},{3,0},{4,1},{5,2},{6,3},{7,4},{8,13},{9,14},{10,... | collective-permute-start | bytes 245768 | tf_op jit(solution)/shard_map/ppermute | solution.py:287
  77.8 12.0 %collective-permute-start.5 = (bf16[32,1280]{1,0:T(8,128)(2,1)S(1)}, bf16[32,1280]{1,0:T(8,128)(2,1)S(1)}, u32[]{:S(2)}, u32[]{:S(2)}) collective-permute-start(bf16[32,1280]{1,0:T(8,128)(2,1)S(1)} %get-tuple-element.19), channel_id=1, source_target_pairs={{0,6},{1,7},{2,0},{3,1},{4,2},{5,3},{6,4},{7,5},{8,14},{9,15},{10,... | collective-permute-start | bytes 245768 | tf_op jit(solution)/shard_map/ppermute | solution.py:287
  82.8 8.0 %collective-permute-start.6 = (bf16[32,1280]{1,0:T(8,128)(2,1)S(1)}, bf16[32,1280]{1,0:T(8,128)(2,1)S(1)}, u32[]{:S(2)}, u32[]{:S(2)}) collective-permute-start(bf16[32,1280]{1,0:T(8,128)(2,1)S(1)} %get-tuple-element.20), channel_id=1, source_target_pairs={{0,7},{1,0},{2,1},{3,2},{4,3},{5,4},{6,5},{7,6},{8,15},{9,8},{10,9... | collective-permute-start | bytes 245768 | tf_op jit(solution)/shard_map/ppermute | solution.py:287

commit v7 on v6

--- a/solution.py
+++ b/solution.py
@@ -2,6 +2,7 @@
 
 import jax
 import jax.numpy as jnp
+import numpy as np
 from jax import lax
 from jax.experimental import pallas as pl
 from jax.experimental.pallas import tpu as pltpu
@@ -38,7 +39,8 @@
                     copy.start()
                     copies[side, i, n] = copy
         list_copy.wait()
-        spread = lax.broadcasted_iota(jnp.int32, (top, width), 0) == lax.broadcasted_iota(jnp.int32, (top, width), 1)
+        lane = lax.broadcasted_iota(jnp.int32, (top, width), 1)
+        spread = lax.rem(lane, top) == lax.broadcasted_iota(jnp.int32, (top, width), 0)
         note = jnp.dot(
             list_buf[...].astype(jnp.bfloat16), spread.astype(jnp.bfloat16), preferred_element_type=jnp.float32
         )
@@ -70,9 +72,9 @@
     )
 
 
-def pick_rows(bands, lists, owned):
-    parts, top = lists.shape
-    width = bands.shape[2]
+def pick_rows(bands, lists, owned, top):
+    parts, _, width = bands.shape
+    each = lists.shape[1] // top
     assert owned & (owned - 1) == 0
     shift = owned.bit_length() - 1
 
@@ -83,7 +85,7 @@
         def one(d, carry):
             found = []
             for j in range(top):
-                passage = lists_ref[d, j]
+                passage = lists_ref[lax.div(d, each), lax.rem(d, each) * top + j]
                 at = pl.multiple_of(lax.bitwise_and(passage, owned - 1) * ROWS, ROWS)
                 found.append(bands_ref[lax.shift_right_logical(passage, shift), pl.ds(at, ROWS)])
             for j in range(top):
@@ -281,12 +283,15 @@
         top = lists.shape[1]
         bands = cut_bands(cache_keys, cache_values, lists, parts)
         bands = lax.all_to_all(bands, "cache", split_axis=0, concat_axis=0, tiled=True)
-        seen = bands[:, owned * ROWS, :top].astype(jnp.int32)
+        lanes = bands.shape[2]
+        each = lanes // top
+        mine = np.arange(parts)[:, None] % each == np.arange(lanes)[None, :] // top
+        seen = jnp.where(mine, bands[:, owned * ROWS], 0).astype(jnp.int32).reshape(parts // each, each, lanes).sum(1)
         cuts = cut_heads(query[0], qkeys[0], qvalues[0], at_tp, tp)
         parts_q = [cuts[0]] + [
             lax.ppermute(cuts[k], "tp", [(d, (d + k) % tp) for d in range(tp)]) for k in range(1, tp)
         ]
-        picked = pick_rows(bands, seen, owned)
+        picked = pick_rows(bands, seen, owned, top)
         received = lax.all_to_all(picked, "cache", split_axis=0, concat_axis=0, tiled=True)
         result = attend(parts_q, received, at_tp, group)
         back = lax.all_to_all(result, "tp", split_axis=0, concat_axis=0, tiled=True)

time: 144 us -> 144 us (level)
  no operation moved by 1% of the time
where the time goes in v7:
time: 144 us; the launch traced here: 143 us
  blocking collectives  69.2 us (48%)
  starting transfers between devices  34.9 us (24%)
  waiting for transfers between devices  22.4 us (16%)
  Pallas kernels  15.8 us (11%)
    all_to_all x1, blocking collectives, local(): lax.all_to_all(bands, 'cache', split_axis=0, concat_axis=0, tiled=True)  46 us
    ppermute x7, starting transfers between devices, local(): lax.ppermute(cuts[k], 'tp', [(d, (d + k) % tp) for d in range(tp)])  28.6 us
    all_to_all x1, blocking collectives, local(): back = lax.all_to_all(result, 'tp', split_axis=0, concat_axis=0, tiled=True)  23.2 us
    all_to_all x1, waiting for transfers between devices, local(): lax.all_to_all(picked, 'cache', split_axis=0, concat_axis=0, tiled=True)  17.6 us
    pallas_call x1, Pallas kernels, attend(): pl.pallas_call(kernel, grid_spec=pltpu.PrefetchScalarGridSpec(num_scalar_...  10.7 us
    all_to_all x1, starting transfers between devices, local(): lax.all_to_all(picked, 'cache', split_axis=0, concat_axis=0, tiled=True)  6.33 us
    ppermute x7, waiting for transfers between devices, local(): lax.ppermute(cuts[k], 'tp', [(d, (d + k) % tp) for d in range(tp)])  4.8 us
  transfers between devices with their start and end apart: 8, of which 3 were waited for; matrix products, arithmetic and copies ran while one was open for 0% of the time, Pallas kernels for 0%

profile of v7, /device:TPU:1, one launch (start us, length us, event | category | flops | bytes accessed | tf_op | source)
XLA Modules:
  0.0 142.8 jit_solution(18105607084664844791)
XLA Ops:
  0.0 1.6 %cut_bands.1 = bf16[64,72,128]{2,1,0:T(8,128)(2,1)S(1)} custom-call(s32[1,8]{1,0:T(1,128)} %lists_ref.1, bf16[4,512,128]{2,1,0:T(8,128)(2,1)} %k_ref.1, bf16[4,512,128]{2,1,0:T(8,128)(2,1)} %v_ref.1), custom_call_target="tpu_custom_call" | custom-call | tf_op jit(solution)/shard_map/cut_bands/pallas_call | solution.py:55
  1.6 0.0 copy-start.3
  1.6 46.0 %all_to_all.15.bands_ref = bf16[64,72,128]{2,1,0:T(8,128)(2,1)S(1)} all-to-all(bf16[64,72,128]{2,1,0:T(8,128)(2,1)S(1)} %cut_bands.1), channel_id=1, replica_groups=mesh['cache'=64,'tp'=8] {'cache'}, dimensions={0} | all-to-all | bytes 2359296 | tf_op jit(solution)/shard_map/all_to_all | solution.py:285
  47.6 0.1 fusion
  47.7 2.6 %pick_rows.1 = bf16[64,8,16,128]{3,2,1,0:T(8,128)(2,1)} custom-call(s32[4,128]{1,0:T(4,128)S(1)} %bitcast_reduce_fusion.lists_ref, bf16[64,72,128]{2,1,0:T(8,128)(2,1)S(1)} %all_to_all.15.bands_ref), custom_call_target="tpu_custom_call" | custom-call | tf_op jit(solution)/shard_map/pick_rows/pallas_call | solution.py:104
  50.3 0.0 copy-start
  50.3 0.0 copy-start.1
  50.3 0.0 copy-start.2
  50.3 6.3 %all-to-all-start.1 = ((bf16[64,8,16,128]{3,2,1,0:T(8,128)(2,1)}), bf16[64,8,16,128]{3,2,1,0:T(8,128)(2,1)S(1)}, u32[]{:S(2)}, u32[]{:S(2)}) async-start(bf16[64,8,16,128]{3,2,1,0:T(8,128)(2,1)} %pick_rows.1), calls=%async_computation.1 | async-start | bytes 4194304 | tf_op jit(solution)/shard_map/all_to_all | solution.py:295
  56.7 0.1 cut_heads.1
  56.8 3.2 %collective-permute-start = (bf16[32,1280]{1,0:T(8,128)(2,1)S(1)}, bf16[32,1280]{1,0:T(8,128)(2,1)S(1)}, u32[]{:S(2)}, u32[]{:S(2)}) collective-permute-start(bf16[32,1280]{1,0:T(8,128)(2,1)S(1)} %get-tuple-element.14), channel_id=1, source_target_pairs={{0,1},{1,2},{2,3},{3,4},{4,5},{5,6},{6,7},{7,0},{8,9},{9,10},{10,1... | collective-permute-start | bytes 245768 | tf_op jit(solution)/shard_map/ppermute | solution.py:292
  60.0 4.2 %collective-permute-start.1 = (bf16[32,1280]{1,0:T(8,128)(2,1)S(1)}, bf16[32,1280]{1,0:T(8,128)(2,1)S(1)}, u32[]{:S(2)}, u32[]{:S(2)}) collective-permute-start(bf16[32,1280]{1,0:T(8,128)(2,1)S(1)} %get-tuple-element.15), channel_id=1, source_target_pairs={{0,2},{1,3},{2,4},{3,5},{4,6},{5,7},{6,0},{7,1},{8,10},{9,11},{10,... | collective-permute-start | bytes 245768 | tf_op jit(solution)/shard_map/ppermute | solution.py:292
  64.2 4.6 %collective-permute-start.2 = (bf16[32,1280]{1,0:T(8,128)(2,1)S(1)}, bf16[32,1280]{1,0:T(8,128)(2,1)S(1)}, u32[]{:S(2)}, u32[]{:S(2)}) collective-permute-start(bf16[32,1280]{1,0:T(8,128)(2,1)S(1)} %get-tuple-element.16), channel_id=1, source_target_pairs={{0,3},{1,4},{2,5},{3,6},{4,7},{5,0},{6,1},{7,2},{8,11},{9,12},{10,... | collective-permute-start | bytes 245768 | tf_op jit(solution)/shard_map/ppermute | solution.py:292
  68.9 3.5 %collective-permute-start.3 = (bf16[32,1280]{1,0:T(8,128)(2,1)S(1)}, bf16[32,1280]{1,0:T(8,128)(2,1)S(1)}, u32[]{:S(2)}, u32[]{:S(2)}) collective-permute-start(bf16[32,1280]{1,0:T(8,128)(2,1)S(1)} %get-tuple-element.17), channel_id=1, source_target_pairs={{0,4},{1,5},{2,6},{3,7},{4,0},{5,1},{6,2},{7,3},{8,12},{9,13},{10,... | collective-permute-start | bytes 245768 | tf_op jit(solution)/shard_map/ppermute | solution.py:292
  72.4 4.9 %collective-permute-start.4 = (bf16[32,1280]{1,0:T(8,128)(2,1)S(1)}, bf16[32,1280]{1,0:T(8,128)(2,1)S(1)}, u32[]{:S(2)}, u32[]{:S(2)}) collective-permute-start(bf16[32,1280]{1,0:T(8,128)(2,1)S(1)} %get-tuple-element.18), channel_id=1, source_target_pairs={{0,5},{1,6},{2,7},{3,0},{4,1},{5,2},{6,3},{7,4},{8,13},{9,14},{10,... | collective-permute-start | bytes 245768 | tf_op jit(solution)/shard_map/ppermute | solution.py:292
  77.3 0.0 collective-permute-done.refs_1_
  77.3 5.0 %collective-permute-start.5 = (bf16[32,1280]{1,0:T(8,128)(2,1)S(1)}, bf16[32,1280]{1,0:T(8,128)(2,1)S(1)}, u32[]{:S(2)}, u32[]{:S(2)}) collective-permute-start(bf16[32,1280]{1,0:T(8,128)(2,1)S(1)} %get-tuple-element.19), channel_id=1, source_target_pairs={{0,6},{1,7},{2,0},{3,1},{4,2},{5,3},{6,4},{7,5},{8,14},{9,15},{10,... | collective-permute-start | bytes 245768 | tf_op jit(solution)/shard_map/ppermute | solution.py:292
  82.3 3.2 %collective-permute-start.6 = (bf16[32,1280]{1,0:T(8,128)(2,1)S(1)}, bf16[32,1280]{1,0:T(8,128)(2,1)S(1)}, u32[]{:S(2)}, u32[]{:S(2)}) collective-permute-start(bf16[32,1280]{1,0:T(8,128)(2,1)S(1)} %get-tuple-element.20), channel_id=1, source_target_pairs={{0,7},{1,0},{2,1},{3,2},{4,3},{5,4},{6,5},{7,6},{8,15},{9,8},{10,9... | collective-permute-start | bytes 245768 | tf_op jit(solution)/shard_map/ppermute | solution.py:292
  85.5 3.8 %collective-permute-done.5.refs_6_ = bf16[32,1280]{1,0:T(8,128)(2,1)S(1)} collective-permute-done((bf16[32,1280]{1,0:T(8,128)(2,1)S(1)}, bf16[32,1280]{1,0:T(8,128)(2,1)S(1)}, u32[]{:S(2)}, u32[]{:S(2)}) %collective-permute-start.5) | collective-permute-done | bytes 81952 | tf_op jit(solution)/shard_map/ppermute | solution.py:292
  89.3 1.0 collective-permute-done.6.refs_7_
  90.3 17.6 %all-to-all-done.1.refs_8_.refs_9_ = bf16[64,8,16,128]{3,2,1,0:T(8,128)(2,1)S(1)} async-done(((bf16[64,8,16,128]{3,2,1,0:T(8,128)(2,1)}), bf16[64,8,16,128]{3,2,1,0:T(8,128)(2,1)S(1)}, u32[]{:S(2)}, u32[]{:S(2)}) %all-to-all-start.1) | async-done | bytes 2097184 | tf_op jit(solution)/shard_map/all_to_all | solution.py:295
  107.9 10.7 %attend.1 = bf16[8,32,1024]{2,1,0:T(8,128)(2,1)S(1)} custom-call(s32[1]{0:T(128)} %bitcast.me_ref, bf16[32,1280]{1,0:T(8,128)(2,1)S(1)} %get-tuple-element.13.refs_0_, bf16[32,1280]{1,0:T(8,128)(2,1)S(1)} %collective-permute-done.refs_1_, bf16[32,1280]{1,0:T(8,128)(2,1)S(1)} %collective-permute-done.1.refs_2_, ...), custom_call_target="tpu_custom_call" | custom-call | flops 4563402752 | bytes 2097152 | tf_op jit(solution)/shard_map/attend/pallas_call | solution.py:224
  118.6 23.2 %all_to_all.16.in_ref = bf16[8,32,1024]{2,1,0:T(8,128)(2,1)S(1)} all-to-all(bf16[8,32,1024]{2,1,0:T(8,128)(2,1)S(1)} %attend.1), channel_id=1, replica_groups=mesh['cache'=64,'tp'=8] {'tp'}, dimensions={0} | all-to-all | bytes 1048576 | tf_op jit(solution)/shard_map/all_to_all | solution.py:297
  141.8 0.8 join_heads.1
  (9 shorter events, 0.0 us)
Async XLA Ops:
  1.6 46.0 %copy-start.3 = (pred[64,1,128]{2,1,0:T(4,128)(4,1)S(1)}, pred[64,1,128]{2,1,0:T(4,128)(4,1)}, u32[]{:S(2)}) copy-start(pred[64,1,128]{2,1,0:T(4,128)(4,1)} %constant.17) | copy-start | bytes 24580
  50.3 6.4 %copy-start = (bf16[1,32,8192]{2,1,0:T(8,128)(2,1)S(1)}, bf16[1,32,8192]{2,1,0:T(8,128)(2,1)}, u32[]{:S(2)}) copy-start(bf16[1,32,8192]{2,1,0:T(8,128)(2,1)} %param.7) | copy-start | bytes 1572868
  50.3 6.4 %copy-start.1 = (bf16[1,32,1024]{2,1,0:T(8,128)(2,1)S(1)}, bf16[1,32,1024]{2,1,0:T(8,128)(2,1)}, u32[]{:S(2)}) copy-start(bf16[1,32,1024]{2,1,0:T(8,128)(2,1)} %param.8) | copy-start | bytes 196612
  50.3 6.4 %copy-start.2 = (bf16[1,32,1024]{2,1,0:T(8,128)(2,1)S(1)}, bf16[1,32,1024]{2,1,0:T(8,128)(2,1)}, u32[]{:S(2)}) copy-start(bf16[1,32,1024]{2,1,0:T(8,128)(2,1)} %param.9) | copy-start | bytes 196612
  50.3 57.6 %all-to-all-start.1 = ((bf16[64,8,16,128]{3,2,1,0:T(8,128)(2,1)}), bf16[64,8,16,128]{3,2,1,0:T(8,128)(2,1)S(1)}, u32[]{:S(2)}, u32[]{:S(2)}) async-start(bf16[64,8,16,128]{3,2,1,0:T(8,128)(2,1)} %pick_rows.1), calls=%async_computation.1 | async-start | bytes 4194304 | tf_op jit(solution)/shard_map/all_to_all | solution.py:295
  56.8 20.5 %collective-permute-start = (bf16[32,1280]{1,0:T(8,128)(2,1)S(1)}, bf16[32,1280]{1,0:T(8,128)(2,1)S(1)}, u32[]{:S(2)}, u32[]{:S(2)}) collective-permute-start(bf16[32,1280]{1,0:T(8,128)(2,1)S(1)} %get-tuple-element.14), channel_id=1, source_target_pairs={{0,1},{1,2},{2,3},{3,4},{4,5},{5,6},{6,7},{7,0},{8,9},{9,10},{10,1... | collective-permute-start | bytes 245768 | tf_op jit(solution)/shard_map/ppermute | solution.py:292
  60.0 22.3 %collective-permute-start.1 = (bf16[32,1280]{1,0:T(8,128)(2,1)S(1)}, bf16[32,1280]{1,0:T(8,128)(2,1)S(1)}, u32[]{:S(2)}, u32[]{:S(2)}) collective-permute-start(bf16[32,1280]{1,0:T(8,128)(2,1)S(1)} %get-tuple-element.15), channel_id=1, source_target_pairs={{0,2},{1,3},{2,4},{3,5},{4,6},{5,7},{6,0},{7,1},{8,10},{9,11},{10,... | collective-permute-start | bytes 245768 | tf_op jit(solution)/shard_map/ppermute | solution.py:292
  64.2 21.2 %collective-permute-start.2 = (bf16[32,1280]{1,0:T(8,128)(2,1)S(1)}, bf16[32,1280]{1,0:T(8,128)(2,1)S(1)}, u32[]{:S(2)}, u32[]{:S(2)}) collective-permute-start(bf16[32,1280]{1,0:T(8,128)(2,1)S(1)} %get-tuple-element.16), channel_id=1, source_target_pairs={{0,3},{1,4},{2,5},{3,6},{4,7},{5,0},{6,1},{7,2},{8,11},{9,12},{10,... | collective-permute-start | bytes 245768 | tf_op jit(solution)/shard_map/ppermute | solution.py:292
  68.9 16.6 %collective-permute-start.3 = (bf16[32,1280]{1,0:T(8,128)(2,1)S(1)}, bf16[32,1280]{1,0:T(8,128)(2,1)S(1)}, u32[]{:S(2)}, u32[]{:S(2)}) collective-permute-start(bf16[32,1280]{1,0:T(8,128)(2,1)S(1)} %get-tuple-element.17), channel_id=1, source_target_pairs={{0,4},{1,5},{2,6},{3,7},{4,0},{5,1},{6,2},{7,3},{8,12},{9,13},{10,... | collective-permute-start | bytes 245768 | tf_op jit(solution)/shard_map/ppermute | solution.py:292
  72.4 13.1 %collective-permute-start.4 = (bf16[32,1280]{1,0:T(8,128)(2,1)S(1)}, bf16[32,1280]{1,0:T(8,128)(2,1)S(1)}, u32[]{:S(2)}, u32[]{:S(2)}) collective-permute-start(bf16[32,1280]{1,0:T(8,128)(2,1)S(1)} %get-tuple-element.18), channel_id=1, source_target_pairs={{0,5},{1,6},{2,7},{3,0},{4,1},{5,2},{6,3},{7,4},{8,13},{9,14},{10,... | collective-permute-start | bytes 245768 | tf_op jit(solution)/shard_map/ppermute | solution.py:292
  77.3 12.0 %collective-permute-start.5 = (bf16[32,1280]{1,0:T(8,128)(2,1)S(1)}, bf16[32,1280]{1,0:T(8,128)(2,1)S(1)}, u32[]{:S(2)}, u32[]{:S(2)}) collective-permute-start(bf16[32,1280]{1,0:T(8,128)(2,1)S(1)} %get-tuple-element.19), channel_id=1, source_target_pairs={{0,6},{1,7},{2,0},{3,1},{4,2},{5,3},{6,4},{7,5},{8,14},{9,15},{10,... | collective-permute-start | bytes 245768 | tf_op jit(solution)/shard_map/ppermute | solution.py:292
  82.3 8.0 %collective-permute-start.6 = (bf16[32,1280]{1,0:T(8,128)(2,1)S(1)}, bf16[32,1280]{1,0:T(8,128)(2,1)S(1)}, u32[]{:S(2)}, u32[]{:S(2)}) collective-permute-start(bf16[32,1280]{1,0:T(8,128)(2,1)S(1)} %get-tuple-element.20), channel_id=1, source_target_pairs={{0,7},{1,0},{2,1},{3,2},{4,3},{5,4},{6,5},{7,6},{8,15},{9,8},{10,9... | collective-permute-start | bytes 245768 | tf_op jit(solution)/shard_map/ppermute | solution.py:292

commit v8 on v7

--- a/solution.py
+++ b/solution.py
@@ -24,10 +24,10 @@
     half = parts // 2
     rows = owned * ROWS
     top = lists.shape[1]
-    pieces = 4
+    pieces = 1
     part = plen // pieces
 
-    def kernel(lists_ref, k_ref, v_ref, out_ref, list_buf, bufs, list_sem, sems):
+    def kernel(lists_ref, k_ref, v_ref, out_ref, note_ref, list_buf, bufs, list_sem, sems):
         list_copy = pltpu.make_async_copy(lists_ref, list_buf, list_sem)
         list_copy.start()
         copies = {}
@@ -44,7 +44,7 @@
         note = jnp.dot(
             list_buf[...].astype(jnp.bfloat16), spread.astype(jnp.bfloat16), preferred_element_type=jnp.float32
         )
-        out_ref[:, rows:] = jnp.broadcast_to(note.astype(out_ref.dtype)[None], (parts, EXTRA, width))
+        note_ref[...] = jnp.broadcast_to(note, (ROWS, width)).astype(note_ref.dtype)
         for i in range(owned):
             at = slice(i * ROWS, (i + 1) * ROWS)
             for side in range(2):
@@ -55,14 +55,17 @@
     return pl.pallas_call(
         kernel,
         in_specs=[pl.BlockSpec(memory_space=pltpu.HBM)] * 3,
-        out_specs=pl.BlockSpec(memory_space=pltpu.VMEM),
+        out_specs=[pl.BlockSpec(memory_space=pltpu.VMEM)] * 2,
         scratch_shapes=[
             pltpu.VMEM(lists.shape, lists.dtype),
             pltpu.VMEM((2, owned, plen, width), cache_keys.dtype),
             pltpu.SemaphoreType.DMA,
             pltpu.SemaphoreType.DMA((2, owned, pieces)),
         ],
-        out_shape=jax.ShapeDtypeStruct((parts, rows + EXTRA, width), cache_keys.dtype),
+        out_shape=[
+            jax.ShapeDtypeStruct((parts, rows + EXTRA, width), cache_keys.dtype),
+            jax.ShapeDtypeStruct((ROWS, width), cache_keys.dtype),
+        ],
         compiler_params=pltpu.CompilerParams(vmem_limit_bytes=40 * 1024 * 1024),
         name="cut_bands",
     )(
@@ -78,7 +81,7 @@
     assert owned & (owned - 1) == 0
     shift = owned.bit_length() - 1
 
-    steps = 16
+    steps = 8
     share = parts // steps
 
     def kernel(lists_ref, bands_ref, out_ref, buf, sems):
@@ -94,7 +97,7 @@
 
         copies = []
         for step in range(steps):
-            lax.fori_loop(step * share, (step + 1) * share, one, 0, unroll=4)
+            lax.fori_loop(step * share, (step + 1) * share, one, 0, unroll=8)
             at = pl.ds(step * share, share)
             copies.append(pltpu.make_async_copy(buf.at[at], out_ref.at[at], sems.at[step]))
             copies[-1].start()
@@ -152,7 +155,7 @@
     half = bands // 2
     keys_n = half * top * rows
     all_n = keys_n + qlen
-    per = 2
+    per = 1
     chunk = 512
     span = 1024
     factor = HD ** (-0.5) * LOG2E
@@ -281,7 +284,8 @@
         group = query.shape[2] // qkeys.shape[2]
 
         top = lists.shape[1]
-        bands = cut_bands(cache_keys, cache_values, lists, parts)
+        bands, note = cut_bands(cache_keys, cache_values, lists, parts)
+        bands = bands.at[:, owned * ROWS :].set(note[None, :EXTRA])
         bands = lax.all_to_all(bands, "cache", split_axis=0, concat_axis=0, tiled=True)
         lanes = bands.shape[2]
         each = lanes // top

time: 144 us -> 143 us (level)
  no operation moved by 1% of the time
where the time goes in v8:
time: 143 us
  blocking collectives  69.1 us (48%)
  starting transfers between devices  34.9 us (24%)
  waiting for transfers between devices  22.4 us (16%)
  Pallas kernels  15.5 us (11%)
    all_to_all x1, blocking collectives, local(): lax.all_to_all(bands, 'cache', split_axis=0, concat_axis=0, tiled=True)  46 us
    ppermute x7, starting transfers between devices, local(): lax.ppermute(cuts[k], 'tp', [(d, (d + k) % tp) for d in range(tp)])  28.6 us
    all_to_all x1, blocking collectives, local(): back = lax.all_to_all(result, 'tp', split_axis=0, concat_axis=0, tiled=True)  23.1 us
    all_to_all x1, waiting for transfers between devices, local(): lax.all_to_all(picked, 'cache', split_axis=0, concat_axis=0, tiled=True)  17.6 us
    pallas_call x1, Pallas kernels, attend(): pl.pallas_call(kernel, grid_spec=pltpu.PrefetchScalarGridSpec(num_scalar_...  10.6 us
    all_to_all x1, starting transfers between devices, local(): lax.all_to_all(picked, 'cache', split_axis=0, concat_axis=0, tiled=True)  6.33 us
    ppermute x7, waiting for transfers between devices, local(): lax.ppermute(cuts[k], 'tp', [(d, (d + k) % tp) for d in range(tp)])  4.8 us
  transfers between devices with their start and end apart: 8, of which 3 were waited for; matrix products, arithmetic and copies ran while one was open for 0% of the time, Pallas kernels for 0%

profile of v8, /device:TPU:1, one launch (start us, length us, event | category | flops | bytes accessed | tf_op | source)
XLA Modules:
  0.0 142.5 jit_solution(10398742847258022054)
XLA Ops:
  0.0 1.4 cut_bands.1
  1.4 0.0 copy-start.3
  1.5 46.0 %all_to_all.15.bands_ref = bf16[64,72,128]{2,1,0:T(8,128)(2,1)S(1)} all-to-all(bf16[64,72,128]{2,1,0:T(8,128)(2,1)S(1)} %broadcast_dynamic-update-slice_fusion), channel_id=1, replica_groups=mesh['cache'=64,'tp'=8] {'cache'}, dimensions={0} | all-to-all | bytes 2359296 | tf_op jit(solution)/shard_map/all_to_all | solution.py:289
  47.5 0.1 fusion
  47.5 2.6 %pick_rows.1 = bf16[64,8,16,128]{3,2,1,0:T(8,128)(2,1)} custom-call(s32[4,128]{1,0:T(4,128)S(1)} %bitcast_reduce_fusion.lists_ref, bf16[64,72,128]{2,1,0:T(8,128)(2,1)S(1)} %all_to_all.15.bands_ref), custom_call_target="tpu_custom_call" | custom-call | tf_op jit(solution)/shard_map/pick_rows/pallas_call | solution.py:107
  50.2 0.0 copy-start
  50.2 0.0 copy-start.1
  50.2 0.0 copy-start.2
  50.2 6.3 %all-to-all-start.1 = ((bf16[64,8,16,128]{3,2,1,0:T(8,128)(2,1)}), bf16[64,8,16,128]{3,2,1,0:T(8,128)(2,1)S(1)}, u32[]{:S(2)}, u32[]{:S(2)}) async-start(bf16[64,8,16,128]{3,2,1,0:T(8,128)(2,1)} %pick_rows.1), calls=%async_computation.1 | async-start | bytes 4194304 | tf_op jit(solution)/shard_map/all_to_all | solution.py:299
  56.6 0.1 cut_heads.1
  56.6 3.2 %collective-permute-start = (bf16[32,1280]{1,0:T(8,128)(2,1)S(1)}, bf16[32,1280]{1,0:T(8,128)(2,1)S(1)}, u32[]{:S(2)}, u32[]{:S(2)}) collective-permute-start(bf16[32,1280]{1,0:T(8,128)(2,1)S(1)} %get-tuple-element.28), channel_id=1, source_target_pairs={{0,1},{1,2},{2,3},{3,4},{4,5},{5,6},{6,7},{7,0},{8,9},{9,10},{10,1... | collective-permute-start | bytes 245768 | tf_op jit(solution)/shard_map/ppermute | solution.py:296
  59.9 4.2 %collective-permute-start.1 = (bf16[32,1280]{1,0:T(8,128)(2,1)S(1)}, bf16[32,1280]{1,0:T(8,128)(2,1)S(1)}, u32[]{:S(2)}, u32[]{:S(2)}) collective-permute-start(bf16[32,1280]{1,0:T(8,128)(2,1)S(1)} %get-tuple-element.29), channel_id=1, source_target_pairs={{0,2},{1,3},{2,4},{3,5},{4,6},{5,7},{6,0},{7,1},{8,10},{9,11},{10,... | collective-permute-start | bytes 245768 | tf_op jit(solution)/shard_map/ppermute | solution.py:296
  64.1 4.6 %collective-permute-start.2 = (bf16[32,1280]{1,0:T(8,128)(2,1)S(1)}, bf16[32,1280]{1,0:T(8,128)(2,1)S(1)}, u32[]{:S(2)}, u32[]{:S(2)}) collective-permute-start(bf16[32,1280]{1,0:T(8,128)(2,1)S(1)} %get-tuple-element.30), channel_id=1, source_target_pairs={{0,3},{1,4},{2,5},{3,6},{4,7},{5,0},{6,1},{7,2},{8,11},{9,12},{10,... | collective-permute-start | bytes 245768 | tf_op jit(solution)/shard_map/ppermute | solution.py:296
  68.7 3.5 %collective-permute-start.3 = (bf16[32,1280]{1,0:T(8,128)(2,1)S(1)}, bf16[32,1280]{1,0:T(8,128)(2,1)S(1)}, u32[]{:S(2)}, u32[]{:S(2)}) collective-permute-start(bf16[32,1280]{1,0:T(8,128)(2,1)S(1)} %get-tuple-element.31), channel_id=1, source_target_pairs={{0,4},{1,5},{2,6},{3,7},{4,0},{5,1},{6,2},{7,3},{8,12},{9,13},{10,... | collective-permute-start | bytes 245768 | tf_op jit(solution)/shard_map/ppermute | solution.py:296
  72.3 4.9 %collective-permute-start.4 = (bf16[32,1280]{1,0:T(8,128)(2,1)S(1)}, bf16[32,1280]{1,0:T(8,128)(2,1)S(1)}, u32[]{:S(2)}, u32[]{:S(2)}) collective-permute-start(bf16[32,1280]{1,0:T(8,128)(2,1)S(1)} %get-tuple-element.32), channel_id=1, source_target_pairs={{0,5},{1,6},{2,7},{3,0},{4,1},{5,2},{6,3},{7,4},{8,13},{9,14},{10,... | collective-permute-start | bytes 245768 | tf_op jit(solution)/shard_map/ppermute | solution.py:296
  77.2 5.0 %collective-permute-start.5 = (bf16[32,1280]{1,0:T(8,128)(2,1)S(1)}, bf16[32,1280]{1,0:T(8,128)(2,1)S(1)}, u32[]{:S(2)}, u32[]{:S(2)}) collective-permute-start(bf16[32,1280]{1,0:T(8,128)(2,1)S(1)} %get-tuple-element.33), channel_id=1, source_target_pairs={{0,6},{1,7},{2,0},{3,1},{4,2},{5,3},{6,4},{7,5},{8,14},{9,15},{10,... | collective-permute-start | bytes 245768 | tf_op jit(solution)/shard_map/ppermute | solution.py:296
  82.1 0.0 collective-permute-done.1.refs_2_
  82.1 3.2 %collective-permute-start.6 = (bf16[32,1280]{1,0:T(8,128)(2,1)S(1)}, bf16[32,1280]{1,0:T(8,128)(2,1)S(1)}, u32[]{:S(2)}, u32[]{:S(2)}) collective-permute-start(bf16[32,1280]{1,0:T(8,128)(2,1)S(1)} %get-tuple-element.34), channel_id=1, source_target_pairs={{0,7},{1,0},{2,1},{3,2},{4,3},{5,4},{6,5},{7,6},{8,15},{9,8},{10,9... | collective-permute-start | bytes 245768 | tf_op jit(solution)/shard_map/ppermute | solution.py:296
  85.3 3.8 %collective-permute-done.5.refs_6_ = bf16[32,1280]{1,0:T(8,128)(2,1)S(1)} collective-permute-done((bf16[32,1280]{1,0:T(8,128)(2,1)S(1)}, bf16[32,1280]{1,0:T(8,128)(2,1)S(1)}, u32[]{:S(2)}, u32[]{:S(2)}) %collective-permute-start.5) | collective-permute-done | bytes 81952 | tf_op jit(solution)/shard_map/ppermute | solution.py:296
  89.2 1.0 collective-permute-done.6.refs_7_
  90.1 17.6 %all-to-all-done.1.refs_8_.refs_9_ = bf16[64,8,16,128]{3,2,1,0:T(8,128)(2,1)S(1)} async-done(((bf16[64,8,16,128]{3,2,1,0:T(8,128)(2,1)}), bf16[64,8,16,128]{3,2,1,0:T(8,128)(2,1)S(1)}, u32[]{:S(2)}, u32[]{:S(2)}) %all-to-all-start.1) | async-done | bytes 2097184 | tf_op jit(solution)/shard_map/all_to_all | solution.py:299
  107.8 10.6 %attend.1 = bf16[8,32,1024]{2,1,0:T(8,128)(2,1)S(1)} custom-call(s32[1]{0:T(128)} %bitcast.me_ref, bf16[32,1280]{1,0:T(8,128)(2,1)S(1)} %get-tuple-element.27.refs_0_, bf16[32,1280]{1,0:T(8,128)(2,1)S(1)} %collective-permute-done.refs_1_, bf16[32,1280]{1,0:T(8,128)(2,1)S(1)} %collective-permute-done.1.refs_2_, ...), custom_call_target="tpu_custom_call" | custom-call | flops 4563402752 | bytes 2097152 | tf_op jit(solution)/shard_map/attend/pallas_call | solution.py:227
  118.4 23.1 %all_to_all.16.in_ref = bf16[8,32,1024]{2,1,0:T(8,128)(2,1)S(1)} all-to-all(bf16[8,32,1024]{2,1,0:T(8,128)(2,1)S(1)} %attend.1), channel_id=1, replica_groups=mesh['cache'=64,'tp'=8] {'tp'}, dimensions={0} | all-to-all | bytes 1048576 | tf_op jit(solution)/shard_map/all_to_all | solution.py:301
  141.5 0.8 join_heads.1
  (11 shorter events, 0.1 us)
Async XLA Ops:
  1.4 46.0 %copy-start.3 = (pred[64,1,128]{2,1,0:T(4,128)(4,1)S(1)}, pred[64,1,128]{2,1,0:T(4,128)(4,1)}, u32[]{:S(2)}) copy-start(pred[64,1,128]{2,1,0:T(4,128)(4,1)} %constant.45) | copy-start | bytes 24580
  50.2 6.4 %copy-start = (bf16[1,32,8192]{2,1,0:T(8,128)(2,1)S(1)}, bf16[1,32,8192]{2,1,0:T(8,128)(2,1)}, u32[]{:S(2)}) copy-start(bf16[1,32,8192]{2,1,0:T(8,128)(2,1)} %param.9) | copy-start | bytes 1572868
  50.2 6.4 %copy-start.1 = (bf16[1,32,1024]{2,1,0:T(8,128)(2,1)S(1)}, bf16[1,32,1024]{2,1,0:T(8,128)(2,1)}, u32[]{:S(2)}) copy-start(bf16[1,32,1024]{2,1,0:T(8,128)(2,1)} %param.10) | copy-start | bytes 196612
  50.2 6.4 %copy-start.2 = (bf16[1,32,1024]{2,1,0:T(8,128)(2,1)S(1)}, bf16[1,32,1024]{2,1,0:T(8,128)(2,1)}, u32[]{:S(2)}) copy-start(bf16[1,32,1024]{2,1,0:T(8,128)(2,1)} %param.11) | copy-start | bytes 196612
  50.2 57.6 %all-to-all-start.1 = ((bf16[64,8,16,128]{3,2,1,0:T(8,128)(2,1)}), bf16[64,8,16,128]{3,2,1,0:T(8,128)(2,1)S(1)}, u32[]{:S(2)}, u32[]{:S(2)}) async-start(bf16[64,8,16,128]{3,2,1,0:T(8,128)(2,1)} %pick_rows.1), calls=%async_computation.1 | async-start | bytes 4194304 | tf_op jit(solution)/shard_map/all_to_all | solution.py:299
  56.6 20.5 %collective-permute-start = (bf16[32,1280]{1,0:T(8,128)(2,1)S(1)}, bf16[32,1280]{1,0:T(8,128)(2,1)S(1)}, u32[]{:S(2)}, u32[]{:S(2)}) collective-permute-start(bf16[32,1280]{1,0:T(8,128)(2,1)S(1)} %get-tuple-element.28), channel_id=1, source_target_pairs={{0,1},{1,2},{2,3},{3,4},{4,5},{5,6},{6,7},{7,0},{8,9},{9,10},{10,1... | collective-permute-start | bytes 245768 | tf_op jit(solution)/shard_map/ppermute | solution.py:296
  59.9 22.3 %collective-permute-start.1 = (bf16[32,1280]{1,0:T(8,128)(2,1)S(1)}, bf16[32,1280]{1,0:T(8,128)(2,1)S(1)}, u32[]{:S(2)}, u32[]{:S(2)}) collective-permute-start(bf16[32,1280]{1,0:T(8,128)(2,1)S(1)} %get-tuple-element.29), channel_id=1, source_target_pairs={{0,2},{1,3},{2,4},{3,5},{4,6},{5,7},{6,0},{7,1},{8,10},{9,11},{10,... | collective-permute-start | bytes 245768 | tf_op jit(solution)/shard_map/ppermute | solution.py:296
  64.1 21.2 %collective-permute-start.2 = (bf16[32,1280]{1,0:T(8,128)(2,1)S(1)}, bf16[32,1280]{1,0:T(8,128)(2,1)S(1)}, u32[]{:S(2)}, u32[]{:S(2)}) collective-permute-start(bf16[32,1280]{1,0:T(8,128)(2,1)S(1)} %get-tuple-element.30), channel_id=1, source_target_pairs={{0,3},{1,4},{2,5},{3,6},{4,7},{5,0},{6,1},{7,2},{8,11},{9,12},{10,... | collective-permute-start | bytes 245768 | tf_op jit(solution)/shard_map/ppermute | solution.py:296
  68.7 16.6 %collective-permute-start.3 = (bf16[32,1280]{1,0:T(8,128)(2,1)S(1)}, bf16[32,1280]{1,0:T(8,128)(2,1)S(1)}, u32[]{:S(2)}, u32[]{:S(2)}) collective-permute-start(bf16[32,1280]{1,0:T(8,128)(2,1)S(1)} %get-tuple-element.31), channel_id=1, source_target_pairs={{0,4},{1,5},{2,6},{3,7},{4,0},{5,1},{6,2},{7,3},{8,12},{9,13},{10,... | collective-permute-start | bytes 245768 | tf_op jit(solution)/shard_map/ppermute | solution.py:296
  72.3 13.1 %collective-permute-start.4 = (bf16[32,1280]{1,0:T(8,128)(2,1)S(1)}, bf16[32,1280]{1,0:T(8,128)(2,1)S(1)}, u32[]{:S(2)}, u32[]{:S(2)}) collective-permute-start(bf16[32,1280]{1,0:T(8,128)(2,1)S(1)} %get-tuple-element.32), channel_id=1, source_target_pairs={{0,5},{1,6},{2,7},{3,0},{4,1},{5,2},{6,3},{7,4},{8,13},{9,14},{10,... | collective-permute-start | bytes 245768 | tf_op jit(solution)/shard_map/ppermute | solution.py:296
  77.2 12.0 %collective-permute-start.5 = (bf16[32,1280]{1,0:T(8,128)(2,1)S(1)}, bf16[32,1280]{1,0:T(8,128)(2,1)S(1)}, u32[]{:S(2)}, u32[]{:S(2)}) collective-permute-start(bf16[32,1280]{1,0:T(8,128)(2,1)S(1)} %get-tuple-element.33), channel_id=1, source_target_pairs={{0,6},{1,7},{2,0},{3,1},{4,2},{5,3},{6,4},{7,5},{8,14},{9,15},{10,... | collective-permute-start | bytes 245768 | tf_op jit(solution)/shard_map/ppermute | solution.py:296
  82.1 8.0 %collective-permute-start.6 = (bf16[32,1280]{1,0:T(8,128)(2,1)S(1)}, bf16[32,1280]{1,0:T(8,128)(2,1)S(1)}, u32[]{:S(2)}, u32[]{:S(2)}) collective-permute-start(bf16[32,1280]{1,0:T(8,128)(2,1)S(1)} %get-tuple-element.34), channel_id=1, source_target_pairs={{0,7},{1,0},{2,1},{3,2},{4,3},{5,4},{6,5},{7,6},{8,15},{9,8},{10,9... | collective-permute-start | bytes 245768 | tf_op jit(solution)/shard_map/ppermute | solution.py:296

commit v9 on v8

--- a/solution.py
+++ b/solution.py
@@ -12,6 +12,7 @@
 EXTRA = 8
 ROWS = 16
 LOG2E = 1.4426950408889634
+LARGE = 1e30
 VMEM = pltpu.CompilerParams(vmem_limit_bytes=48 * 1024 * 1024)
 
 
@@ -155,7 +156,6 @@
     half = bands // 2
     keys_n = half * top * rows
     all_n = keys_n + qlen
-    per = 1
     chunk = 512
     span = 1024
     factor = HD ** (-0.5) * LOG2E
@@ -179,50 +179,71 @@
             owner = lax.bitwise_and(mine - index // tokens + tp, tp - 1)
             return owner * tokens + lax.rem(index, tokens)
 
-        sees = jnp.concatenate([position(0) >= position(1)] * per, axis=0)
+        sees = position(0) >= position(1)
         own_keys = jnp.concatenate([q_refs[k][:, width : width + HD] for k in range(tp)], axis=0)
 
-        def score_steps(g):
-            heads = [slice((g * per + p) * HD, (g * per + p + 1) * HD) for p in range(per)]
-            q = jnp.concatenate([q_refs[k][:, at] for at in heads for k in range(tp)], axis=0)
-
-            def own_step(most):
-                s = lax.dot_general(q, own_keys, dims, preferred_element_type=jnp.float32)
-                s = jnp.where(sees, s, -jnp.inf)
-                scores[g % 2, :, keys_n:] = s
-                return lane_max(s, most)
-
-            def step(c, most):
-                keys = k_ref[c // (top * rows) : (c + chunk) // (top * rows)].reshape(chunk, HD)
-                s = lax.dot_general(q, keys, dims, preferred_element_type=jnp.float32)
-                scores[g % 2, :, c : c + chunk] = s
-                return lane_max(s, most)
-
-            return [own_step] + [functools.partial(step, c) for c in range(0, keys_n, chunk)]
-
-        most = None
-        for step in score_steps(0):
-            most = step(most)
-        spans = [(c, min(c + span, all_n)) for c in range(0, all_n, span)]
-        groups = group // per
-        for g in range(groups):
-            m = jnp.max(most, axis=1, keepdims=True)
-            steps = score_steps(g + 1) if g + 1 < groups else []
-            most, total_o, done = None, None, 0
-            for i, (lo, hi) in enumerate(spans):
-                upto = -(-len(steps) * (i + 1) // len(spans))
-                for step in steps[done:upto]:
-                    most = step(most)
-                done = upto
-                w = jnp.exp2((scores[g % 2, :, lo:hi] - m) * factor).astype(values.dtype)
-                o = jnp.dot(w, values[lo:hi], preferred_element_type=jnp.float32)
-                total_o = o if total_o is None else total_o + o
-            o = (total_o[:, :HD] / total_o[:, HD:]).astype(out_ref.dtype)
-            for p in range(per):
-                for k in range(tp):
-                    owner = lax.bitwise_and(mine - k + tp, tp - 1)
-                    at = p * qlen + k * tokens
-                    out_ref[owner, :, (g * per + p) * HD : (g * per + p + 1) * HD] = o[at : at + tokens]
+        def columns(g):
+            return pl.ds(pl.multiple_of(g * HD, HD), HD)
+
+        def queries(at):
+            return jnp.concatenate([q_refs[k][:, at] for k in range(tp)], axis=0)
+
+        def own_scores(q):
+            return jnp.where(sees, lax.dot_general(q, own_keys, dims, preferred_element_type=jnp.float32), -jnp.inf)
+
+        def listed_scores(q, c):
+            keys = k_ref[c // (top * rows) : (c + chunk) // (top * rows)].reshape(chunk, HD)
+            return lax.dot_general(q, keys, dims, preferred_element_type=jnp.float32)
+
+        def weigh(s, m):
+            return jnp.exp2((s - m) * factor).astype(values.dtype)
+
+        def add_up(w, lo):
+            return jnp.dot(w, values[lo : lo + w.shape[1]], preferred_element_type=jnp.float32)
+
+        def store(at, sums):
+            o = (sums[:, :HD] / sums[:, HD:]).astype(out_ref.dtype)
+            for k in range(tp):
+                owner = lax.bitwise_and(mine - k + tp, tp - 1)
+                out_ref[owner, :, at] = o[k * tokens : (k + 1) * tokens]
+
+        def begin(g):
+            q = queries(slice(g * HD, (g + 1) * HD))
+            s = own_scores(q)
+            return q, s, jnp.max(lane_max(s, None), axis=1, keepdims=True)
+
+        following = begin(0)
+        too_large = jnp.zeros((qlen, HD), jnp.float32)
+        for g in range(group):
+            q, s, m = following
+            sums = add_up(weigh(s, m), keys_n)
+            for lo in range(0, keys_n, span):
+                w = [weigh(listed_scores(q, c), m) for c in range(lo, lo + span, chunk)]
+                sums = sums + add_up(jnp.concatenate(w, axis=1), lo)
+                if lo == keys_n // 2 and g + 1 < group:
+                    following = begin(g + 1)
+            too_large = jnp.maximum(too_large, jnp.where(sums[:, HD:] < LARGE, 0.0, 1.0))
+            store(slice(g * HD, (g + 1) * HD), sums)
+
+        @pl.when(jnp.max(too_large) > 0.0)
+        def _():
+            def again(g, carry):
+                q = queries(columns(g))
+                s = own_scores(q)
+                scores[:, keys_n:] = s
+                most = lane_max(s, None)
+                for c in range(0, keys_n, chunk):
+                    s = listed_scores(q, c)
+                    scores[:, c : c + chunk] = s
+                    most = lane_max(s, most)
+                m = jnp.max(most, axis=1, keepdims=True)
+                sums = add_up(weigh(scores[:, keys_n:], m), keys_n)
+                for c in range(0, keys_n, chunk):
+                    sums = sums + add_up(weigh(scores[:, c : c + chunk], m), c)
+                store(columns(g), sums)
+                return carry
+
+            lax.fori_loop(0, group, again, 0)
 
     return pl.pallas_call(
         kernel,
@@ -236,7 +257,7 @@
             ],
             out_specs=whole((tp, tokens, width)),
             scratch_shapes=[
-                pltpu.VMEM((2, per * qlen, all_n), jnp.float32),
+                pltpu.VMEM((qlen, all_n), jnp.float32),
                 pltpu.VMEM((all_n, 2 * HD), jnp.bfloat16),
             ],
         ),

time: 143 us -> 143 us (level)
  no operation moved by 1% of the time
where the time goes in v9:
time: 143 us; the launch traced here: 142 us
  blocking collectives  69.2 us (48%)
  starting transfers between devices  34.9 us (24%)
  waiting for transfers between devices  22.4 us (16%)
  Pallas kernels  14.8 us (10%)
    all_to_all x1, blocking collectives, local(): lax.all_to_all(bands, 'cache', split_axis=0, concat_axis=0, tiled=True)  46 us
    ppermute x7, starting transfers between devices, local(): lax.ppermute(cuts[k], 'tp', [(d, (d + k) % tp) for d in range(tp)])  28.6 us
    all_to_all x1, blocking collectives, local(): back = lax.all_to_all(result, 'tp', split_axis=0, concat_axis=0, tiled=True)  23.2 us
    all_to_all x1, waiting for transfers between devices, local(): lax.all_to_all(picked, 'cache', split_axis=0, concat_axis=0, tiled=True)  17.6 us
    pallas_call x1, Pallas kernels, attend(): pl.pallas_call(kernel, grid_spec=pltpu.PrefetchScalarGridSpec(num_scalar_...  9.93 us
    all_to_all x1, starting transfers between devices, local(): lax.all_to_all(picked, 'cache', split_axis=0, concat_axis=0, tiled=True)  6.33 us
    ppermute x7, waiting for transfers between devices, local(): lax.ppermute(cuts[k], 'tp', [(d, (d + k) % tp) for d in range(tp)])  4.8 us
  transfers between devices with their start and end apart: 8, of which 3 were waited for; matrix products, arithmetic and copies ran while one was open for 0% of the time, Pallas kernels for 0%

profile of v9, /device:TPU:1, one launch (start us, length us, event | category | flops | bytes accessed | tf_op | source)
XLA Modules:
  0.0 141.9 jit_solution(14052959986570910237)
XLA Ops:
  0.0 1.4 cut_bands.1
  1.4 0.0 copy-start.3
  1.5 46.0 %all_to_all.15.bands_ref = bf16[64,72,128]{2,1,0:T(8,128)(2,1)S(1)} all-to-all(bf16[64,72,128]{2,1,0:T(8,128)(2,1)S(1)} %broadcast_dynamic-update-slice_fusion), channel_id=1, replica_groups=mesh['cache'=64,'tp'=8] {'cache'}, dimensions={0} | all-to-all | bytes 2359296 | tf_op jit(solution)/shard_map/all_to_all | solution.py:310
  47.5 0.1 fusion
  47.5 2.6 %pick_rows.1 = bf16[64,8,16,128]{3,2,1,0:T(8,128)(2,1)} custom-call(s32[4,128]{1,0:T(4,128)S(1)} %bitcast_reduce_fusion.lists_ref, bf16[64,72,128]{2,1,0:T(8,128)(2,1)S(1)} %all_to_all.15.bands_ref), custom_call_target="tpu_custom_call" | custom-call | tf_op jit(solution)/shard_map/pick_rows/pallas_call | solution.py:108
  50.2 0.0 copy-start
  50.2 0.0 copy-start.1
  50.2 0.0 copy-start.2
  50.2 6.3 %all-to-all-start.1 = ((bf16[64,8,16,128]{3,2,1,0:T(8,128)(2,1)}), bf16[64,8,16,128]{3,2,1,0:T(8,128)(2,1)S(1)}, u32[]{:S(2)}, u32[]{:S(2)}) async-start(bf16[64,8,16,128]{3,2,1,0:T(8,128)(2,1)} %pick_rows.1), calls=%async_computation.1 | async-start | bytes 4194304 | tf_op jit(solution)/shard_map/all_to_all | solution.py:320
  56.6 0.1 cut_heads.1
  56.6 3.2 %collective-permute-start = (bf16[32,1280]{1,0:T(8,128)(2,1)S(1)}, bf16[32,1280]{1,0:T(8,128)(2,1)S(1)}, u32[]{:S(2)}, u32[]{:S(2)}) collective-permute-start(bf16[32,1280]{1,0:T(8,128)(2,1)S(1)} %get-tuple-element.28), channel_id=1, source_target_pairs={{0,1},{1,2},{2,3},{3,4},{4,5},{5,6},{6,7},{7,0},{8,9},{9,10},{10,1... | collective-permute-start | bytes 245768 | tf_op jit(solution)/shard_map/ppermute | solution.py:317
  59.9 4.2 %collective-permute-start.1 = (bf16[32,1280]{1,0:T(8,128)(2,1)S(1)}, bf16[32,1280]{1,0:T(8,128)(2,1)S(1)}, u32[]{:S(2)}, u32[]{:S(2)}) collective-permute-start(bf16[32,1280]{1,0:T(8,128)(2,1)S(1)} %get-tuple-element.29), channel_id=1, source_target_pairs={{0,2},{1,3},{2,4},{3,5},{4,6},{5,7},{6,0},{7,1},{8,10},{9,11},{10,... | collective-permute-start | bytes 245768 | tf_op jit(solution)/shard_map/ppermute | solution.py:317
  64.1 4.6 %collective-permute-start.2 = (bf16[32,1280]{1,0:T(8,128)(2,1)S(1)}, bf16[32,1280]{1,0:T(8,128)(2,1)S(1)}, u32[]{:S(2)}, u32[]{:S(2)}) collective-permute-start(bf16[32,1280]{1,0:T(8,128)(2,1)S(1)} %get-tuple-element.30), channel_id=1, source_target_pairs={{0,3},{1,4},{2,5},{3,6},{4,7},{5,0},{6,1},{7,2},{8,11},{9,12},{10,... | collective-permute-start | bytes 245768 | tf_op jit(solution)/shard_map/ppermute | solution.py:317
  68.7 3.5 %collective-permute-start.3 = (bf16[32,1280]{1,0:T(8,128)(2,1)S(1)}, bf16[32,1280]{1,0:T(8,128)(2,1)S(1)}, u32[]{:S(2)}, u32[]{:S(2)}) collective-permute-start(bf16[32,1280]{1,0:T(8,128)(2,1)S(1)} %get-tuple-element.31), channel_id=1, source_target_pairs={{0,4},{1,5},{2,6},{3,7},{4,0},{5,1},{6,2},{7,3},{8,12},{9,13},{10,... | collective-permute-start | bytes 245768 | tf_op jit(solution)/shard_map/ppermute | solution.py:317
  72.3 4.9 %collective-permute-start.4 = (bf16[32,1280]{1,0:T(8,128)(2,1)S(1)}, bf16[32,1280]{1,0:T(8,128)(2,1)S(1)}, u32[]{:S(2)}, u32[]{:S(2)}) collective-permute-start(bf16[32,1280]{1,0:T(8,128)(2,1)S(1)} %get-tuple-element.32), channel_id=1, source_target_pairs={{0,5},{1,6},{2,7},{3,0},{4,1},{5,2},{6,3},{7,4},{8,13},{9,14},{10,... | collective-permute-start | bytes 245768 | tf_op jit(solution)/shard_map/ppermute | solution.py:317
  77.2 5.0 %collective-permute-start.5 = (bf16[32,1280]{1,0:T(8,128)(2,1)S(1)}, bf16[32,1280]{1,0:T(8,128)(2,1)S(1)}, u32[]{:S(2)}, u32[]{:S(2)}) collective-permute-start(bf16[32,1280]{1,0:T(8,128)(2,1)S(1)} %get-tuple-element.33), channel_id=1, source_target_pairs={{0,6},{1,7},{2,0},{3,1},{4,2},{5,3},{6,4},{7,5},{8,14},{9,15},{10,... | collective-permute-start | bytes 245768 | tf_op jit(solution)/shard_map/ppermute | solution.py:317
  82.1 0.0 collective-permute-done.1.refs_2_
  82.1 3.2 %collective-permute-start.6 = (bf16[32,1280]{1,0:T(8,128)(2,1)S(1)}, bf16[32,1280]{1,0:T(8,128)(2,1)S(1)}, u32[]{:S(2)}, u32[]{:S(2)}) collective-permute-start(bf16[32,1280]{1,0:T(8,128)(2,1)S(1)} %get-tuple-element.34), channel_id=1, source_target_pairs={{0,7},{1,0},{2,1},{3,2},{4,3},{5,4},{6,5},{7,6},{8,15},{9,8},{10,9... | collective-permute-start | bytes 245768 | tf_op jit(solution)/shard_map/ppermute | solution.py:317
  85.3 3.8 %collective-permute-done.5.refs_6_ = bf16[32,1280]{1,0:T(8,128)(2,1)S(1)} collective-permute-done((bf16[32,1280]{1,0:T(8,128)(2,1)S(1)}, bf16[32,1280]{1,0:T(8,128)(2,1)S(1)}, u32[]{:S(2)}, u32[]{:S(2)}) %collective-permute-start.5) | collective-permute-done | bytes 81952 | tf_op jit(solution)/shard_map/ppermute | solution.py:317
  89.2 1.0 collective-permute-done.6.refs_7_
  90.1 17.6 %all-to-all-done.1.refs_8_.refs_9_ = bf16[64,8,16,128]{3,2,1,0:T(8,128)(2,1)S(1)} async-done(((bf16[64,8,16,128]{3,2,1,0:T(8,128)(2,1)}), bf16[64,8,16,128]{3,2,1,0:T(8,128)(2,1)S(1)}, u32[]{:S(2)}, u32[]{:S(2)}) %all-to-all-start.1) | async-done | bytes 2097184 | tf_op jit(solution)/shard_map/all_to_all | solution.py:320
  107.8 9.9 %attend.1 = bf16[8,32,1024]{2,1,0:T(8,128)(2,1)S(1)} custom-call(s32[1]{0:T(128)} %bitcast.me_ref, bf16[32,1280]{1,0:T(8,128)(2,1)S(1)} %get-tuple-element.27.refs_0_, bf16[32,1280]{1,0:T(8,128)(2,1)S(1)} %collective-permute-done.refs_1_, bf16[32,1280]{1,0:T(8,128)(2,1)S(1)} %collective-permute-done.1.refs_2_, ...), custom_call_target="tpu_custom_call" | custom-call | flops 4563402752 | bytes 2097152 | tf_op jit(solution)/shard_map/attend/pallas_call | solution.py:248
  117.7 23.2 %all_to_all.16.in_ref = bf16[8,32,1024]{2,1,0:T(8,128)(2,1)S(1)} all-to-all(bf16[8,32,1024]{2,1,0:T(8,128)(2,1)S(1)} %attend.1), channel_id=1, replica_groups=mesh['cache'=64,'tp'=8] {'tp'}, dimensions={0} | all-to-all | bytes 1048576 | tf_op jit(solution)/shard_map/all_to_all | solution.py:322
  140.9 0.8 join_heads.1
  (11 shorter events, 0.1 us)
Async XLA Ops:
  1.4 46.0 %copy-start.3 = (pred[64,1,128]{2,1,0:T(4,128)(4,1)S(1)}, pred[64,1,128]{2,1,0:T(4,128)(4,1)}, u32[]{:S(2)}) copy-start(pred[64,1,128]{2,1,0:T(4,128)(4,1)} %constant.45) | copy-start | bytes 24580
  50.2 6.4 %copy-start = (bf16[1,32,8192]{2,1,0:T(8,128)(2,1)S(1)}, bf16[1,32,8192]{2,1,0:T(8,128)(2,1)}, u32[]{:S(2)}) copy-start(bf16[1,32,8192]{2,1,0:T(8,128)(2,1)} %param.9) | copy-start | bytes 1572868
  50.2 6.4 %copy-start.1 = (bf16[1,32,1024]{2,1,0:T(8,128)(2,1)S(1)}, bf16[1,32,1024]{2,1,0:T(8,128)(2,1)}, u32[]{:S(2)}) copy-start(bf16[1,32,1024]{2,1,0:T(8,128)(2,1)} %param.10) | copy-start | bytes 196612
  50.2 6.4 %copy-start.2 = (bf16[1,32,1024]{2,1,0:T(8,128)(2,1)S(1)}, bf16[1,32,1024]{2,1,0:T(8,128)(2,1)}, u32[]{:S(2)}) copy-start(bf16[1,32,1024]{2,1,0:T(8,128)(2,1)} %param.11) | copy-start | bytes 196612
  50.2 57.6 %all-to-all-start.1 = ((bf16[64,8,16,128]{3,2,1,0:T(8,128)(2,1)}), bf16[64,8,16,128]{3,2,1,0:T(8,128)(2,1)S(1)}, u32[]{:S(2)}, u32[]{:S(2)}) async-start(bf16[64,8,16,128]{3,2,1,0:T(8,128)(2,1)} %pick_rows.1), calls=%async_computation.1 | async-start | bytes 4194304 | tf_op jit(solution)/shard_map/all_to_all | solution.py:320
  56.6 20.5 %collective-permute-start = (bf16[32,1280]{1,0:T(8,128)(2,1)S(1)}, bf16[32,1280]{1,0:T(8,128)(2,1)S(1)}, u32[]{:S(2)}, u32[]{:S(2)}) collective-permute-start(bf16[32,1280]{1,0:T(8,128)(2,1)S(1)} %get-tuple-element.28), channel_id=1, source_target_pairs={{0,1},{1,2},{2,3},{3,4},{4,5},{5,6},{6,7},{7,0},{8,9},{9,10},{10,1... | collective-permute-start | bytes 245768 | tf_op jit(solution)/shard_map/ppermute | solution.py:317
  59.9 22.3 %collective-permute-start.1 = (bf16[32,1280]{1,0:T(8,128)(2,1)S(1)}, bf16[32,1280]{1,0:T(8,128)(2,1)S(1)}, u32[]{:S(2)}, u32[]{:S(2)}) collective-permute-start(bf16[32,1280]{1,0:T(8,128)(2,1)S(1)} %get-tuple-element.29), channel_id=1, source_target_pairs={{0,2},{1,3},{2,4},{3,5},{4,6},{5,7},{6,0},{7,1},{8,10},{9,11},{10,... | collective-permute-start | bytes 245768 | tf_op jit(solution)/shard_map/ppermute | solution.py:317
  64.1 21.2 %collective-permute-start.2 = (bf16[32,1280]{1,0:T(8,128)(2,1)S(1)}, bf16[32,1280]{1,0:T(8,128)(2,1)S(1)}, u32[]{:S(2)}, u32[]{:S(2)}) collective-permute-start(bf16[32,1280]{1,0:T(8,128)(2,1)S(1)} %get-tuple-element.30), channel_id=1, source_target_pairs={{0,3},{1,4},{2,5},{3,6},{4,7},{5,0},{6,1},{7,2},{8,11},{9,12},{10,... | collective-permute-start | bytes 245768 | tf_op jit(solution)/shard_map/ppermute | solution.py:317
  68.7 16.6 %collective-permute-start.3 = (bf16[32,1280]{1,0:T(8,128)(2,1)S(1)}, bf16[32,1280]{1,0:T(8,128)(2,1)S(1)}, u32[]{:S(2)}, u32[]{:S(2)}) collective-permute-start(bf16[32,1280]{1,0:T(8,128)(2,1)S(1)} %get-tuple-element.31), channel_id=1, source_target_pairs={{0,4},{1,5},{2,6},{3,7},{4,0},{5,1},{6,2},{7,3},{8,12},{9,13},{10,... | collective-permute-start | bytes 245768 | tf_op jit(solution)/shard_map/ppermute | solution.py:317
  72.3 13.1 %collective-permute-start.4 = (bf16[32,1280]{1,0:T(8,128)(2,1)S(1)}, bf16[32,1280]{1,0:T(8,128)(2,1)S(1)}, u32[]{:S(2)}, u32[]{:S(2)}) collective-permute-start(bf16[32,1280]{1,0:T(8,128)(2,1)S(1)} %get-tuple-element.32), channel_id=1, source_target_pairs={{0,5},{1,6},{2,7},{3,0},{4,1},{5,2},{6,3},{7,4},{8,13},{9,14},{10,... | collective-permute-start | bytes 245768 | tf_op jit(solution)/shard_map/ppermute | solution.py:317
  77.2 12.0 %collective-permute-start.5 = (bf16[32,1280]{1,0:T(8,128)(2,1)S(1)}, bf16[32,1280]{1,0:T(8,128)(2,1)S(1)}, u32[]{:S(2)}, u32[]{:S(2)}) collective-permute-start(bf16[32,1280]{1,0:T(8,128)(2,1)S(1)} %get-tuple-element.33), channel_id=1, source_target_pairs={{0,6},{1,7},{2,0},{3,1},{4,2},{5,3},{6,4},{7,5},{8,14},{9,15},{10,... | collective-permute-start | bytes 245768 | tf_op jit(solution)/shard_map/ppermute | solution.py:317
  82.1 8.0 %collective-permute-start.6 = (bf16[32,1280]{1,0:T(8,128)(2,1)S(1)}, bf16[32,1280]{1,0:T(8,128)(2,1)S(1)}, u32[]{:S(2)}, u32[]{:S(2)}) collective-permute-start(bf16[32,1280]{1,0:T(8,128)(2,1)S(1)} %get-tuple-element.34), channel_id=1, source_target_pairs={{0,7},{1,0},{2,1},{3,2},{4,3},{5,4},{6,5},{7,6},{8,15},{9,8},{10,9... | collective-permute-start | bytes 245768 | tf_op jit(solution)/shard_map/ppermute | solution.py:317

commit v10 on v9

--- a/solution.py
+++ b/solution.py
@@ -157,7 +157,7 @@
     keys_n = half * top * rows
     all_n = keys_n + qlen
     chunk = 512
-    span = 1024
+    span = 2048
     factor = HD ** (-0.5) * LOG2E
     dims = (((1,), (1,)), ((), ()))
 
@@ -274,11 +274,17 @@
 
 def join_heads(back):
     groups, tokens, width = back.shape
+    half = tokens // 2
 
     def kernel(in_ref, out_ref, sems):
         copies = [
-            pltpu.make_async_copy(in_ref.at[g], out_ref.at[0, :, pl.ds(g * width, width)], sems.at[g])
+            pltpu.make_async_copy(
+                in_ref.at[g, pl.ds(n * half, half)],
+                out_ref.at[0, pl.ds(n * half, half), pl.ds(g * width, width)],
+                sems.at[g, n],
+            )
             for g in range(groups)
+            for n in range(2)
         ]
         for copy in copies:
             copy.start()
@@ -289,7 +295,7 @@
         kernel,
         in_specs=[pl.BlockSpec(memory_space=pltpu.VMEM)],
         out_specs=pl.BlockSpec(memory_space=pl.ANY),
-        scratch_shapes=[pltpu.SemaphoreType.DMA((groups,))],
+        scratch_shapes=[pltpu.SemaphoreType.DMA((groups, 2))],
         out_shape=jax.ShapeDtypeStruct((1, tokens, groups * width), back.dtype),
         compiler_params=VMEM,
         name="join_heads",

time: 143 us -> 143 us (level)
  no operation moved by 1% of the time
where the time goes in v10:
time: 143 us; the launch traced here: 142 us
  blocking collectives  69.2 us (48%)
  starting transfers between devices  34.9 us (24%)
  waiting for transfers between devices  22.4 us (16%)
  Pallas kernels  15 us (10%)
    all_to_all x1, blocking collectives, local(): lax.all_to_all(bands, 'cache', split_axis=0, concat_axis=0, tiled=True)  46 us
    ppermute x7, starting transfers between devices, local(): lax.ppermute(cuts[k], 'tp', [(d, (d + k) % tp) for d in range(tp)])  28.6 us
    all_to_all x1, blocking collectives, local(): back = lax.all_to_all(result, 'tp', split_axis=0, concat_axis=0, tiled=True)  23.2 us
    all_to_all x1, waiting for transfers between devices, local(): lax.all_to_all(picked, 'cache', split_axis=0, concat_axis=0, tiled=True)  17.6 us
    pallas_call x1, Pallas kernels, attend(): pl.pallas_call(kernel, grid_spec=pltpu.PrefetchScalarGridSpec(num_scalar_...  10 us
    all_to_all x1, starting transfers between devices, local(): lax.all_to_all(picked, 'cache', split_axis=0, concat_axis=0, tiled=True)  6.33 us
    ppermute x7, waiting for transfers between devices, local(): lax.ppermute(cuts[k], 'tp', [(d, (d + k) % tp) for d in range(tp)])  4.8 us
  transfers between devices with their start and end apart: 8, of which 3 were waited for; matrix products, arithmetic and copies ran while one was open for 0% of the time, Pallas kernels for 0%

profile of v10, /device:TPU:1, one launch (start us, length us, event | category | flops | bytes accessed | tf_op | source)
XLA Modules:
  0.0 142.1 jit_solution(6420964532382667725)
XLA Ops:
  0.0 1.4 cut_bands.1
  1.4 0.0 copy-start.3
  1.5 46.0 %all_to_all.15.bands_ref = bf16[64,72,128]{2,1,0:T(8,128)(2,1)S(1)} all-to-all(bf16[64,72,128]{2,1,0:T(8,128)(2,1)S(1)} %broadcast_dynamic-update-slice_fusion), channel_id=1, replica_groups=mesh['cache'=64,'tp'=8] {'cache'}, dimensions={0} | all-to-all | bytes 2359296 | tf_op jit(solution)/shard_map/all_to_all | solution.py:316
  47.5 0.1 fusion
  47.5 2.6 %pick_rows.1 = bf16[64,8,16,128]{3,2,1,0:T(8,128)(2,1)} custom-call(s32[4,128]{1,0:T(4,128)S(1)} %bitcast_reduce_fusion.lists_ref, bf16[64,72,128]{2,1,0:T(8,128)(2,1)S(1)} %all_to_all.15.bands_ref), custom_call_target="tpu_custom_call" | custom-call | tf_op jit(solution)/shard_map/pick_rows/pallas_call | solution.py:108
  50.2 0.0 copy-start
  50.2 0.0 copy-start.1
  50.2 0.0 copy-start.2
  50.2 6.3 %all-to-all-start.1 = ((bf16[64,8,16,128]{3,2,1,0:T(8,128)(2,1)}), bf16[64,8,16,128]{3,2,1,0:T(8,128)(2,1)S(1)}, u32[]{:S(2)}, u32[]{:S(2)}) async-start(bf16[64,8,16,128]{3,2,1,0:T(8,128)(2,1)} %pick_rows.1), calls=%async_computation.1 | async-start | bytes 4194304 | tf_op jit(solution)/shard_map/all_to_all | solution.py:326
  56.6 0.1 cut_heads.1
  56.6 3.2 %collective-permute-start = (bf16[32,1280]{1,0:T(8,128)(2,1)S(1)}, bf16[32,1280]{1,0:T(8,128)(2,1)S(1)}, u32[]{:S(2)}, u32[]{:S(2)}) collective-permute-start(bf16[32,1280]{1,0:T(8,128)(2,1)S(1)} %get-tuple-element.28), channel_id=1, source_target_pairs={{0,1},{1,2},{2,3},{3,4},{4,5},{5,6},{6,7},{7,0},{8,9},{9,10},{10,1... | collective-permute-start | bytes 245768 | tf_op jit(solution)/shard_map/ppermute | solution.py:323
  59.9 4.2 %collective-permute-start.1 = (bf16[32,1280]{1,0:T(8,128)(2,1)S(1)}, bf16[32,1280]{1,0:T(8,128)(2,1)S(1)}, u32[]{:S(2)}, u32[]{:S(2)}) collective-permute-start(bf16[32,1280]{1,0:T(8,128)(2,1)S(1)} %get-tuple-element.29), channel_id=1, source_target_pairs={{0,2},{1,3},{2,4},{3,5},{4,6},{5,7},{6,0},{7,1},{8,10},{9,11},{10,... | collective-permute-start | bytes 245768 | tf_op jit(solution)/shard_map/ppermute | solution.py:323
  64.1 4.6 %collective-permute-start.2 = (bf16[32,1280]{1,0:T(8,128)(2,1)S(1)}, bf16[32,1280]{1,0:T(8,128)(2,1)S(1)}, u32[]{:S(2)}, u32[]{:S(2)}) collective-permute-start(bf16[32,1280]{1,0:T(8,128)(2,1)S(1)} %get-tuple-element.30), channel_id=1, source_target_pairs={{0,3},{1,4},{2,5},{3,6},{4,7},{5,0},{6,1},{7,2},{8,11},{9,12},{10,... | collective-permute-start | bytes 245768 | tf_op jit(solution)/shard_map/ppermute | solution.py:323
  68.7 3.5 %collective-permute-start.3 = (bf16[32,1280]{1,0:T(8,128)(2,1)S(1)}, bf16[32,1280]{1,0:T(8,128)(2,1)S(1)}, u32[]{:S(2)}, u32[]{:S(2)}) collective-permute-start(bf16[32,1280]{1,0:T(8,128)(2,1)S(1)} %get-tuple-element.31), channel_id=1, source_target_pairs={{0,4},{1,5},{2,6},{3,7},{4,0},{5,1},{6,2},{7,3},{8,12},{9,13},{10,... | collective-permute-start | bytes 245768 | tf_op jit(solution)/shard_map/ppermute | solution.py:323
  72.3 4.9 %collective-permute-start.4 = (bf16[32,1280]{1,0:T(8,128)(2,1)S(1)}, bf16[32,1280]{1,0:T(8,128)(2,1)S(1)}, u32[]{:S(2)}, u32[]{:S(2)}) collective-permute-start(bf16[32,1280]{1,0:T(8,128)(2,1)S(1)} %get-tuple-element.32), channel_id=1, source_target_pairs={{0,5},{1,6},{2,7},{3,0},{4,1},{5,2},{6,3},{7,4},{8,13},{9,14},{10,... | collective-permute-start | bytes 245768 | tf_op jit(solution)/shard_map/ppermute | solution.py:323
  77.2 5.0 %collective-permute-start.5 = (bf16[32,1280]{1,0:T(8,128)(2,1)S(1)}, bf16[32,1280]{1,0:T(8,128)(2,1)S(1)}, u32[]{:S(2)}, u32[]{:S(2)}) collective-permute-start(bf16[32,1280]{1,0:T(8,128)(2,1)S(1)} %get-tuple-element.33), channel_id=1, source_target_pairs={{0,6},{1,7},{2,0},{3,1},{4,2},{5,3},{6,4},{7,5},{8,14},{9,15},{10,... | collective-permute-start | bytes 245768 | tf_op jit(solution)/shard_map/ppermute | solution.py:323
  82.1 0.0 collective-permute-done.1.refs_2_
  82.1 3.2 %collective-permute-start.6 = (bf16[32,1280]{1,0:T(8,128)(2,1)S(1)}, bf16[32,1280]{1,0:T(8,128)(2,1)S(1)}, u32[]{:S(2)}, u32[]{:S(2)}) collective-permute-start(bf16[32,1280]{1,0:T(8,128)(2,1)S(1)} %get-tuple-element.34), channel_id=1, source_target_pairs={{0,7},{1,0},{2,1},{3,2},{4,3},{5,4},{6,5},{7,6},{8,15},{9,8},{10,9... | collective-permute-start | bytes 245768 | tf_op jit(solution)/shard_map/ppermute | solution.py:323
  85.3 3.8 %collective-permute-done.5.refs_6_ = bf16[32,1280]{1,0:T(8,128)(2,1)S(1)} collective-permute-done((bf16[32,1280]{1,0:T(8,128)(2,1)S(1)}, bf16[32,1280]{1,0:T(8,128)(2,1)S(1)}, u32[]{:S(2)}, u32[]{:S(2)}) %collective-permute-start.5) | collective-permute-done | bytes 81952 | tf_op jit(solution)/shard_map/ppermute | solution.py:323
  89.2 1.0 collective-permute-done.6.refs_7_
  90.1 17.6 %all-to-all-done.1.refs_8_.refs_9_ = bf16[64,8,16,128]{3,2,1,0:T(8,128)(2,1)S(1)} async-done(((bf16[64,8,16,128]{3,2,1,0:T(8,128)(2,1)}), bf16[64,8,16,128]{3,2,1,0:T(8,128)(2,1)S(1)}, u32[]{:S(2)}, u32[]{:S(2)}) %all-to-all-start.1) | async-done | bytes 2097184 | tf_op jit(solution)/shard_map/all_to_all | solution.py:326
  107.8 10.0 %attend.1 = bf16[8,32,1024]{2,1,0:T(8,128)(2,1)S(1)} custom-call(s32[1]{0:T(128)} %bitcast.me_ref, bf16[32,1280]{1,0:T(8,128)(2,1)S(1)} %get-tuple-element.27.refs_0_, bf16[32,1280]{1,0:T(8,128)(2,1)S(1)} %collective-permute-done.refs_1_, bf16[32,1280]{1,0:T(8,128)(2,1)S(1)} %collective-permute-done.1.refs_2_, ...), custom_call_target="tpu_custom_call" | custom-call | flops 4563402752 | bytes 2097152 | tf_op jit(solution)/shard_map/attend/pallas_call | solution.py:248
  117.8 23.2 %all_to_all.16.in_ref = bf16[8,32,1024]{2,1,0:T(8,128)(2,1)S(1)} all-to-all(bf16[8,32,1024]{2,1,0:T(8,128)(2,1)S(1)} %attend.1), channel_id=1, replica_groups=mesh['cache'=64,'tp'=8] {'tp'}, dimensions={0} | all-to-all | bytes 1048576 | tf_op jit(solution)/shard_map/all_to_all | solution.py:328
  141.0 0.9 join_heads.1
  (11 shorter events, 0.1 us)
Async XLA Ops:
  1.4 46.0 %copy-start.3 = (pred[64,1,128]{2,1,0:T(4,128)(4,1)S(1)}, pred[64,1,128]{2,1,0:T(4,128)(4,1)}, u32[]{:S(2)}) copy-start(pred[64,1,128]{2,1,0:T(4,128)(4,1)} %constant.45) | copy-start | bytes 24580
  50.2 6.4 %copy-start = (bf16[1,32,8192]{2,1,0:T(8,128)(2,1)S(1)}, bf16[1,32,8192]{2,1,0:T(8,128)(2,1)}, u32[]{:S(2)}) copy-start(bf16[1,32,8192]{2,1,0:T(8,128)(2,1)} %param.9) | copy-start | bytes 1572868
  50.2 6.4 %copy-start.1 = (bf16[1,32,1024]{2,1,0:T(8,128)(2,1)S(1)}, bf16[1,32,1024]{2,1,0:T(8,128)(2,1)}, u32[]{:S(2)}) copy-start(bf16[1,32,1024]{2,1,0:T(8,128)(2,1)} %param.10) | copy-start | bytes 196612
  50.2 6.4 %copy-start.2 = (bf16[1,32,1024]{2,1,0:T(8,128)(2,1)S(1)}, bf16[1,32,1024]{2,1,0:T(8,128)(2,1)}, u32[]{:S(2)}) copy-start(bf16[1,32,1024]{2,1,0:T(8,128)(2,1)} %param.11) | copy-start | bytes 196612
  50.2 57.6 %all-to-all-start.1 = ((bf16[64,8,16,128]{3,2,1,0:T(8,128)(2,1)}), bf16[64,8,16,128]{3,2,1,0:T(8,128)(2,1)S(1)}, u32[]{:S(2)}, u32[]{:S(2)}) async-start(bf16[64,8,16,128]{3,2,1,0:T(8,128)(2,1)} %pick_rows.1), calls=%async_computation.1 | async-start | bytes 4194304 | tf_op jit(solution)/shard_map/all_to_all | solution.py:326
  56.6 20.5 %collective-permute-start = (bf16[32,1280]{1,0:T(8,128)(2,1)S(1)}, bf16[32,1280]{1,0:T(8,128)(2,1)S(1)}, u32[]{:S(2)}, u32[]{:S(2)}) collective-permute-start(bf16[32,1280]{1,0:T(8,128)(2,1)S(1)} %get-tuple-element.28), channel_id=1, source_target_pairs={{0,1},{1,2},{2,3},{3,4},{4,5},{5,6},{6,7},{7,0},{8,9},{9,10},{10,1... | collective-permute-start | bytes 245768 | tf_op jit(solution)/shard_map/ppermute | solution.py:323
  59.9 22.3 %collective-permute-start.1 = (bf16[32,1280]{1,0:T(8,128)(2,1)S(1)}, bf16[32,1280]{1,0:T(8,128)(2,1)S(1)}, u32[]{:S(2)}, u32[]{:S(2)}) collective-permute-start(bf16[32,1280]{1,0:T(8,128)(2,1)S(1)} %get-tuple-element.29), channel_id=1, source_target_pairs={{0,2},{1,3},{2,4},{3,5},{4,6},{5,7},{6,0},{7,1},{8,10},{9,11},{10,... | collective-permute-start | bytes 245768 | tf_op jit(solution)/shard_map/ppermute | solution.py:323
  64.1 21.2 %collective-permute-start.2 = (bf16[32,1280]{1,0:T(8,128)(2,1)S(1)}, bf16[32,1280]{1,0:T(8,128)(2,1)S(1)}, u32[]{:S(2)}, u32[]{:S(2)}) collective-permute-start(bf16[32,1280]{1,0:T(8,128)(2,1)S(1)} %get-tuple-element.30), channel_id=1, source_target_pairs={{0,3},{1,4},{2,5},{3,6},{4,7},{5,0},{6,1},{7,2},{8,11},{9,12},{10,... | collective-permute-start | bytes 245768 | tf_op jit(solution)/shard_map/ppermute | solution.py:323
  68.7 16.6 %collective-permute-start.3 = (bf16[32,1280]{1,0:T(8,128)(2,1)S(1)}, bf16[32,1280]{1,0:T(8,128)(2,1)S(1)}, u32[]{:S(2)}, u32[]{:S(2)}) collective-permute-start(bf16[32,1280]{1,0:T(8,128)(2,1)S(1)} %get-tuple-element.31), channel_id=1, source_target_pairs={{0,4},{1,5},{2,6},{3,7},{4,0},{5,1},{6,2},{7,3},{8,12},{9,13},{10,... | collective-permute-start | bytes 245768 | tf_op jit(solution)/shard_map/ppermute | solution.py:323
  72.3 13.1 %collective-permute-start.4 = (bf16[32,1280]{1,0:T(8,128)(2,1)S(1)}, bf16[32,1280]{1,0:T(8,128)(2,1)S(1)}, u32[]{:S(2)}, u32[]{:S(2)}) collective-permute-start(bf16[32,1280]{1,0:T(8,128)(2,1)S(1)} %get-tuple-element.32), channel_id=1, source_target_pairs={{0,5},{1,6},{2,7},{3,0},{4,1},{5,2},{6,3},{7,4},{8,13},{9,14},{10,... | collective-permute-start | bytes 245768 | tf_op jit(solution)/shard_map/ppermute | solution.py:323
  77.2 12.0 %collective-permute-start.5 = (bf16[32,1280]{1,0:T(8,128)(2,1)S(1)}, bf16[32,1280]{1,0:T(8,128)(2,1)S(1)}, u32[]{:S(2)}, u32[]{:S(2)}) collective-permute-start(bf16[32,1280]{1,0:T(8,128)(2,1)S(1)} %get-tuple-element.33), channel_id=1, source_target_pairs={{0,6},{1,7},{2,0},{3,1},{4,2},{5,3},{6,4},{7,5},{8,14},{9,15},{10,... | collective-permute-start | bytes 245768 | tf_op jit(solution)/shard_map/ppermute | solution.py:323
  82.1 8.0 %collective-permute-start.6 = (bf16[32,1280]{1,0:T(8,128)(2,1)S(1)}, bf16[32,1280]{1,0:T(8,128)(2,1)S(1)}, u32[]{:S(2)}, u32[]{:S(2)}) collective-permute-start(bf16[32,1280]{1,0:T(8,128)(2,1)S(1)} %get-tuple-element.34), channel_id=1, source_target_pairs={{0,7},{1,0},{2,1},{3,2},{4,3},{5,4},{6,5},{7,6},{8,15},{9,8},{10,9... | collective-permute-start | bytes 245768 | tf_op jit(solution)/shard_map/ppermute | solution.py:323
